TPU v7x, 512 devices: a whole 4x8x8 slice. The times are simulated.
512 devices in a mesh: narrow: 4 (over z_hi, core), wide: 128 (over x, y, z_lo).
Axes of the slice: x: 4, y: 8, z: 8 (z_hi: 2, z_lo: 4; z = z_hi * 4 + z_lo), core: 2. Of those that a mesh axis runs over, the one named last changes fastest.
Arguments:
- picture_vectors: float32 [65536, 1152], P(('narrow', 'wide')), may hold values from -1.5 to 1.5
- caption_vectors: float32 [65536, 1152], P(('narrow', 'wide')), may hold values from -1.5 to 1.5
- sharpness_factor: float32 [1], replicated, may hold values from 8 to 16
- score_shift_term: float32 [1], replicated, may hold values from -6 to -3
Outputs:
- row_loss: float32 [65536], P(('narrow', 'wide'))
- grad_images: float32 [65536, 1152], P(('narrow', 'wide'))
- grad_texts: float32 [65536, 1152], P(('narrow', 'wide'))
All inputs are finite; a program needn't handle non-finite values.
Results may differ from a plain program's by a relative error of at most 0.013.
Values may be sent and summed in bfloat16 or wider, within the bound.
No kernel may reach another device: no remote copies, remote signals or barrier semaphores. Data moves between devices by JAX's collectives and lax.ppermute only.
A program may use at most 64 MiB of HBM per device.

v0:
```python
import jax
import jax.numpy as jnp
from jax import lax
from jax.sharding import PartitionSpec as P


def shifted(shard, axis, by):
    peers = lax.axis_size(axis)
    return lax.ppermute(shard, axis, [(i, (i + by) % peers) for i in range(peers)])


def unit_normalize(raw_rows):
    row_size = jnp.sqrt(jnp.sum(raw_rows * raw_rows, axis=1, keepdims=True) + 1e-06)
    return (raw_rows / row_size, row_size)


def backward(gradient, unit_rows, row_size):
    projected = jnp.sum(gradient * unit_rows, axis=1, keepdims=True)
    return (gradient - projected * unit_rows) / row_size


def block_sweep_step(
    collected_embedding_rows,
    neighbor_device_rows,
    score_scaling_factor,
    window_displacement,
    matched_pair_score,
):
    similarity_matrix = lax.dot_general(
        collected_embedding_rows,
        neighbor_device_rows,
        (((1,), (1,)), ((), ())),
        preferred_element_type=jnp.float32,
    )
    pairwise_score_matrix = score_scaling_factor * similarity_matrix + window_displacement
    target_sign = 2.0 * matched_pair_score - 1.0
    losses = jax.nn.softplus(-target_sign * pairwise_score_matrix)
    pair_label_factors = (
        score_scaling_factor * (jax.nn.sigmoid(pairwise_score_matrix) - matched_pair_score)
    ).astype(jnp.bfloat16)
    picture_slice = jnp.dot(
        pair_label_factors, neighbor_device_rows, preferred_element_type=jnp.float32
    )
    caption_slice = lax.dot_general(
        pair_label_factors,
        collected_embedding_rows,
        (((0,), (0,)), ((), ())),
        preferred_element_type=jnp.float32,
    )
    return (picture_slice, jnp.sum(losses, axis=1), caption_slice)


def body(picture_vectors, caption_vectors, sharpness_factor, score_shift_term):
    img_unit, img_size = unit_normalize(picture_vectors)
    txt_unit, txt_size = unit_normalize(caption_vectors)
    caption_lower_slice = txt_unit.astype(jnp.bfloat16)
    collected_embedding_rows = lax.all_gather(
        img_unit.astype(jnp.bfloat16), "narrow", axis=0, tiled=True
    )
    score_scaling_factor = sharpness_factor[0]
    window_displacement = score_shift_term[0]
    row_count = caption_lower_slice.shape[0]
    tall_count = collected_embedding_rows.shape[0]
    narrow_index = lax.axis_index("narrow")
    matched_pair_score = (
        lax.broadcasted_iota(jnp.int32, (tall_count, row_count), 0)
        == narrow_index * row_count + lax.broadcasted_iota(jnp.int32, (tall_count, row_count), 1)
    ).astype(jnp.float32)
    mismatched_pair_scores = jnp.zeros((tall_count, row_count), jnp.float32)
    radius = min(4, (lax.axis_size("wide") - 1) // 2)
    img_grad, row_total, text_home_part = block_sweep_step(
        collected_embedding_rows,
        caption_lower_slice,
        score_scaling_factor,
        window_displacement,
        matched_pair_score,
    )
    toward_higher_neighbor = caption_lower_slice
    toward_lower_neighbor = caption_lower_slice
    for hop_count in range(1, radius + 1):
        toward_higher_neighbor = shifted(toward_higher_neighbor, "wide", 1)
        toward_lower_neighbor = shifted(toward_lower_neighbor, "wide", -1)
        image_upward_part, loss_up, txt_up = block_sweep_step(
            collected_embedding_rows,
            toward_higher_neighbor,
            score_scaling_factor,
            window_displacement,
            mismatched_pair_scores,
        )
        img_down, loss_down, text_downward_part = block_sweep_step(
            collected_embedding_rows,
            toward_lower_neighbor,
            score_scaling_factor,
            window_displacement,
            mismatched_pair_scores,
        )
        img_grad = img_grad + image_upward_part + img_down
        row_total = row_total + loss_up + loss_down
        text_home_part = text_home_part + shifted(
            txt_up.astype(jnp.bfloat16), "wide", -hop_count
        ).astype(txt_up.dtype)
        text_home_part = text_home_part + shifted(
            text_downward_part.astype(jnp.bfloat16), "wide", hop_count
        ).astype(text_downward_part.dtype)
    share_grad, share_loss = (
        lax.psum_scatter(
            img_grad.astype(jnp.bfloat16), "narrow", scatter_dimension=0, tiled=True
        ).astype(jnp.float32),
        lax.psum_scatter(
            row_total.astype(jnp.bfloat16), "narrow", scatter_dimension=0, tiled=True
        ).astype(jnp.float32),
    )
    grad_images = backward(share_grad, img_unit, img_size)
    grad_texts = backward(text_home_part, txt_unit, txt_size)
    return (share_loss, grad_images, grad_texts)


def solution(mesh):
    return jax.shard_map(
        body,
        mesh=mesh,
        in_specs=(P(("narrow", "wide"), None), P(("narrow", "wide"), None), P(), P()),
        out_specs=(P(("narrow", "wide")), P(("narrow", "wide"), None), P(("narrow", "wide"), None)),
        check_vma=False,
    )
```

profile of v0, /device:TPU:1, one launch (start us, length us, event | category | flops | bytes accessed | tf_op | source)
XLA Modules:
  0.0 193.6 jit_solution(8647212997434361141)
XLA Ops:
  7.2 0.0 all-gather.2.cloned.1.call-start
  7.2 1.2 multiply_reduce_fusion.2
  8.5 1.9 fusion.30
  10.4 0.0 reduce-scatter.2.cloned.1.call-start
  10.4 0.1 multiply_reduce_fusion.1
  10.6 0.1 fusion.29
  10.7 4.8 %collective-permute-start = (bf16[128,1152]{1,0:T(8,128)(2,1)S(1)}, bf16[128,1152]{1,0:T(8,128)(2,1)S(1)}, u32[]{:S(2)}, u32[]{:S(2)}) collective-permute-start(bf16[128,1152]{1,0:T(8,128)(2,1)S(1)} %fusion.29), channel_id=1, source_target_pairs={{0,1},{1,2},{2,3},{3,4},{4,5},{5,6},{6,7},{7,8},{8,9},{9,10},{10,1... | collective-permute-start | bytes 884744 | tf_op jit(solution)/shard_map/ppermute | solution.py:9
  15.5 10.6 %collective-permute-start.1 = (bf16[128,1152]{1,0:T(8,128)(2,1)S(1)}, bf16[128,1152]{1,0:T(8,128)(2,1)S(1)}, u32[]{:S(2)}, u32[]{:S(2)}) collective-permute-start(bf16[128,1152]{1,0:T(8,128)(2,1)S(1)} %fusion.29), channel_id=1, source_target_pairs={{0,127},{1,0},{2,1},{3,2},{4,3},{5,4},{6,5},{7,6},{8,7},{9,8},{10,... | collective-permute-start | bytes 884744 | tf_op jit(solution)/shard_map/ppermute | solution.py:9
  26.2 2.4 %collective-permute-done = bf16[128,1152]{1,0:T(8,128)(2,1)S(1)} collective-permute-done((bf16[128,1152]{1,0:T(8,128)(2,1)S(1)}, bf16[128,1152]{1,0:T(8,128)(2,1)S(1)}, u32[]{:S(2)}, u32[]{:S(2)}) %collective-permute-start) | collective-permute-done | bytes 294944 | tf_op jit(solution)/shard_map/ppermute | solution.py:9
  28.6 1.9 collective-permute-start.2
  30.5 0.2 collective-permute-done.1
  30.7 9.3 %collective-permute-start.3 = (bf16[128,1152]{1,0:T(8,128)(2,1)S(1)}, bf16[128,1152]{1,0:T(8,128)(2,1)S(1)}, u32[]{:S(2)}, u32[]{:S(2)}) collective-permute-start(bf16[128,1152]{1,0:T(8,128)(2,1)S(1)} %collective-permute-done.1), channel_id=1, source_target_pairs={{0,127},{1,0},{2,1},{3,2},{4,3},{5,4},{6,5},{7,6},{8,7},{9,8},{10,... | collective-permute-start | bytes 884744 | tf_op jit(solution)/shard_map/ppermute | solution.py:9
  40.0 9.0 %collective-permute-done.2 = bf16[128,1152]{1,0:T(8,128)(2,1)S(1)} collective-permute-done((bf16[128,1152]{1,0:T(8,128)(2,1)S(1)}, bf16[128,1152]{1,0:T(8,128)(2,1)S(1)}, u32[]{:S(2)}, u32[]{:S(2)}) %collective-permute-start.2) | collective-permute-done | bytes 294944 | tf_op jit(solution)/shard_map/ppermute | solution.py:9
  49.0 5.0 %collective-permute-start.4 = (bf16[128,1152]{1,0:T(8,128)(2,1)S(1)}, bf16[128,1152]{1,0:T(8,128)(2,1)S(1)}, u32[]{:S(2)}, u32[]{:S(2)}) collective-permute-start(bf16[128,1152]{1,0:T(8,128)(2,1)S(1)} %collective-permute-done.2), channel_id=1, source_target_pairs={{0,1},{1,2},{2,3},{3,4},{4,5},{5,6},{6,7},{7,8},{8,9},{9,10},{10,1... | collective-permute-start | bytes 884744 | tf_op jit(solution)/shard_map/ppermute | solution.py:9
  53.9 5.4 %collective-permute-done.3 = bf16[128,1152]{1,0:T(8,128)(2,1)S(1)} collective-permute-done((bf16[128,1152]{1,0:T(8,128)(2,1)S(1)}, bf16[128,1152]{1,0:T(8,128)(2,1)S(1)}, u32[]{:S(2)}, u32[]{:S(2)}) %collective-permute-start.3) | collective-permute-done | bytes 294944 | tf_op jit(solution)/shard_map/ppermute | solution.py:9
  59.4 7.6 %collective-permute-start.5 = (bf16[128,1152]{1,0:T(8,128)(2,1)S(1)}, bf16[128,1152]{1,0:T(8,128)(2,1)S(1)}, u32[]{:S(2)}, u32[]{:S(2)}) collective-permute-start(bf16[128,1152]{1,0:T(8,128)(2,1)S(1)} %collective-permute-done.3), channel_id=1, source_target_pairs={{0,127},{1,0},{2,1},{3,2},{4,3},{5,4},{6,5},{7,6},{8,7},{9,8},{10,... | collective-permute-start | bytes 884744 | tf_op jit(solution)/shard_map/ppermute | solution.py:9
  67.0 1.9 collective-permute-start.6
  70.2 1.3 dynamic-slice
  72.2 3.6 %collective-permute-done.5 = bf16[128,1152]{1,0:T(8,128)(2,1)S(1)} collective-permute-done((bf16[128,1152]{1,0:T(8,128)(2,1)S(1)}, bf16[128,1152]{1,0:T(8,128)(2,1)S(1)}, u32[]{:S(2)}, u32[]{:S(2)}) %collective-permute-start.5) | collective-permute-done | bytes 294944 | tf_op jit(solution)/shard_map/ppermute | solution.py:9
  75.8 7.8 %collective-permute-start.7 = (bf16[128,1152]{1,0:T(8,128)(2,1)S(1)}, bf16[128,1152]{1,0:T(8,128)(2,1)S(1)}, u32[]{:S(2)}, u32[]{:S(2)}) collective-permute-start(bf16[128,1152]{1,0:T(8,128)(2,1)S(1)} %collective-permute-done.5), channel_id=1, source_target_pairs={{0,127},{1,0},{2,1},{3,2},{4,3},{5,4},{6,5},{7,6},{8,7},{9,8},{10,... | collective-permute-start | bytes 884744 | tf_op jit(solution)/shard_map/ppermute | solution.py:9
  83.6 0.0 all-gather.2.cloned.1.call-done
  83.6 2.0 %fusion.22 = (f32[512]{0:T(512)S(1)}, f32[512,128]{0,1:T(8,128)S(1)}) fusion(f32[]{:T(128)} %bitcast.68, bf16[512,1152]{1,0:T(8,128)(2,1)} %all-gather.2.cloned.1.call-done, bf16[128,1152]{1,0:T(8,128)(2,1)S(1)} %collective-permute-done.6, f32[]{:T(128)} %bitcast.50), kind=kOutput, calls=%fused_computation.62 | convolution fusion | flops 151584256 | bytes 1738760 | tf_op jit(solution)/shard_map/dot_general | solution.py:29
  85.7 1.1 convolution_convert_fusion.1
  86.7 9.4 %collective-permute-start.14 = (bf16[128,1152]{1,0:T(8,128)(2,1)}, bf16[128,1152]{1,0:T(8,128)(2,1)}, u32[]{:S(2)}, u32[]{:S(2)}) collective-permute-start(bf16[128,1152]{1,0:T(8,128)(2,1)} %convolution_convert_fusion.1), channel_id=1, source_target_pairs={{0,124},{1,125},{2,126},{3,127},{4,0},{5,1},{6,2},{7,3},{8,4},{9,5... | collective-permute-start | bytes 884744 | tf_op jit(solution)/shard_map/ppermute | solution.py:9
  96.1 0.7 fusion.23
  96.8 1.1 convolution_convert_fusion
  97.9 1.9 collective-permute-start.15
  99.8 0.7 fusion.20
  100.5 1.1 convolution_convert_fusion.3
  101.5 5.0 %collective-permute-start.12 = (bf16[128,1152]{1,0:T(8,128)(2,1)}, bf16[128,1152]{1,0:T(8,128)(2,1)}, u32[]{:S(2)}, u32[]{:S(2)}) collective-permute-start(bf16[128,1152]{1,0:T(8,128)(2,1)} %convolution_convert_fusion.3), channel_id=1, source_target_pairs={{0,125},{1,126},{2,127},{3,0},{4,1},{5,2},{6,3},{7,4},{8,5},{9,6},... | collective-permute-start | bytes 884744 | tf_op jit(solution)/shard_map/ppermute | solution.py:9
  106.5 0.7 fusion.15
  107.2 0.6 fusion.28
  107.8 0.1 copy-done.6
  108.0 0.5 fusion.26
  108.5 0.7 fusion.21
  109.2 0.7 fusion.18
  109.8 0.7 fusion.19
  110.5 0.7 fusion.16
  111.2 0.7 fusion.17
  111.9 0.5 fusion.24
  112.4 0.5 fusion.25
  112.9 0.5 convolution_add_fusion.4
  113.5 0.5 convolution_add_fusion.3
  114.0 0.5 fusion
  114.5 0.5 fusion.1
  115.1 1.6 fusion.3
  116.7 0.9 copy-done.5
  117.6 2.3 %convolution_convert_fusion.2 = bf16[128,1152]{1,0:T(8,128)(2,1)} fusion(bf16[512,1152]{1,0:T(8,128)(2,1)} %all-gather.2.cloned.1.call-done, f32[512,128]{0,1:T(8,128)S(1)} %copy-done.5, f32[]{:T(128)} %bitcast.62), kind=kOutput, calls=%fused_computation.11 | convolution fusion | flops 151470080 | bytes 1736708 | tf_op jit(solution)/shard_map/dot_general | solution.py:44
  120.0 2.1 %collective-permute-start.13 = (bf16[128,1152]{1,0:T(8,128)(2,1)}, bf16[128,1152]{1,0:T(8,128)(2,1)S(1)}, u32[]{:S(2)}, u32[]{:S(2)}) collective-permute-start(bf16[128,1152]{1,0:T(8,128)(2,1)} %convolution_convert_fusion.2), channel_id=1, source_target_pairs={{0,3},{1,4},{2,5},{3,6},{4,7},{5,8},{6,9},{7,10},{8,11},{9,12},{10... | collective-permute-start | bytes 884744 | tf_op jit(solution)/shard_map/ppermute | solution.py:9
  122.1 1.1 convolution_convert_fusion.5
  123.1 7.2 %collective-permute-start.10 = (bf16[128,1152]{1,0:T(8,128)(2,1)}, bf16[128,1152]{1,0:T(8,128)(2,1)}, u32[]{:S(2)}, u32[]{:S(2)}) collective-permute-start(bf16[128,1152]{1,0:T(8,128)(2,1)} %convolution_convert_fusion.5), channel_id=1, source_target_pairs={{0,126},{1,127},{2,0},{3,1},{4,2},{5,3},{6,4},{7,5},{8,6},{9,7},{1... | collective-permute-start | bytes 884744 | tf_op jit(solution)/shard_map/ppermute | solution.py:9
  130.3 1.1 convolution_convert_fusion.4
  131.4 1.1 convolution_convert_fusion.7
  132.5 1.1 convolution_convert_fusion.6
  133.6 1.9 collective-permute-start.11
  135.5 8.1 %collective-permute-start.8 = (bf16[128,1152]{1,0:T(8,128)(2,1)}, bf16[128,1152]{1,0:T(8,128)(2,1)S(1)}, u32[]{:S(2)}, u32[]{:S(2)}) collective-permute-start(bf16[128,1152]{1,0:T(8,128)(2,1)} %convolution_convert_fusion.7), channel_id=1, source_target_pairs={{0,127},{1,0},{2,1},{3,2},{4,3},{5,4},{6,5},{7,6},{8,7},{9,8},{10,... | collective-permute-start | bytes 884744 | tf_op jit(solution)/shard_map/ppermute | solution.py:9
  143.6 1.9 collective-permute-start.9
  145.6 34.2 %all-reduce = bf16[512]{0:T(512)(128)(2,1)S(1)} all-reduce(bf16[512]{0:T(512)(128)(2,1)S(1)} %add_convert_fusion), channel_id=2, replica_groups=mesh['narrow'=4,'wide'=128] {'narrow'}, use_global_device_ids=true, to_apply=%region_11.12.clone | all-reduce | flops 512 | bytes 2048
  179.8 0.6 dynamic-slice_convert_fusion
  180.4 2.1 %multiply_reduce_fusion = (f32[128]{0:T(128)S(1)}, f32[128,1152]{1,0:T(8,128)S(1)}) fusion(f32[128,1152]{1,0:T(8,128)S(1)} %copy-done.1, f32[128]{0:T(128)S(1)} %add_sqrt_fusion, bf16[128,1152]{1,0:T(8,128)(2,1)} %collective-permute-done.15, bf16[128,1152]{1,0:T(8,128)(2,1)} %collective-permute-done.14, bf16[128,1152]{1,0:T(8,128)(2,1)S(1)} %collective-permute-done.13, ...), kind=kOutput, calls=%fused_computation.49 | convolution fusion | flops 154320768 | bytes 4982276 | tf_op jit(solution)/shard_map/dot_general | solution.py:44
  182.5 1.0 subtract_divide_fusion
  183.5 0.1 copy-done
  183.6 1.2 fusion.13
  184.8 2.0 %fusion.14 = f32[128,1152]{1,0:T(8,128)} fusion(bf16[128,1152]{1,0:T(8,128)(2,1)} %reduce-scatter.2.cloned.1.call-done, f32[128]{0:T(128)S(1)} %fusion.13, f32[128]{0:T(128)S(1)} %add_sqrt_fusion.1, f32[128,1152]{1,0:T(8,128)S(1)} %copy-done), kind=kLoop, calls=%fused_computation.47 | loop fusion | flops 737280 | bytes 1475584 | tf_op jit(solution)/shard_map/div | solution.py:19
  (35 shorter events, 0.1 us)
Async XLA Ops:
  7.2 3.3 %copy-start.1 = (f32[128,1152]{1,0:T(8,128)S(1)}, f32[128,1152]{1,0:T(8,128)}, u32[]{:S(2)}) copy-start(f32[128,1152]{1,0:T(8,128)} %param.5) | copy-start | bytes 1769476
  7.2 76.4 %all-gather.2.cloned.1.call-start = ((), (), s32[]{:S(2)}) async-start(), calls=%async_computation.1 | async-start | bytes 1474560 | tf_op jit(solution)/shard_map/all_gather | solution.py:57
  10.4 173.1 %reduce-scatter.2.cloned.1.call-start = ((), (), s32[]{:S(2)}) async-start(), calls=%async_computation.2 | async-start | bytes 1474560 | tf_op jit(solution)/shard_map/reduce_scatter | solution.py:106
  10.7 17.9 %collective-permute-start = (bf16[128,1152]{1,0:T(8,128)(2,1)S(1)}, bf16[128,1152]{1,0:T(8,128)(2,1)S(1)}, u32[]{:S(2)}, u32[]{:S(2)}) collective-permute-start(bf16[128,1152]{1,0:T(8,128)(2,1)S(1)} %fusion.29), channel_id=1, source_target_pairs={{0,1},{1,2},{2,3},{3,4},{4,5},{5,6},{6,7},{7,8},{8,9},{9,10},{10,1... | collective-permute-start | bytes 884744 | tf_op jit(solution)/shard_map/ppermute | solution.py:9
  15.5 15.1 %collective-permute-start.1 = (bf16[128,1152]{1,0:T(8,128)(2,1)S(1)}, bf16[128,1152]{1,0:T(8,128)(2,1)S(1)}, u32[]{:S(2)}, u32[]{:S(2)}) collective-permute-start(bf16[128,1152]{1,0:T(8,128)(2,1)S(1)} %fusion.29), channel_id=1, source_target_pairs={{0,127},{1,0},{2,1},{3,2},{4,3},{5,4},{6,5},{7,6},{8,7},{9,8},{10,... | collective-permute-start | bytes 884744 | tf_op jit(solution)/shard_map/ppermute | solution.py:9
  28.6 20.4 %collective-permute-start.2 = (bf16[128,1152]{1,0:T(8,128)(2,1)S(1)}, bf16[128,1152]{1,0:T(8,128)(2,1)S(1)}, u32[]{:S(2)}, u32[]{:S(2)}) collective-permute-start(bf16[128,1152]{1,0:T(8,128)(2,1)S(1)} %collective-permute-done), channel_id=1, source_target_pairs={{0,1},{1,2},{2,3},{3,4},{4,5},{5,6},{6,7},{7,8},{8,9},{9,10},{10,1... | collective-permute-start | bytes 884744 | tf_op jit(solution)/shard_map/ppermute | solution.py:9
  30.7 28.7 %collective-permute-start.3 = (bf16[128,1152]{1,0:T(8,128)(2,1)S(1)}, bf16[128,1152]{1,0:T(8,128)(2,1)S(1)}, u32[]{:S(2)}, u32[]{:S(2)}) collective-permute-start(bf16[128,1152]{1,0:T(8,128)(2,1)S(1)} %collective-permute-done.1), channel_id=1, source_target_pairs={{0,127},{1,0},{2,1},{3,2},{4,3},{5,4},{6,5},{7,6},{8,7},{9,8},{10,... | collective-permute-start | bytes 884744 | tf_op jit(solution)/shard_map/ppermute | solution.py:9
  49.0 18.0 %collective-permute-start.4 = (bf16[128,1152]{1,0:T(8,128)(2,1)S(1)}, bf16[128,1152]{1,0:T(8,128)(2,1)S(1)}, u32[]{:S(2)}, u32[]{:S(2)}) collective-permute-start(bf16[128,1152]{1,0:T(8,128)(2,1)S(1)} %collective-permute-done.2), channel_id=1, source_target_pairs={{0,1},{1,2},{2,3},{3,4},{4,5},{5,6},{6,7},{7,8},{8,9},{9,10},{10,1... | collective-permute-start | bytes 884744 | tf_op jit(solution)/shard_map/ppermute | solution.py:9
  59.4 16.4 %collective-permute-start.5 = (bf16[128,1152]{1,0:T(8,128)(2,1)S(1)}, bf16[128,1152]{1,0:T(8,128)(2,1)S(1)}, u32[]{:S(2)}, u32[]{:S(2)}) collective-permute-start(bf16[128,1152]{1,0:T(8,128)(2,1)S(1)} %collective-permute-done.3), channel_id=1, source_target_pairs={{0,127},{1,0},{2,1},{3,2},{4,3},{5,4},{6,5},{7,6},{8,7},{9,8},{10,... | collective-permute-start | bytes 884744 | tf_op jit(solution)/shard_map/ppermute | solution.py:9
  67.0 16.6 %collective-permute-start.6 = (bf16[128,1152]{1,0:T(8,128)(2,1)S(1)}, bf16[128,1152]{1,0:T(8,128)(2,1)S(1)}, u32[]{:S(2)}, u32[]{:S(2)}) collective-permute-start(bf16[128,1152]{1,0:T(8,128)(2,1)S(1)} %collective-permute-done.4), channel_id=1, source_target_pairs={{0,1},{1,2},{2,3},{3,4},{4,5},{5,6},{6,7},{7,8},{8,9},{9,10},{10,1... | collective-permute-start | bytes 884744 | tf_op jit(solution)/shard_map/ppermute | solution.py:9
  75.8 20.4 %collective-permute-start.7 = (bf16[128,1152]{1,0:T(8,128)(2,1)S(1)}, bf16[128,1152]{1,0:T(8,128)(2,1)S(1)}, u32[]{:S(2)}, u32[]{:S(2)}) collective-permute-start(bf16[128,1152]{1,0:T(8,128)(2,1)S(1)} %collective-permute-done.5), channel_id=1, source_target_pairs={{0,127},{1,0},{2,1},{3,2},{4,3},{5,4},{6,5},{7,6},{8,7},{9,8},{10,... | collective-permute-start | bytes 884744 | tf_op jit(solution)/shard_map/ppermute | solution.py:9
  83.6 2.0 %copy-start.8 = (bf16[512,1152]{1,0:T(8,128)(2,1)S(1)}, bf16[512,1152]{1,0:T(8,128)(2,1)}, u32[]{:S(2)}) copy-start(bf16[512,1152]{1,0:T(8,128)(2,1)} %all-gather.2.cloned.1.call-done) | copy-start | bytes 3538948
  86.7 46.8 %collective-permute-start.14 = (bf16[128,1152]{1,0:T(8,128)(2,1)}, bf16[128,1152]{1,0:T(8,128)(2,1)}, u32[]{:S(2)}, u32[]{:S(2)}) collective-permute-start(bf16[128,1152]{1,0:T(8,128)(2,1)} %convolution_convert_fusion.1), channel_id=1, source_target_pairs={{0,124},{1,125},{2,126},{3,127},{4,0},{5,1},{6,2},{7,3},{8,4},{9,5... | collective-permute-start | bytes 884744 | tf_op jit(solution)/shard_map/ppermute | solution.py:9
  97.9 37.6 %collective-permute-start.15 = (bf16[128,1152]{1,0:T(8,128)(2,1)}, bf16[128,1152]{1,0:T(8,128)(2,1)}, u32[]{:S(2)}, u32[]{:S(2)}) collective-permute-start(bf16[128,1152]{1,0:T(8,128)(2,1)} %convolution_convert_fusion), channel_id=1, source_target_pairs={{0,4},{1,5},{2,6},{3,7},{4,8},{5,9},{6,10},{7,11},{8,12},{9,13},{1... | collective-permute-start | bytes 884744 | tf_op jit(solution)/shard_map/ppermute | solution.py:9
  101.5 42.1 %collective-permute-start.12 = (bf16[128,1152]{1,0:T(8,128)(2,1)}, bf16[128,1152]{1,0:T(8,128)(2,1)}, u32[]{:S(2)}, u32[]{:S(2)}) collective-permute-start(bf16[128,1152]{1,0:T(8,128)(2,1)} %convolution_convert_fusion.3), channel_id=1, source_target_pairs={{0,125},{1,126},{2,127},{3,0},{4,1},{5,2},{6,3},{7,4},{8,5},{9,6},... | collective-permute-start | bytes 884744 | tf_op jit(solution)/shard_map/ppermute | solution.py:9
  107.2 0.7 copy-start.6
  109.2 3.2 %copy-start.4 = (f32[512,128]{0,1:T(8,128)}, f32[512,128]{0,1:T(8,128)S(1)}, u32[]{:S(2)}) copy-start(f32[512,128]{0,1:T(8,128)S(1)} %get-tuple-element.8) | copy-start | bytes 786436
  109.8 4.2 %copy-start.2 = (f32[512,128]{0,1:T(8,128)}, f32[512,128]{0,1:T(8,128)S(1)}, u32[]{:S(2)}) copy-start(f32[512,128]{0,1:T(8,128)S(1)} %get-tuple-element.14) | copy-start | bytes 786436
  116.7 0.9 copy-start.5
  116.7 5.3 %copy-start.3 = (f32[512,128]{0,1:T(8,128)S(1)}, f32[512,128]{0,1:T(8,128)}, u32[]{:S(2)}) copy-start(f32[512,128]{0,1:T(8,128)} %copy-done.2) | copy-start | bytes 786436
  116.7 5.3 %copy-start.9 = (bf16[512,1152]{1,0:T(8,128)(2,1)S(1)}, bf16[512,1152]{1,0:T(8,128)(2,1)}, u32[]{:S(2)}) copy-start(bf16[512,1152]{1,0:T(8,128)(2,1)} %all-gather.2.cloned.1.call-done) | copy-start | bytes 3538948
  120.0 60.4 %collective-permute-start.13 = (bf16[128,1152]{1,0:T(8,128)(2,1)}, bf16[128,1152]{1,0:T(8,128)(2,1)S(1)}, u32[]{:S(2)}, u32[]{:S(2)}) collective-permute-start(bf16[128,1152]{1,0:T(8,128)(2,1)} %convolution_convert_fusion.2), channel_id=1, source_target_pairs={{0,3},{1,4},{2,5},{3,6},{4,7},{5,8},{6,9},{7,10},{8,11},{9,12},{10... | collective-permute-start | bytes 884744 | tf_op jit(solution)/shard_map/ppermute | solution.py:9
  123.1 57.3 %collective-permute-start.10 = (bf16[128,1152]{1,0:T(8,128)(2,1)}, bf16[128,1152]{1,0:T(8,128)(2,1)}, u32[]{:S(2)}, u32[]{:S(2)}) collective-permute-start(bf16[128,1152]{1,0:T(8,128)(2,1)} %convolution_convert_fusion.5), channel_id=1, source_target_pairs={{0,126},{1,127},{2,0},{3,1},{4,2},{5,3},{6,4},{7,5},{8,6},{9,7},{1... | collective-permute-start | bytes 884744 | tf_op jit(solution)/shard_map/ppermute | solution.py:9
  132.5 47.9 %copy-start.7 = (f32[512,128]{0,1:T(8,128)S(1)}, f32[512,128]{0,1:T(8,128)}, u32[]{:S(2)}) copy-start(f32[512,128]{0,1:T(8,128)} %copy-done.6) | copy-start | bytes 786436
  133.6 46.8 %collective-permute-start.11 = (bf16[128,1152]{1,0:T(8,128)(2,1)}, bf16[128,1152]{1,0:T(8,128)(2,1)S(1)}, u32[]{:S(2)}, u32[]{:S(2)}) collective-permute-start(bf16[128,1152]{1,0:T(8,128)(2,1)} %convolution_convert_fusion.4), channel_id=1, source_target_pairs={{0,2},{1,3},{2,4},{3,5},{4,6},{5,7},{6,8},{7,9},{8,10},{9,11},{10,... | collective-permute-start | bytes 884744 | tf_op jit(solution)/shard_map/ppermute | solution.py:9
  135.5 44.9 %collective-permute-start.8 = (bf16[128,1152]{1,0:T(8,128)(2,1)}, bf16[128,1152]{1,0:T(8,128)(2,1)S(1)}, u32[]{:S(2)}, u32[]{:S(2)}) collective-permute-start(bf16[128,1152]{1,0:T(8,128)(2,1)} %convolution_convert_fusion.7), channel_id=1, source_target_pairs={{0,127},{1,0},{2,1},{3,2},{4,3},{5,4},{6,5},{7,6},{8,7},{9,8},{10,... | collective-permute-start | bytes 884744 | tf_op jit(solution)/shard_map/ppermute | solution.py:9
  143.6 36.8 %collective-permute-start.9 = (bf16[128,1152]{1,0:T(8,128)(2,1)}, bf16[128,1152]{1,0:T(8,128)(2,1)}, u32[]{:S(2)}, u32[]{:S(2)}) collective-permute-start(bf16[128,1152]{1,0:T(8,128)(2,1)} %convolution_convert_fusion.6), channel_id=1, source_target_pairs={{0,1},{1,2},{2,3},{3,4},{4,5},{5,6},{6,7},{7,8},{8,9},{9,10},{10,1... | collective-permute-start | bytes 884744 | tf_op jit(solution)/shard_map/ppermute | solution.py:9
  182.5 1.1 copy-start
Sparse Core Ops, SparseCore 0:
  10.7 43.8 all-gather.1
  116.8 58.4 reduce-scatter.1
where the time goes:
time: 195 us; the launch traced here: 194 us
  starting transfers between devices  86.5 us (44%)
  blocking collectives  34.2 us (18%)
  matrix products  25.2 us (13%)
  waiting for transfers between devices  20.6 us (11%)
  between operations  16.4 us (8%)
  other arithmetic  8.14 us (4%)
  local copies, waits for them, and re-layouts  2.4 us (1%)
    ppermute x16, starting transfers between devices, shifted(): lax.ppermute(shard, axis, [(i, (i + by) % peers) for i in range(peers)])  86.5 us
    unnamed x1, blocking collectives  34.2 us
    ppermute x16, waiting for transfers between devices, shifted(): lax.ppermute(shard, axis, [(i, (i + by) % peers) for i in range(peers)])  20.6 us
    dot_general x9, matrix products, block_sweep_step(): lax.dot_general(pair_label_factors, collected_embedding_rows, (((0,), (0,...  11.9 us
    dot_general x9, matrix products, block_sweep_step(): lax.dot_general(collected_embedding_rows, neighbor_device_rows, (((1,), (...  7.43 us
    dot_general x9, matrix products, block_sweep_step(): jnp.dot(pair_label_factors, neighbor_device_rows, preferred_element_type=...  5.86 us
  transfers between devices with their start and end apart: 18, of which 5 were waited for; matrix products, arithmetic and copies ran while one was open for 15% of the time, Pallas kernels for 0%

commit v1 on v0

v1 whole, which is shorter than its diff:
```python
import jax
import jax.numpy as jnp
from jax import lax
from jax.sharding import PartitionSpec as P

AXES = ("narrow", "wide")
SEG = 4


def unit_normalize(raw_rows):
    row_size = jnp.sqrt(jnp.sum(raw_rows * raw_rows, axis=1, keepdims=True) + 1e-06)
    return (raw_rows / row_size, row_size)


def backward(gradient, unit_rows, row_size):
    projected = jnp.sum(gradient * unit_rows, axis=1, keepdims=True)
    return (gradient - projected * unit_rows) / row_size


def routes(n_narrow, n_wide):
    chips = n_narrow // 2

    def flat(hi, core, block):
        return (hi * 2 + core) * n_wide + block % n_wide

    pairs = {name: [] for name in ("core", "hi", "a", "b", "c", "d", "e")}
    for hi in range(chips):
        for core in range(2):
            for block in range(n_wide):
                me = flat(hi, core, block)
                place = block % SEG
                rank, step = (place, 1) if core == 0 else (SEG - 1 - place, -1)
                along = [flat(hi, core, block + step * k) for k in range(SEG - rank)]
                across = flat(hi, 1 - core, block - step * SEG)
                pairs["core"].append((me, flat(hi, 1 - core, block)))
                pairs["hi"].append((me, flat(chips - 1 - hi, core, block)))
                pairs["a"].append((me, along[1] if rank <= 2 else across))
                if rank <= 2:
                    pairs["b"].append((me, along[2] if rank <= 1 else across))
                pairs["c"].append((me, along[3] if rank == 0 else across))
                pairs["d"].append((me, across))
                if rank == 3:
                    pairs["e"].append((me, across))
    return pairs


def scores(images, texts, scale, shift, labels):
    similarity = lax.dot_general(
        images, texts, (((1,), (1,)), ((), ())), preferred_element_type=jnp.float32
    )
    logits = scale * similarity + shift
    if labels is None:
        losses = jax.nn.softplus(logits)
        coef = scale * jax.nn.sigmoid(logits)
    else:
        losses = jax.nn.softplus((1.0 - 2.0 * labels) * logits)
        coef = scale * (jax.nn.sigmoid(logits) - labels)
    coef = coef.astype(jnp.bfloat16)
    text_part = lax.dot_general(
        coef, images, (((0,), (0,)), ((), ())), preferred_element_type=jnp.float32
    )
    return coef, jnp.sum(losses, axis=1, keepdims=True), text_part


def make_body(pairs):
    def send(x, name):
        return lax.ppermute(x, AXES, pairs[name])

    def send_back(x, name):
        return lax.ppermute(x, AXES, [(b, a) for a, b in pairs[name]])

    def body(picture_vectors, caption_vectors, sharpness_factor, score_shift_term):
        bf16, f32 = jnp.bfloat16, jnp.float32
        rows = picture_vectors.shape[0]
        width = picture_vectors.shape[1]
        scale, shift = sharpness_factor[0], score_shift_term[0]
        place = lax.axis_index("wide") % SEG
        rank = jnp.where(lax.axis_index("narrow") % 2 == 0, place, SEG - 1 - place)

        img_unit, img_size = unit_normalize(picture_vectors)
        txt_unit, txt_size = unit_normalize(caption_vectors)
        img_low, txt_low = img_unit.astype(bf16), txt_unit.astype(bf16)

        from_hi = send(img_low, "hi")
        from_core = send(jnp.concatenate([txt_low, img_low]), "core")
        own = jnp.concatenate([txt_low, from_core[:rows]])
        got_a = send(own, "a")
        got_b = send(own, "b")
        from_both = send(from_hi, "core")
        images = jnp.concatenate([img_low, from_core[rows:], from_hi, from_both])
        got_c = send(jnp.where(rank <= 1, own, got_a), "c")
        got_d = send(jnp.where(rank == 0, own, jnp.where(rank == 1, got_a, got_b)), "d")
        got_e = send(got_c, "e")
        got_x = jnp.where(rank == 0, got_e, got_b)

        labels = (
            lax.broadcasted_iota(jnp.int32, (4 * rows, rows), 0)
            == lax.broadcasted_iota(jnp.int32, (4 * rows, rows), 1)
        ).astype(f32)
        coef_h, loss_h, text_h = scores(images, txt_low, scale, shift, labels)
        coef_a, loss_a, text_a = scores(images, got_a, scale, shift, None)
        coef_c, loss_c, text_c = scores(images, got_c, scale, shift, None)
        coef_d, loss_d, text_d = scores(images, got_d, scale, shift, None)
        coef_x, loss_x, text_x = scores(images, got_x, scale, shift, None)

        text_c = text_c + send_back(text_x.astype(bf16), "e").astype(f32)
        back_d = send_back(text_d.astype(bf16), "d").astype(f32)
        back_c = send_back(text_c.astype(bf16), "c").astype(f32)
        text_b = text_x + jnp.where(rank >= 2, back_d, 0.0)
        back_b = send_back(text_b.astype(bf16), "b").astype(f32)
        text_a = text_a + jnp.where(rank >= 2, back_c, 0.0) + jnp.where(rank == 1, back_d, 0.0)
        back_a = send_back(text_a.astype(bf16), "a").astype(f32)
        total = (
            back_a
            + back_b
            + jnp.where(rank <= 1, back_c, 0.0)
            + jnp.where(rank == 0, back_d, 0.0)
        )
        back_core = send(total[rows:].astype(bf16), "core").astype(f32)
        txt_total = text_h + total[:rows] + back_core

        coef = jnp.concatenate([coef_h, coef_a, coef_c, coef_d, coef_x], axis=1)
        texts = jnp.concatenate([txt_low, got_a, got_c, got_d, got_x])
        img_part = jnp.dot(coef, texts, preferred_element_type=f32)
        loss = loss_h + loss_a + loss_c + loss_d + loss_x

        def packed(grad, loss):
            high = loss.astype(bf16)
            low = (loss - high.astype(f32)).astype(bf16)
            pad = jnp.zeros((grad.shape[0], 126), bf16)
            return jnp.concatenate([grad.astype(bf16), high, low, pad], axis=1)

        def unpacked(x):
            x = x.astype(f32)
            return x[:, :width], x[:, width : width + 1] + x[:, width + 1 : width + 2]

        def block(x, k):
            return x[k * rows : (k + 1) * rows]

        pick = lambda x, i, j: jnp.concatenate([block(x, i), block(x, j)])
        grad_in, loss_in = unpacked(
            send(packed(pick(img_part, 1, 3), pick(loss, 1, 3)), "core")
        )
        img_half = pick(img_part, 0, 2) + grad_in
        loss_half = pick(loss, 0, 2) + loss_in
        grad_in, loss_in = unpacked(
            send(packed(img_half[rows:], loss_half[rows:]), "hi")
        )
        img_total = img_half[:rows] + grad_in
        row_loss = (loss_half[:rows] + loss_in)[:, 0]

        grad_images = backward(img_total, img_unit, img_size)
        grad_texts = backward(txt_total, txt_unit, txt_size)
        return (row_loss, grad_images, grad_texts)

    return body


def solution(mesh):
    pairs = routes(mesh.shape["narrow"], mesh.shape["wide"])
    return jax.shard_map(
        make_body(pairs),
        mesh=mesh,
        in_specs=(P(AXES, None), P(AXES, None), P(), P()),
        out_specs=(P(AXES), P(AXES, None), P(AXES, None)),
        check_vma=False,
    )
```

time: 195 us -> 174 us (0.89)
  blocking collectives: 34.2 us -> 0 us
  waiting for transfers between devices: 20.6 us -> 53.3 us
  between operations: 16.4 us -> 2.53 us
  starting transfers between devices: 86.5 us -> 76.9 us
  local copies, waits for them, and re-layouts: 2.4 us -> 9.58 us
  matrix products: 25.2 us -> 22.6 us
    unnamed x1 -> x0, blocking collectives: 34.2 us -> none
    ppermute x16, waiting for transfers between devices: 20.6 us -> 53.3 us  [the longest x11 44 us: send(): return lax.ppermute(x, AXES, pairs[name])]
    ppermute x16, starting transfers between devices: 86.5 us -> 76.9 us  [the longest x11 66.3 us: send(): return lax.ppermute(x, AXES, pairs[name])]
    unnamed x21 -> x40, local copies, waits for them, and re-layouts: 2.4 us -> 6.12 us
    dot_general x27 -> x11, matrix products: 25.2 us -> 22.6 us  [the longest x5 10.9 us: scores(): lax.dot_general(coef, images, (((0,), (0,)), ((), ())), preferred_element...]
    convert_element_type x4 -> x6, other arithmetic: 2.61 us -> 0.21 us  [the longest x2 0.14 us: unpacked(): x = x.astype(f32)]
    slice x0 -> x7, local copies, waits for them, and re-layouts: none -> 2.29 us  [the longest x3 1.45 us: block(): return x[k * rows:(k + 1) * rows]]
  transfers between devices with their start and end apart: 18 -> 16, of which waited for: 5 -> 9; matrix products, arithmetic and copies ran while one was open for 15% -> 13% of each run, Pallas kernels for 0% -> 0%
where the time goes in v1:
time: 174 us; the launch traced here: 173 us
  starting transfers between devices  76.9 us (44%)
  waiting for transfers between devices  53.3 us (31%)
  matrix products  22.6 us (13%)
  local copies, waits for them, and re-layouts  9.58 us (6%)
  other arithmetic  7.89 us (5%)
  between operations  2.53 us (1%)
    ppermute x11, starting transfers between devices, send(): return lax.ppermute(x, AXES, pairs[name])  66.3 us
    ppermute x11, waiting for transfers between devices, send(): return lax.ppermute(x, AXES, pairs[name])  44 us
    dot_general x5, matrix products, scores(): lax.dot_general(coef, images, (((0,), (0,)), ((), ())), preferred_element...  10.9 us
    ppermute x5, starting transfers between devices, send_back(): return lax.ppermute(x, AXES, [(b, a) for a, b in pairs[name]])  10.6 us
    ppermute x5, waiting for transfers between devices, send_back(): return lax.ppermute(x, AXES, [(b, a) for a, b in pairs[name]])  9.32 us
    dot_general x5, matrix products, scores(): lax.dot_general(images, texts, (((1,), (1,)), ((), ())), preferred_elemen...  8.58 us
    unnamed x40, local copies, waits for them, and re-layouts  6.12 us
  transfers between devices with their start and end apart: 16, of which 9 were waited for; matrix products, arithmetic and copies ran while one was open for 13% of the time, Pallas kernels for 0%

profile of v1, /device:TPU:1, one launch (start us, length us, event | category | flops | bytes accessed | tf_op | source)
XLA Modules:
  0.0 172.8 jit_solution(11711933864128610422)
XLA Ops:
  0.6 1.4 copy.19
  2.0 0.1 multiply_reduce_fusion.2
  2.2 0.2 copy.18
  2.4 0.1 multiply_reduce_fusion.3
  2.6 0.8 constant_dynamic-update-slice_fusion.3
  3.5 0.1 pad_maximum_fusion.2
  3.5 8.8 %collective-permute-start = (bf16[256,1152]{0,1:T(8,128)(2,1)S(1)}, bf16[256,1152]{0,1:T(8,128)(2,1)S(1)}, u32[]{:S(2)}, u32[]{:S(2)}) collective-permute-start(bf16[256,1152]{0,1:T(8,128)(2,1)S(1)} %pad_maximum_fusion.2), channel_id=1, source_target_pairs={{0,128},{1,129},{2,130},{3,131},{4,132},{5,133},{6,134},{7,135},{8... | collective-permute-start | bytes 1769480 | tf_op jit(solution)/shard_map/ppermute | solution.py:67
  12.3 5.3 %collective-permute-start.1 = (bf16[128,1152]{0,1:T(8,128)(2,1)S(1)}, bf16[128,1152]{0,1:T(8,128)(2,1)}, u32[]{:S(2)}, u32[]{:S(2)}) collective-permute-start(bf16[128,1152]{0,1:T(8,128)(2,1)S(1)} %fusion.23), channel_id=1, source_target_pairs={{0,256},{1,257},{2,258},{3,259},{4,260},{5,261},{6,262},{7,263},{8... | collective-permute-start | bytes 884744 | tf_op jit(solution)/shard_map/ppermute | solution.py:67
  17.7 0.1 pad_maximum_fusion.1
  17.7 3.4 %collective-permute-start.3 = (bf16[256,1152]{0,1:T(8,128)(2,1)S(1)}, bf16[256,1152]{0,1:T(8,128)(2,1)}, u32[]{:S(2)}, u32[]{:S(2)}) collective-permute-start(bf16[256,1152]{0,1:T(8,128)(2,1)S(1)} %pad_maximum_fusion.1), channel_id=1, source_target_pairs={{0,1},{1,2},{2,3},{3,255},{4,5},{5,6},{6,7},{7,131},{8,9},{9,10},{... | collective-permute-start | bytes 1769480 | tf_op jit(solution)/shard_map/ppermute | solution.py:67
  21.1 1.3 collective-permute-start.5
  22.4 6.6 %collective-permute-done.1 = bf16[128,1152]{0,1:T(8,128)(2,1)} collective-permute-done((bf16[128,1152]{0,1:T(8,128)(2,1)S(1)}, bf16[128,1152]{0,1:T(8,128)(2,1)}, u32[]{:S(2)}, u32[]{:S(2)}) %collective-permute-start.1) | collective-permute-done | bytes 294944 | tf_op jit(solution)/shard_map/ppermute | solution.py:67
  29.0 4.9 %collective-permute-start.2 = (bf16[128,1152]{0,1:T(8,128)(2,1)}, bf16[128,1152]{0,1:T(8,128)(2,1)}, u32[]{:S(2)}, u32[]{:S(2)}) collective-permute-start(bf16[128,1152]{0,1:T(8,128)(2,1)} %collective-permute-done.1), channel_id=1, source_target_pairs={{0,128},{1,129},{2,130},{3,131},{4,132},{5,133},{6,134},{7,135},{8... | collective-permute-start | bytes 884744 | tf_op jit(solution)/shard_map/ppermute | solution.py:67
  35.2 0.2 collective-permute-done.2
  35.4 1.6 constant_dynamic-update-slice_fusion.8
  37.0 1.7 %collective-permute-done.3 = bf16[256,1152]{0,1:T(8,128)(2,1)} collective-permute-done((bf16[256,1152]{0,1:T(8,128)(2,1)S(1)}, bf16[256,1152]{0,1:T(8,128)(2,1)}, u32[]{:S(2)}, u32[]{:S(2)}) %collective-permute-start.3) | collective-permute-done | bytes 589856 | tf_op jit(solution)/shard_map/ppermute | solution.py:67
  38.8 12.5 %collective-permute-done.5 = bf16[256,1152]{0,1:T(8,128)(2,1)S(1)} collective-permute-done((bf16[256,1152]{0,1:T(8,128)(2,1)S(1)}, bf16[256,1152]{0,1:T(8,128)(2,1)S(1)}, u32[]{:S(2)}, u32[]{:S(2)}) %collective-permute-start.5) | collective-permute-done | bytes 589856 | tf_op jit(solution)/shard_map/ppermute | solution.py:67
  51.3 1.4 select_select_fusion
  52.7 1.9 %collective-permute-start.4 = (bf16[256,1152]{0,1:T(8,128)(2,1)S(1)}, bf16[256,1152]{0,1:T(8,128)(2,1)S(1)}, u32[]{:S(2)}, u32[]{:S(2)}) collective-permute-start(bf16[256,1152]{0,1:T(8,128)(2,1)S(1)} %get-tuple-element.15), channel_id=1, source_target_pairs={{0,3},{1,253},{2,254},{3,255},{4,7},{5,129},{6,130},{7,131},{8,11}... | collective-permute-start | bytes 1769480 | tf_op jit(solution)/shard_map/ppermute | solution.py:67
  54.6 0.2 fusion.17
  54.8 6.2 %collective-permute-start.6 = (bf16[256,1152]{0,1:T(8,128)(2,1)S(1)}, bf16[256,1152]{0,1:T(8,128)(2,1)S(1)}, u32[]{:S(2)}, u32[]{:S(2)}) collective-permute-start(bf16[256,1152]{0,1:T(8,128)(2,1)S(1)} %get-tuple-element.14), channel_id=1, source_target_pairs={{0,252},{1,253},{2,254},{3,255},{4,128},{5,129},{6,130},{7,131},{8... | collective-permute-start | bytes 1769480 | tf_op jit(solution)/shard_map/ppermute | solution.py:67
  60.9 1.9 %constant_dynamic-update-slice_fusion.7 = (bf16[512,1152]{0,1:T(8,128)(2,1)S(1)}, f32[512,256]{0,1:T(8,128)S(1)}) fusion(bf16[512,1152]{0,1:T(8,128)(2,1)S(1)} %get-tuple-element.23, f32[]{:T(128)} %bitcast.23, f32[]{:T(128)} %bitcast.29, bf16[256,1152]{0,1:T(8,128)(2,1)} %collective-permute-done.3, bf16[128,1152]{0,1:T(8,128)(2,1)} %collective-permute-done.2, ...), kind=kOutput, calls=%fused_computation.70 | convolution fusion | flops 307625984 | bytes 2555912 | tf_op jit(solution)/shard_map/dot_general | solution.py:48
  62.8 0.3 fusion.13
  63.1 2.2 %collective-permute-done.4 = bf16[256,1152]{0,1:T(8,128)(2,1)S(1)} collective-permute-done((bf16[256,1152]{0,1:T(8,128)(2,1)S(1)}, bf16[256,1152]{0,1:T(8,128)(2,1)S(1)}, u32[]{:S(2)}, u32[]{:S(2)}) %collective-permute-start.4) | collective-permute-done | bytes 589856 | tf_op jit(solution)/shard_map/ppermute | solution.py:67
  65.4 1.7 constant_dynamic-update-slice_fusion.6
  67.1 1.7 collective-permute-done.6
  68.8 1.7 constant_dynamic-update-slice_fusion.5
  70.5 0.3 fusion.15
  70.8 1.6 convolution_convert_fusion
  72.4 3.4 %collective-permute-start.12 = (bf16[256,1152]{0,1:T(8,128)(2,1)S(1)}, bf16[256,1152]{0,1:T(8,128)(2,1)S(1)}, u32[]{:S(2)}, u32[]{:S(2)}) collective-permute-start(bf16[256,1152]{0,1:T(8,128)(2,1)S(1)} %convolution_convert_fusion), channel_id=1, source_target_pairs={{252,0},{253,1},{254,2},{255,3},{128,4},{129,5},{130,6},{131,7},{1... | collective-permute-start | bytes 1769480 | tf_op jit(solution)/shard_map/ppermute | solution.py:70
  75.8 2.2 %collective-permute-start.7 = (bf16[256,1152]{0,1:T(8,128)(2,1)S(1)}, bf16[256,1152]{0,1:T(8,128)(2,1)S(1)}, u32[]{:S(2)}, u32[]{:S(2)}) collective-permute-start(bf16[256,1152]{0,1:T(8,128)(2,1)S(1)} %collective-permute-done.4), channel_id=1, source_target_pairs={{3,255},{7,131},{11,135},{15,139},{19,143},{23,147},{27,151},{31,1... | collective-permute-start | bytes 1769480 | tf_op jit(solution)/shard_map/ppermute | solution.py:67
  78.0 0.3 fusion.14
  78.5 10.4 %collective-permute-done.7 = bf16[256,1152]{0,1:T(8,128)(2,1)S(1)} collective-permute-done((bf16[256,1152]{0,1:T(8,128)(2,1)S(1)}, bf16[256,1152]{0,1:T(8,128)(2,1)S(1)}, u32[]{:S(2)}, u32[]{:S(2)}) %collective-permute-start.7) | collective-permute-done | bytes 589856 | tf_op jit(solution)/shard_map/ppermute | solution.py:67
  88.9 1.7 constant_dynamic-update-slice_fusion.4
  90.6 0.3 fusion.16
  90.9 0.1 fusion.18
  91.1 3.1 %fusion.30 = (bf16[512,1152]{0,1:T(8,128)(2,1)S(1)}, f32[512,1152]{0,1:T(8,128)}) fusion(bf16[1152,1152]{0,1:T(8,128)(2,1)S(1)} %fusion.18, bf16[512,1152]{0,1:T(8,128)(2,1)S(1)} %get-tuple-element.31), kind=kOutput, calls=%fused_computation.95 | convolution fusion | flops 1359544320 | bytes 7372800 | tf_op jit(solution)/shard_map/dot_general | solution.py:124
  94.3 2.9 %fusion.11 = (bf16[256,1152]{0,1:T(8,128)(2,1)}, bf16[256,1152]{0,1:T(8,128)(2,1)}) fusion(bf16[256,1152]{0,1:T(8,128)(2,1)S(1)} %collective-permute-done.12, pred[]{:T(512)S(6)} %ge.4, bf16[128,1152]{0,1:T(8,128)(2,1)} %collective-permute-done.2, bf16[128,1152]{0,1:T(8,128)(2,1)} %collective-permute-done.1, bf16[128,1152]{0,1:T(8,128)(2,1)S(1)} %copy-done.13, ...), kind=kOutput, calls=%fused_computation.28 | convolution fusion | flops 308838400 | bytes 3473413 | tf_op jit(solution)/shard_map/dot_general | solution.py:59
  97.1 1.3 collective-permute-start.10
  98.5 0.7 concatenate.62
  99.3 12.5 %collective-permute-start.8 = (bf16[256,1280]{0,1:T(8,128)(2,1)S(1)}, bf16[256,1280]{0,1:T(8,128)(2,1)S(1)}, u32[]{:S(2)}, u32[]{:S(2)}) collective-permute-start(bf16[256,1280]{0,1:T(8,128)(2,1)S(1)} %concatenate.62), channel_id=1, source_target_pairs={{0,128},{1,129},{2,130},{3,131},{4,132},{5,133},{6,134},{7,135},{8... | collective-permute-start | bytes 1966088 | tf_op jit(solution)/shard_map/ppermute | solution.py:67
  111.8 2.1 %collective-permute-start.14 = (bf16[256,1152]{0,1:T(8,128)(2,1)}, bf16[256,1152]{0,1:T(8,128)(2,1)}, u32[]{:S(2)}, u32[]{:S(2)}) collective-permute-start(bf16[256,1152]{0,1:T(8,128)(2,1)} %get-tuple-element.10), channel_id=1, source_target_pairs={{2,0},{3,1},{254,2},{6,4},{7,5},{130,6},{10,8},{11,9},{134,10},{14... | collective-permute-start | bytes 1769480 | tf_op jit(solution)/shard_map/ppermute | solution.py:70
  114.0 1.4 fusion.27
  115.5 1.9 %fusion.1 = bf16[256,1152]{0,1:T(8,128)(2,1)S(1)} fusion(bf16[256,1152]{0,1:T(8,128)(2,1)} %collective-permute-done.10, f32[512,256]{0,1:T(8,128)S(1)} %copy-done.11, f32[]{:T(128)} %bitcast.26, bf16[128,1152]{0,1:T(8,128)(2,1)} %collective-permute-done.2, bf16[128,1152]{0,1:T(8,128)(2,1)} %collective-permute-done.1, bf16[128,1152]{0,1:T(8,128)(2,1)S(1)} %copy-done.14, ...), kind=kOutput, calls=%fused_computation.3 | convolution fusion | flops 308248576 | bytes 2883588 | tf_op jit(solution)/shard_map/dot_general | solution.py:59
  117.3 1.9 %collective-permute-start.11 = (bf16[256,1152]{0,1:T(8,128)(2,1)S(1)}, bf16[256,1152]{0,1:T(8,128)(2,1)S(1)}, u32[]{:S(2)}, u32[]{:S(2)}) collective-permute-start(bf16[256,1152]{0,1:T(8,128)(2,1)S(1)} %fusion.1), channel_id=1, source_target_pairs={{3,0},{253,1},{254,2},{255,3},{7,4},{129,5},{130,6},{131,7},{11,8}... | collective-permute-start | bytes 1769480 | tf_op jit(solution)/shard_map/ppermute | solution.py:70
  119.3 0.1 convert_element_type.123
  119.4 0.1 slice_add_fusion
  119.5 9.3 %collective-permute-done.11 = bf16[256,1152]{0,1:T(8,128)(2,1)S(1)} collective-permute-done((bf16[256,1152]{0,1:T(8,128)(2,1)S(1)}, bf16[256,1152]{0,1:T(8,128)(2,1)S(1)}, u32[]{:S(2)}, u32[]{:S(2)}) %collective-permute-start.11) | collective-permute-done | bytes 589856 | tf_op jit(solution)/shard_map/ppermute | solution.py:70
  128.8 2.7 %fusion.2 = bf16[256,1152]{0,1:T(8,128)(2,1)} fusion(bf16[256,1152]{0,1:T(8,128)(2,1)S(1)} %collective-permute-done.11, bf16[256,1152]{0,1:T(8,128)(2,1)S(1)} %collective-permute-done.12, pred[]{:T(512)S(6)} %ge.4, pred[]{:T(512)S(6)} %eq.23, f32[512,256]{0,1:T(8,128)S(1)} %copy-done.9, f32[]{:T(128)} %bitcast.25, ...), kind=kOutput, calls=%fused_computation.4 | convolution fusion | flops 309428224 | bytes 3473414 | tf_op jit(solution)/shard_map/dot_general | solution.py:59
  131.6 1.9 %collective-permute-start.13 = (bf16[256,1152]{0,1:T(8,128)(2,1)}, bf16[256,1152]{0,1:T(8,128)(2,1)}, u32[]{:S(2)}, u32[]{:S(2)}) collective-permute-start(bf16[256,1152]{0,1:T(8,128)(2,1)} %fusion.2), channel_id=1, source_target_pairs={{1,0},{2,1},{3,2},{255,3},{5,4},{6,5},{7,6},{131,7},{9,8},{10,9},{... | collective-permute-start | bytes 1769480 | tf_op jit(solution)/shard_map/ppermute | solution.py:70
  133.6 0.4 concatenate.64
  134.0 4.0 %collective-permute-start.9 = (bf16[128,1280]{0,1:T(8,128)(2,1)S(1)}, bf16[128,1280]{0,1:T(8,128)(2,1)S(1)}, u32[]{:S(2)}, u32[]{:S(2)}) collective-permute-start(bf16[128,1280]{0,1:T(8,128)(2,1)S(1)} %concatenate.64), channel_id=1, source_target_pairs={{0,256},{1,257},{2,258},{3,259},{4,260},{5,261},{6,262},{7,263},{8... | collective-permute-start | bytes 983048 | tf_op jit(solution)/shard_map/ppermute | solution.py:67
  138.0 8.6 %collective-permute-done.9 = bf16[128,1280]{0,1:T(8,128)(2,1)S(1)} collective-permute-done((bf16[128,1280]{0,1:T(8,128)(2,1)S(1)}, bf16[128,1280]{0,1:T(8,128)(2,1)S(1)}, u32[]{:S(2)}, u32[]{:S(2)}) %collective-permute-start.9) | collective-permute-done | bytes 327712 | tf_op jit(solution)/shard_map/ppermute | solution.py:67
  146.7 0.2 multiply_reduce_fusion.1
  146.9 1.6 fusion.9
  148.5 1.0 copy-done.2
  149.5 0.8 slice.163
  150.3 15.9 %collective-permute-start.15 = (bf16[128,1152]{0,1:T(8,128)(2,1)}, bf16[128,1152]{0,1:T(8,128)(2,1)}, u32[]{:S(2)}, u32[]{:S(2)}) collective-permute-start(bf16[128,1152]{0,1:T(8,128)(2,1)} %slice.163), channel_id=1, source_target_pairs={{0,128},{1,129},{2,130},{3,131},{4,132},{5,133},{6,134},{7,135},{8... | collective-permute-start | bytes 884744 | tf_op jit(solution)/shard_map/ppermute | solution.py:67
  166.2 0.9 subtract_divide_fusion.1
  167.1 2.2 %copy.29 = f32[128,1152]{1,0:T(8,128)} copy(f32[128,1152]{0,1:T(8,128)} %subtract_divide_fusion.1) | data formatting | bytes 1179648
  169.3 0.5 fusion.21
  169.9 1.8 %multiply_reduce_fusion = (f32[128]{0:T(128)S(1)}, f32[128,1152]{0,1:T(8,128)S(1)}) fusion(f32[128,1152]{0,1:T(8,128)S(1)} %copy.19, f32[128]{0:T(128)S(1)} %add_sqrt_fusion, bf16[128,1152]{0,1:T(8,128)(2,1)} %collective-permute-done.15, f32[256,1152]{0,1:T(8,128)S(1)} %copy-done.3, bf16[128,1152]{0,1:T(8,128)(2,1)} %collective-permute-done.2, ...), kind=kOutput, calls=%fused_computation.41 | convolution fusion | flops 157122432 | bytes 3507204 | tf_op jit(solution)/shard_map/dot_general | solution.py:59
  171.7 0.1 subtract_divide_fusion
  171.8 1.1 copy.30
  (59 shorter events, 0.6 us)
Async XLA Ops:
  0.6 1.4 copy-start
  0.6 1.5 copy-start.1
  3.5 14.1 %collective-permute-start = (bf16[256,1152]{0,1:T(8,128)(2,1)S(1)}, bf16[256,1152]{0,1:T(8,128)(2,1)S(1)}, u32[]{:S(2)}, u32[]{:S(2)}) collective-permute-start(bf16[256,1152]{0,1:T(8,128)(2,1)S(1)} %pad_maximum_fusion.2), channel_id=1, source_target_pairs={{0,128},{1,129},{2,130},{3,131},{4,132},{5,133},{6,134},{7,135},{8... | collective-permute-start | bytes 1769480 | tf_op jit(solution)/shard_map/ppermute | solution.py:67
  12.3 16.7 %collective-permute-start.1 = (bf16[128,1152]{0,1:T(8,128)(2,1)S(1)}, bf16[128,1152]{0,1:T(8,128)(2,1)}, u32[]{:S(2)}, u32[]{:S(2)}) collective-permute-start(bf16[128,1152]{0,1:T(8,128)(2,1)S(1)} %fusion.23), channel_id=1, source_target_pairs={{0,256},{1,257},{2,258},{3,259},{4,260},{5,261},{6,262},{7,263},{8... | collective-permute-start | bytes 884744 | tf_op jit(solution)/shard_map/ppermute | solution.py:67
  17.7 53.1 %copy-start.12 = (bf16[128,1152]{0,1:T(8,128)(2,1)}, bf16[128,1152]{0,1:T(8,128)(2,1)S(1)}, u32[]{:S(2)}) copy-start(bf16[128,1152]{0,1:T(8,128)(2,1)S(1)} %get-tuple-element.16) | copy-start | bytes 884740
  17.7 21.1 %collective-permute-start.3 = (bf16[256,1152]{0,1:T(8,128)(2,1)S(1)}, bf16[256,1152]{0,1:T(8,128)(2,1)}, u32[]{:S(2)}, u32[]{:S(2)}) collective-permute-start(bf16[256,1152]{0,1:T(8,128)(2,1)S(1)} %pad_maximum_fusion.1), channel_id=1, source_target_pairs={{0,1},{1,2},{2,3},{3,255},{4,5},{5,6},{6,7},{7,131},{8,9},{9,10},{... | collective-permute-start | bytes 1769480 | tf_op jit(solution)/shard_map/ppermute | solution.py:67
  21.1 30.1 %collective-permute-start.5 = (bf16[256,1152]{0,1:T(8,128)(2,1)S(1)}, bf16[256,1152]{0,1:T(8,128)(2,1)S(1)}, u32[]{:S(2)}, u32[]{:S(2)}) collective-permute-start(bf16[256,1152]{0,1:T(8,128)(2,1)S(1)} %pad_maximum_fusion.1), channel_id=1, source_target_pairs={{0,2},{1,3},{2,254},{4,6},{5,7},{6,130},{8,10},{9,11},{10,134},{12... | collective-permute-start | bytes 1769480 | tf_op jit(solution)/shard_map/ppermute | solution.py:67
  29.0 6.4 %collective-permute-start.2 = (bf16[128,1152]{0,1:T(8,128)(2,1)}, bf16[128,1152]{0,1:T(8,128)(2,1)}, u32[]{:S(2)}, u32[]{:S(2)}) collective-permute-start(bf16[128,1152]{0,1:T(8,128)(2,1)} %collective-permute-done.1), channel_id=1, source_target_pairs={{0,128},{1,129},{2,130},{3,131},{4,132},{5,133},{6,134},{7,135},{8... | collective-permute-start | bytes 884744 | tf_op jit(solution)/shard_map/ppermute | solution.py:67
  35.4 15.9 %copy-start.16 = (bf16[1152,1152]{0,1:T(8,128)(2,1)S(1)}, bf16[1152,1152]{0,1:T(8,128)(2,1)}, u32[]{:S(2)}) copy-start(bf16[1152,1152]{0,1:T(8,128)(2,1)} %get-tuple-element.6) | copy-start | bytes 7962628
  37.0 25.8 %copy-start.15 = (f32[512,128]{0,1:T(8,128)}, f32[512,128]{0,1:T(8,128)S(1)}, u32[]{:S(2)}) copy-start(f32[512,128]{0,1:T(8,128)S(1)} %get-tuple-element.24) | copy-start | bytes 786436
  52.7 12.7 %collective-permute-start.4 = (bf16[256,1152]{0,1:T(8,128)(2,1)S(1)}, bf16[256,1152]{0,1:T(8,128)(2,1)S(1)}, u32[]{:S(2)}, u32[]{:S(2)}) collective-permute-start(bf16[256,1152]{0,1:T(8,128)(2,1)S(1)} %get-tuple-element.15), channel_id=1, source_target_pairs={{0,3},{1,253},{2,254},{3,255},{4,7},{5,129},{6,130},{7,131},{8,11}... | collective-permute-start | bytes 1769480 | tf_op jit(solution)/shard_map/ppermute | solution.py:67
  54.8 14.0 %collective-permute-start.6 = (bf16[256,1152]{0,1:T(8,128)(2,1)S(1)}, bf16[256,1152]{0,1:T(8,128)(2,1)S(1)}, u32[]{:S(2)}, u32[]{:S(2)}) collective-permute-start(bf16[256,1152]{0,1:T(8,128)(2,1)S(1)} %get-tuple-element.14), channel_id=1, source_target_pairs={{0,252},{1,253},{2,254},{3,255},{4,128},{5,129},{6,130},{7,131},{8... | collective-permute-start | bytes 1769480 | tf_op jit(solution)/shard_map/ppermute | solution.py:67
  62.8 4.3 %copy-start.8 = (f32[512,256]{0,1:T(8,128)}, f32[512,256]{0,1:T(8,128)S(1)}, u32[]{:S(2)}) copy-start(f32[512,256]{0,1:T(8,128)S(1)} %get-tuple-element.26) | copy-start | bytes 1572868
  67.1 11.0 %copy-start.10 = (f32[512,256]{0,1:T(8,128)}, f32[512,256]{0,1:T(8,128)S(1)}, u32[]{:S(2)}) copy-start(f32[512,256]{0,1:T(8,128)S(1)} %get-tuple-element.28) | copy-start | bytes 1572868
  72.4 21.8 %collective-permute-start.12 = (bf16[256,1152]{0,1:T(8,128)(2,1)S(1)}, bf16[256,1152]{0,1:T(8,128)(2,1)S(1)}, u32[]{:S(2)}, u32[]{:S(2)}) collective-permute-start(bf16[256,1152]{0,1:T(8,128)(2,1)S(1)} %convolution_convert_fusion), channel_id=1, source_target_pairs={{252,0},{253,1},{254,2},{255,3},{128,4},{129,5},{130,6},{131,7},{1... | collective-permute-start | bytes 1769480 | tf_op jit(solution)/shard_map/ppermute | solution.py:70
  75.8 13.1 %collective-permute-start.7 = (bf16[256,1152]{0,1:T(8,128)(2,1)S(1)}, bf16[256,1152]{0,1:T(8,128)(2,1)S(1)}, u32[]{:S(2)}, u32[]{:S(2)}) collective-permute-start(bf16[256,1152]{0,1:T(8,128)(2,1)S(1)} %collective-permute-done.4), channel_id=1, source_target_pairs={{3,255},{7,131},{11,135},{15,139},{19,143},{23,147},{27,151},{31,1... | collective-permute-start | bytes 1769480 | tf_op jit(solution)/shard_map/ppermute | solution.py:67
  78.4 10.6 %copy-start.13 = (bf16[128,1152]{0,1:T(8,128)(2,1)S(1)}, bf16[128,1152]{0,1:T(8,128)(2,1)}, u32[]{:S(2)}) copy-start(bf16[128,1152]{0,1:T(8,128)(2,1)} %copy-done.12) | copy-start | bytes 884740
  94.3 34.6 %copy-start.4 = (bf16[256,1152]{0,1:T(8,128)(2,1)}, bf16[256,1152]{0,1:T(8,128)(2,1)S(1)}, u32[]{:S(2)}) copy-start(bf16[256,1152]{0,1:T(8,128)(2,1)S(1)} %collective-permute-done.12) | copy-start | bytes 1769476
  97.1 18.2 %collective-permute-start.10 = (bf16[256,1152]{0,1:T(8,128)(2,1)}, bf16[256,1152]{0,1:T(8,128)(2,1)}, u32[]{:S(2)}, u32[]{:S(2)}) collective-permute-start(bf16[256,1152]{0,1:T(8,128)(2,1)} %get-tuple-element.11), channel_id=1, source_target_pairs={{255,3},{131,7},{135,11},{139,15},{143,19},{147,23},{151,27},{155,... | collective-permute-start | bytes 1769480 | tf_op jit(solution)/shard_map/ppermute | solution.py:70
  99.3 20.0 %collective-permute-start.8 = (bf16[256,1280]{0,1:T(8,128)(2,1)S(1)}, bf16[256,1280]{0,1:T(8,128)(2,1)S(1)}, u32[]{:S(2)}, u32[]{:S(2)}) collective-permute-start(bf16[256,1280]{0,1:T(8,128)(2,1)S(1)} %concatenate.62), channel_id=1, source_target_pairs={{0,128},{1,129},{2,130},{3,131},{4,132},{5,133},{6,134},{7,135},{8... | collective-permute-start | bytes 1966088 | tf_op jit(solution)/shard_map/ppermute | solution.py:67
  111.8 35.0 %collective-permute-start.14 = (bf16[256,1152]{0,1:T(8,128)(2,1)}, bf16[256,1152]{0,1:T(8,128)(2,1)}, u32[]{:S(2)}, u32[]{:S(2)}) collective-permute-start(bf16[256,1152]{0,1:T(8,128)(2,1)} %get-tuple-element.10), channel_id=1, source_target_pairs={{2,0},{3,1},{254,2},{6,4},{7,5},{130,6},{10,8},{11,9},{134,10},{14... | collective-permute-start | bytes 1769480 | tf_op jit(solution)/shard_map/ppermute | solution.py:70
  114.0 1.4 copy-start.11
  114.0 1.5 copy-start.14
  117.3 11.5 %collective-permute-start.11 = (bf16[256,1152]{0,1:T(8,128)(2,1)S(1)}, bf16[256,1152]{0,1:T(8,128)(2,1)S(1)}, u32[]{:S(2)}, u32[]{:S(2)}) collective-permute-start(bf16[256,1152]{0,1:T(8,128)(2,1)S(1)} %fusion.1), channel_id=1, source_target_pairs={{3,0},{253,1},{254,2},{255,3},{7,4},{129,5},{130,6},{131,7},{11,8}... | collective-permute-start | bytes 1769480 | tf_op jit(solution)/shard_map/ppermute | solution.py:70
  119.4 9.4 %copy-start.9 = (f32[512,256]{0,1:T(8,128)S(1)}, f32[512,256]{0,1:T(8,128)}, u32[]{:S(2)}) copy-start(f32[512,256]{0,1:T(8,128)} %copy-done.8) | copy-start | bytes 1572868
  128.8 2.7 %copy-start.6 = (bf16[256,1152]{0,1:T(8,128)(2,1)}, bf16[256,1152]{0,1:T(8,128)(2,1)S(1)}, u32[]{:S(2)}) copy-start(bf16[256,1152]{0,1:T(8,128)(2,1)S(1)} %collective-permute-done.11) | copy-start | bytes 1769476
  131.6 15.3 %collective-permute-start.13 = (bf16[256,1152]{0,1:T(8,128)(2,1)}, bf16[256,1152]{0,1:T(8,128)(2,1)}, u32[]{:S(2)}, u32[]{:S(2)}) collective-permute-start(bf16[256,1152]{0,1:T(8,128)(2,1)} %fusion.2), channel_id=1, source_target_pairs={{1,0},{2,1},{3,2},{255,3},{5,4},{6,5},{7,6},{131,7},{9,8},{10,9},{... | collective-permute-start | bytes 1769480 | tf_op jit(solution)/shard_map/ppermute | solution.py:70
  134.0 12.9 %copy-start.5 = (bf16[256,1152]{0,1:T(8,128)(2,1)S(1)}, bf16[256,1152]{0,1:T(8,128)(2,1)}, u32[]{:S(2)}) copy-start(bf16[256,1152]{0,1:T(8,128)(2,1)} %copy-done.4) | copy-start | bytes 1769476
  134.0 12.9 %copy-start.7 = (bf16[256,1152]{0,1:T(8,128)(2,1)S(1)}, bf16[256,1152]{0,1:T(8,128)(2,1)}, u32[]{:S(2)}) copy-start(bf16[256,1152]{0,1:T(8,128)(2,1)} %copy-done.6) | copy-start | bytes 1769476
  134.0 12.6 %collective-permute-start.9 = (bf16[128,1280]{0,1:T(8,128)(2,1)S(1)}, bf16[128,1280]{0,1:T(8,128)(2,1)S(1)}, u32[]{:S(2)}, u32[]{:S(2)}) collective-permute-start(bf16[128,1280]{0,1:T(8,128)(2,1)S(1)} %concatenate.64), channel_id=1, source_target_pairs={{0,256},{1,257},{2,258},{3,259},{4,260},{5,261},{6,262},{7,263},{8... | collective-permute-start | bytes 983048 | tf_op jit(solution)/shard_map/ppermute | solution.py:67
  148.5 1.0 copy-start.2
  150.3 19.6 %collective-permute-start.15 = (bf16[128,1152]{0,1:T(8,128)(2,1)}, bf16[128,1152]{0,1:T(8,128)(2,1)}, u32[]{:S(2)}, u32[]{:S(2)}) collective-permute-start(bf16[128,1152]{0,1:T(8,128)(2,1)} %slice.163), channel_id=1, source_target_pairs={{0,128},{1,129},{2,130},{3,131},{4,132},{5,133},{6,134},{7,135},{8... | collective-permute-start | bytes 884744 | tf_op jit(solution)/shard_map/ppermute | solution.py:67
  167.1 2.7 %copy-start.3 = (f32[256,1152]{0,1:T(8,128)S(1)}, f32[256,1152]{0,1:T(8,128)}, u32[]{:S(2)}) copy-start(f32[256,1152]{0,1:T(8,128)} %copy-done.2) | copy-start | bytes 3538948

commit v2 on v1

v2 whole, which is shorter than its diff:
```python
import jax
import jax.numpy as jnp
from jax import lax
from jax.sharding import PartitionSpec as P

AXES = ("narrow", "wide")
RUN = 4


def unit_normalize(raw_rows):
    row_size = jnp.sqrt(jnp.sum(raw_rows * raw_rows, axis=1, keepdims=True) + 1e-06)
    return (raw_rows / row_size, row_size)


def backward(gradient, unit_rows, row_size):
    projected = jnp.sum(gradient * unit_rows, axis=1, keepdims=True)
    return (gradient - projected * unit_rows) / row_size


def routes(n_wide):
    def flat(half, core, block):
        return (half * 2 + core) * n_wide + block % n_wide

    names = ("core", "pair", "text0", "text1", "text2", "text3", "small", "big")
    pairs = {name: [] for name in names}
    for half in range(2):
        for core in range(2):
            for block in range(n_wide):
                me = flat(half, core, block)
                run, pair, odd = block // RUN, block // 2 % 2, block % 2
                pairs["core"].append((me, flat(half, 1 - core, block)))
                pairs["pair"].append((me, flat(half, core, block ^ 1)))
                for j in range(4):
                    to_pair = pair if j < 2 else 1 - pair
                    to = flat(odd ^ (j & 1), half, RUN * run + 2 * to_pair + core)
                    pairs[f"text{j}"].append((me, to))
                away = RUN if pair == 0 else -RUN
                pairs["big"].append((me, flat(half, core, block + away)))
                pairs["small"].append((me, flat(half, core, block - away)))
    return pairs


def scores(images, texts, scale, shift, labels=None, mask=None):
    similarity = lax.dot_general(
        images, texts, (((1,), (1,)), ((), ())), preferred_element_type=jnp.float32
    )
    logits = scale * similarity + shift
    if labels is None:
        losses = jax.nn.softplus(logits)
        coef = scale * jax.nn.sigmoid(logits)
    else:
        losses = jax.nn.softplus((1.0 - 2.0 * labels) * logits)
        coef = scale * (jax.nn.sigmoid(logits) - labels)
    if mask is not None:
        losses = jnp.where(mask, losses, 0.0)
        coef = jnp.where(mask, coef, 0.0)
    coef = coef.astype(jnp.bfloat16)
    text_part = lax.dot_general(
        coef, images, (((0,), (0,)), ((), ())), preferred_element_type=jnp.float32
    )
    return coef, jnp.sum(losses, axis=1, keepdims=True), text_part


def make_body(pairs):
    def send(x, name):
        return lax.ppermute(x, AXES, pairs[name])

    def send_back(x, name):
        return lax.ppermute(x, AXES, [(b, a) for a, b in pairs[name]])

    def body(picture_vectors, caption_vectors, sharpness_factor, score_shift_term):
        bf16, f32 = jnp.bfloat16, jnp.float32
        rows, width = picture_vectors.shape
        scale, shift = sharpness_factor[0], score_shift_term[0]
        narrow, wide = lax.axis_index("narrow"), lax.axis_index("wide")
        half, core = narrow // 2, narrow % 2
        pair, odd = wide // 2 % 2, wide % 2

        img_unit, img_size = unit_normalize(picture_vectors)
        txt_unit, txt_size = unit_normalize(caption_vectors)
        img_low, txt_low = img_unit.astype(bf16), txt_unit.astype(bf16)

        got = [send(txt_low, f"text{j}") for j in range(4)]
        img_core = send(img_low, "core")
        img_pair = send(img_low, "pair")
        img_both = send(img_pair, "core")
        images = jnp.concatenate([img_low, img_core, img_pair, img_both])
        near = jnp.concatenate(got[:2])
        far = jnp.concatenate(got[2:])
        got_small = send(near, "small")
        got_big = send(near, "big")
        got_far = send(far, "big")

        row = lax.broadcasted_iota(jnp.int32, (4 * rows, 2 * rows), 0)
        col = lax.broadcasted_iota(jnp.int32, (4 * rows, 2 * rows), 1)
        slot, inner = col // rows, col % rows
        first = jnp.where(odd == core, 0, 3 * rows)
        second = jnp.where(odd == core, 2 * rows, rows)
        match = inner + jnp.where(slot == 0, first, second)
        labels = ((row == match) & (half == core)).astype(f32)
        img_odd = jnp.where(row < 2 * rows, odd, 1 - odd)
        txt_odd = slot ^ half
        later = jnp.where(pair == 0, txt_odd >= img_odd, txt_odd <= img_odd)
        earlier = jnp.where(pair == 0, txt_odd <= img_odd, txt_odd >= img_odd)

        coef_n, loss_n, text_n = scores(images, near, scale, shift, labels=labels)
        coef_s, loss_s, text_s = scores(images, got_small, scale, shift, mask=earlier)
        coef_b, loss_b, text_b = scores(images, got_big, scale, shift, mask=later)
        coef_f, loss_f, text_f = scores(images, far, scale, shift)
        coef_g, loss_g, text_g = scores(images, got_far, scale, shift)

        text_n = (
            text_n
            + send_back(text_s.astype(bf16), "small").astype(f32)
            + send_back(text_b.astype(bf16), "big").astype(f32)
        )
        back0 = send_back(text_n[:rows].astype(bf16), "text0")
        back1 = send_back(text_n[rows:].astype(bf16), "text1")
        text_f = text_f + send_back(text_g.astype(bf16), "big").astype(f32)
        back2 = send_back(text_f[:rows].astype(bf16), "text2")
        back3 = send_back(text_f[rows:].astype(bf16), "text3")
        txt_total = (
            back0.astype(f32) + back1.astype(f32) + back2.astype(f32) + back3.astype(f32)
        )

        coef = jnp.concatenate([coef_n, coef_s, coef_b, coef_f, coef_g], axis=1)
        texts = jnp.concatenate([near, got_small, got_big, far, got_far])
        img_part = jnp.dot(coef, texts, preferred_element_type=f32)
        loss = loss_n + loss_s + loss_b + loss_f + loss_g

        def packed(grad, loss):
            high = loss.astype(bf16)
            low = (loss - high.astype(f32)).astype(bf16)
            pad = jnp.zeros((grad.shape[0], 126), bf16)
            return jnp.concatenate([grad.astype(bf16), high, low, pad], axis=1)

        def unpacked(x):
            x = x.astype(f32)
            return x[:, :width], x[:, width : width + 1] + x[:, width + 1 : width + 2]

        def pick(x, i, j):
            return jnp.concatenate([x[k * rows : (k + 1) * rows] for k in (i, j)])

        grad_in, loss_in = unpacked(
            send(packed(pick(img_part, 1, 3), pick(loss, 1, 3)), "core")
        )
        img_half = pick(img_part, 0, 2) + grad_in
        loss_half = pick(loss, 0, 2) + loss_in
        grad_in, loss_in = unpacked(
            send(packed(img_half[rows:], loss_half[rows:]), "pair")
        )
        img_total = img_half[:rows] + grad_in
        row_loss = (loss_half[:rows] + loss_in)[:, 0]

        grad_images = backward(img_total, img_unit, img_size)
        grad_texts = backward(txt_total, txt_unit, txt_size)
        return (row_loss, grad_images, grad_texts)

    return body


def solution(mesh):
    pairs = routes(mesh.shape["wide"])
    return jax.shard_map(
        make_body(pairs),
        mesh=mesh,
        in_specs=(P(AXES, None), P(AXES, None), P(), P()),
        out_specs=(P(AXES), P(AXES, None), P(AXES, None)),
        check_vma=False,
    )
```

time: 174 us -> 145 us (0.83)
  waiting for transfers between devices: 53.3 us -> 26.2 us
  matrix products: 22.6 us -> 14 us
  starting transfers between devices: 76.9 us -> 82.8 us
  other arithmetic: 7.89 us -> 9.66 us
    ppermute x11 -> x12, waiting for transfers between devices: 44 us -> 20.3 us  [send(): return lax.ppermute(x, AXES, pairs[name])]
    ppermute x5 -> x7, starting transfers between devices: 10.6 us -> 33.4 us  [send_back(): return lax.ppermute(x, AXES, [(b, a) for a, b in pairs[name]])]
    ppermute x11 -> x12, starting transfers between devices: 66.3 us -> 49.4 us  [send(): return lax.ppermute(x, AXES, pairs[name])]
    dot_general x5, matrix products: 8.58 us -> 3.15 us  [scores(): lax.dot_general(images, texts, (((1,), (1,)), ((), ())), preferred_elemen...]
    unnamed x40 -> x34, local copies, waits for them, and re-layouts: 6.12 us -> 1.7 us
    concatenate x2, local copies, waits for them, and re-layouts: 1.16 us -> 4.71 us  [packed(): return jnp.concatenate([grad.astype(bf16), high, low, pad], axis=1)]
    ppermute x5 -> x7, waiting for transfers between devices: 9.32 us -> 5.88 us  [send_back(): return lax.ppermute(x, AXES, [(b, a) for a, b in pairs[name]])]
    dot_general x5, matrix products: 10.9 us -> 7.64 us  [scores(): lax.dot_general(coef, images, (((0,), (0,)), ((), ())), preferred_element...]
  transfers between devices with their start and end apart: 16 -> 19, of which waited for: 9 -> 5; matrix products, arithmetic and copies ran while one was open for 13% -> 20% of each run, Pallas kernels for 0% -> 0%
where the time goes in v2:
time: 145 us; the launch traced here: 144 us
  starting transfers between devices  82.8 us (57%)
  waiting for transfers between devices  26.2 us (18%)
  matrix products  14 us (10%)
  other arithmetic  9.66 us (7%)
  local copies, waits for them, and re-layouts  9.01 us (6%)
  between operations  2.68 us (2%)
    ppermute x12, starting transfers between devices, send(): return lax.ppermute(x, AXES, pairs[name])  49.4 us
    ppermute x7, starting transfers between devices, send_back(): return lax.ppermute(x, AXES, [(b, a) for a, b in pairs[name]])  33.4 us
    ppermute x12, waiting for transfers between devices, send(): return lax.ppermute(x, AXES, pairs[name])  20.3 us
    dot_general x5, matrix products, scores(): lax.dot_general(coef, images, (((0,), (0,)), ((), ())), preferred_element...  7.64 us
    ppermute x7, waiting for transfers between devices, send_back(): return lax.ppermute(x, AXES, [(b, a) for a, b in pairs[name]])  5.88 us
    concatenate x2, local copies, waits for them, and re-layouts, packed(): return jnp.concatenate([grad.astype(bf16), high, low, pad], axis=1)  4.71 us
    dot_general x1, matrix products, body(): img_part = jnp.dot(coef, texts, preferred_element_type=f32)  3.18 us
    dot_general x5, matrix products, scores(): lax.dot_general(images, texts, (((1,), (1,)), ((), ())), preferred_elemen...  3.15 us
  transfers between devices with their start and end apart: 19, of which 5 were waited for; matrix products, arithmetic and copies ran while one was open for 20% of the time, Pallas kernels for 0%

profile of v2, /device:TPU:1, one launch (start us, length us, event | category | flops | bytes accessed | tf_op | source)
XLA Modules:
  0.0 144.3 jit_solution(11190417612772392256)
XLA Ops:
  0.6 1.2 multiply_reduce_fusion.2
  1.9 1.2 fusion.28
  3.1 5.4 %collective-permute-start.3 = (bf16[128,1152]{1,0:T(8,128)(2,1)S(1)}, bf16[128,1152]{1,0:T(8,128)(2,1)S(1)}, u32[]{:S(2)}, u32[]{:S(2)}) collective-permute-start(bf16[128,1152]{1,0:T(8,128)(2,1)S(1)} %fusion.28), channel_id=1, source_target_pairs={{0,0},{1,256},{2,2},{3,258},{4,4},{5,260},{6,6},{7,262},{8,8},{9,2... | collective-permute-start | bytes 884744 | tf_op jit(solution)/shard_map/ppermute | solution.py:66
  8.5 0.2 copy.18
  8.7 0.1 multiply_reduce_fusion.3
  8.9 0.1 fusion.27
  8.9 9.7 %collective-permute-start.1 = (bf16[128,1152]{0,1:T(8,128)(2,1)S(1)}, bf16[128,1152]{0,1:T(8,128)(2,1)S(1)}, u32[]{:S(2)}, u32[]{:S(2)}) collective-permute-start(bf16[128,1152]{0,1:T(8,128)(2,1)S(1)} %fusion.27), channel_id=1, source_target_pairs={{0,1},{1,0},{2,3},{3,2},{4,5},{5,4},{6,7},{7,6},{8,9},{9,8},{10,11... | collective-permute-start | bytes 884744 | tf_op jit(solution)/shard_map/ppermute | solution.py:66
  18.7 1.9 %collective-permute-start.4 = (bf16[128,1152]{1,0:T(8,128)(2,1)S(1)}, bf16[128,1152]{1,0:T(8,128)(2,1)S(1)}, u32[]{:S(2)}, u32[]{:S(2)}) collective-permute-start(bf16[128,1152]{1,0:T(8,128)(2,1)S(1)} %fusion.28), channel_id=1, source_target_pairs={{0,256},{1,0},{2,258},{3,2},{4,260},{5,4},{6,262},{7,6},{8,264},{9... | collective-permute-start | bytes 884744 | tf_op jit(solution)/shard_map/ppermute | solution.py:66
  20.6 2.6 %collective-permute-start = (bf16[128,1152]{0,1:T(8,128)(2,1)S(1)}, bf16[128,1152]{0,1:T(8,128)(2,1)S(1)}, u32[]{:S(2)}, u32[]{:S(2)}) collective-permute-start(bf16[128,1152]{0,1:T(8,128)(2,1)S(1)} %fusion.27), channel_id=1, source_target_pairs={{0,128},{1,129},{2,130},{3,131},{4,132},{5,133},{6,134},{7,135},{8... | collective-permute-start | bytes 884744 | tf_op jit(solution)/shard_map/ppermute | solution.py:66
  23.2 4.4 %collective-permute-start.7 = (bf16[128,1152]{1,0:T(8,128)(2,1)S(1)}, bf16[128,1152]{1,0:T(8,128)(2,1)S(1)}, u32[]{:S(2)}, u32[]{:S(2)}) collective-permute-start(bf16[128,1152]{1,0:T(8,128)(2,1)S(1)} %fusion.28), channel_id=1, source_target_pairs={{0,2},{1,258},{2,0},{3,256},{4,6},{5,262},{6,4},{7,260},{8,10},{9,... | collective-permute-start | bytes 884744 | tf_op jit(solution)/shard_map/ppermute | solution.py:66
  29.0 3.5 %collective-permute-start.8 = (bf16[128,1152]{1,0:T(8,128)(2,1)S(1)}, bf16[128,1152]{1,0:T(8,128)(2,1)S(1)}, u32[]{:S(2)}, u32[]{:S(2)}) collective-permute-start(bf16[128,1152]{1,0:T(8,128)(2,1)S(1)} %fusion.28), channel_id=1, source_target_pairs={{0,258},{1,2},{2,256},{3,0},{4,262},{5,6},{6,260},{7,4},{8,266},{9... | collective-permute-start | bytes 884744 | tf_op jit(solution)/shard_map/ppermute | solution.py:66
  32.5 4.7 %collective-permute-done.1 = bf16[128,1152]{0,1:T(8,128)(2,1)S(1)} collective-permute-done((bf16[128,1152]{0,1:T(8,128)(2,1)S(1)}, bf16[128,1152]{0,1:T(8,128)(2,1)S(1)}, u32[]{:S(2)}, u32[]{:S(2)}) %collective-permute-start.1) | collective-permute-done | bytes 294944 | tf_op jit(solution)/shard_map/ppermute | solution.py:66
  37.2 1.9 %collective-permute-start.2 = (bf16[128,1152]{0,1:T(8,128)(2,1)S(1)}, bf16[128,1152]{0,1:T(8,128)(2,1)S(1)}, u32[]{:S(2)}, u32[]{:S(2)}) collective-permute-start(bf16[128,1152]{0,1:T(8,128)(2,1)S(1)} %collective-permute-done.1), channel_id=1, source_target_pairs={{0,128},{1,129},{2,130},{3,131},{4,132},{5,133},{6,134},{7,135},{8... | collective-permute-start | bytes 884744 | tf_op jit(solution)/shard_map/ppermute | solution.py:66
  39.2 0.1 constant_dynamic-update-slice_fusion.14
  39.2 7.3 %collective-permute-start.5 = (bf16[256,1152]{1,0:T(8,128)(2,1)S(1)}, bf16[256,1152]{1,0:T(8,128)(2,1)S(1)}, u32[]{:S(2)}, u32[]{:S(2)}) collective-permute-start(bf16[256,1152]{1,0:T(8,128)(2,1)S(1)} %get-tuple-element.22), channel_id=1, source_target_pairs={{0,124},{1,125},{2,6},{3,7},{4,0},{5,1},{6,10},{7,11},{8,4},{9,5},... | collective-permute-start | bytes 1769480 | tf_op jit(solution)/shard_map/ppermute | solution.py:66
  46.6 1.9 %collective-permute-start.6 = (bf16[256,1152]{1,0:T(8,128)(2,1)S(1)}, bf16[256,1152]{1,0:T(8,128)(2,1)S(1)}, u32[]{:S(2)}, u32[]{:S(2)}) collective-permute-start(bf16[256,1152]{1,0:T(8,128)(2,1)S(1)} %get-tuple-element.22), channel_id=1, source_target_pairs={{0,4},{1,5},{2,126},{3,127},{4,8},{5,9},{6,2},{7,3},{8,12},{9,13},... | collective-permute-start | bytes 1769480 | tf_op jit(solution)/shard_map/ppermute | solution.py:66
  48.5 0.6 constant_dynamic-update-slice_fusion.8
  49.2 6.7 %collective-permute-done.5 = bf16[256,1152]{1,0:T(8,128)(2,1)S(1)} collective-permute-done((bf16[256,1152]{1,0:T(8,128)(2,1)S(1)}, bf16[256,1152]{1,0:T(8,128)(2,1)S(1)}, u32[]{:S(2)}, u32[]{:S(2)}) %collective-permute-start.5) | collective-permute-done | bytes 589856 | tf_op jit(solution)/shard_map/ppermute | solution.py:66
  55.9 0.1 constant_dynamic-update-slice_fusion.13
  56.0 7.1 %collective-permute-done.6 = bf16[256,1152]{1,0:T(8,128)(2,1)S(1)} collective-permute-done((bf16[256,1152]{1,0:T(8,128)(2,1)S(1)}, bf16[256,1152]{1,0:T(8,128)(2,1)S(1)}, u32[]{:S(2)}, u32[]{:S(2)}) %collective-permute-start.6) | collective-permute-done | bytes 589856 | tf_op jit(solution)/shard_map/ppermute | solution.py:66
  63.1 0.1 constant_dynamic-update-slice_fusion.12
  63.3 0.1 constant_dynamic-update-slice_fusion.10
  63.3 1.9 %collective-permute-start.9 = (bf16[256,1152]{1,0:T(8,128)(2,1)S(1)}, bf16[256,1152]{1,0:T(8,128)(2,1)S(1)}, u32[]{:S(2)}, u32[]{:S(2)}) collective-permute-start(bf16[256,1152]{1,0:T(8,128)(2,1)S(1)} %get-tuple-element.18), channel_id=1, source_target_pairs={{0,4},{1,5},{2,126},{3,127},{4,8},{5,9},{6,2},{7,3},{8,12},{9,13},... | collective-permute-start | bytes 1769480 | tf_op jit(solution)/shard_map/ppermute | solution.py:66
  65.3 0.7 constant_dynamic-update-slice_fusion.7
  65.9 0.7 constant_dynamic-update-slice_fusion.6
  66.6 1.5 %convolution_convert_fusion.1 = bf16[256,1152]{1,0:T(8,128)(2,1)} fusion(f32[512,256]{0,1:T(8,128)S(1)} %get-tuple-element.34, f32[]{:T(128)} %bitcast.28, s32[512]{0:T(512)S(1)} %fusion.20, s32[]{:T(128)S(6)} %select_n.99, s32[256]{0:T(256)S(1)} %get-tuple-element.43, s32[256]{0:T(256)S(1)} %get-tuple-element.46, pred[256]{0:T(512)(128)(4,1)S(1)} %get-tuple-element.41, ...), kind=kOutput, calls=%fused_computation.6 | convolution fusion | flops 308445184 | bytes 2298121 | tf_op jit(solution)/shard_map/dot_general | solution.py:58
  68.1 6.7 %collective-permute-start.13 = (bf16[256,1152]{1,0:T(8,128)(2,1)}, bf16[256,1152]{1,0:T(8,128)(2,1)}, u32[]{:S(2)}, u32[]{:S(2)}) collective-permute-start(bf16[256,1152]{1,0:T(8,128)(2,1)} %convolution_convert_fusion.1), channel_id=1, source_target_pairs={{4,0},{5,1},{126,2},{127,3},{8,4},{9,5},{2,6},{3,7},{12,8},{13,9},... | collective-permute-start | bytes 1769480 | tf_op jit(solution)/shard_map/ppermute | solution.py:69
  74.8 1.5 %convolution_convert_fusion.2 = bf16[256,1152]{1,0:T(8,128)(2,1)} fusion(f32[512,256]{0,1:T(8,128)S(1)} %get-tuple-element.32, f32[]{:T(128)} %bitcast.27, s32[512]{0:T(512)S(1)} %fusion.20, s32[]{:T(128)S(6)} %select_n.99, s32[256]{0:T(256)S(1)} %get-tuple-element.43, s32[256]{0:T(256)S(1)} %get-tuple-element.46, pred[256]{0:T(512)(128)(4,1)S(1)} %get-tuple-element.41, ...), kind=kOutput, calls=%fused_computation.7 | convolution fusion | flops 308445184 | bytes 2298121 | tf_op jit(solution)/shard_map/dot_general | solution.py:58
  76.3 1.9 %collective-permute-start.12 = (bf16[256,1152]{1,0:T(8,128)(2,1)}, bf16[256,1152]{1,0:T(8,128)(2,1)}, u32[]{:S(2)}, u32[]{:S(2)}) collective-permute-start(bf16[256,1152]{1,0:T(8,128)(2,1)} %convolution_convert_fusion.2), channel_id=1, source_target_pairs={{124,0},{125,1},{6,2},{7,3},{0,4},{1,5},{10,6},{11,7},{4,8},{5,9},... | collective-permute-start | bytes 1769480 | tf_op jit(solution)/shard_map/ppermute | solution.py:69
  78.3 0.6 constant_dynamic-update-slice_fusion.5
  78.9 0.3 fusion.15
  79.2 1.5 %fusion.12 = (f32[512]{0:T(512)S(1)}, f32[512]{0:T(512)S(1)}, f32[512]{0:T(512)S(1)}) fusion(f32[512,256]{0,1:T(8,128)S(1)} %get-tuple-element.32, s32[512]{0:T(512)S(1)} %fusion.20, s32[]{:T(128)S(6)} %select_n.99, s32[256]{0:T(256)S(1)} %get-tuple-element.43, s32[256]{0:T(256)S(1)} %get-tuple-element.46, pred[256]{0:T(512)(128)(4,1)S(1)} %get-tuple-element.41, ...), kind=kLoop, calls=%fused_computation.41 | loop fusion | flops 4979200 | bytes 1585678 | tf_op jit(solution)/shard_map/reduce_sum | solution.py:61
  80.7 0.1 constant_dynamic-update-slice_fusion.9
  80.8 0.6 constant_dynamic-update-slice_fusion.4
  81.4 3.2 %fusion.33 = (bf16[512,1152]{0,1:T(8,128)(2,1)S(1)}, f32[512,1152]{0,1:T(8,128)}) fusion(bf16[512,1280]{0,1:T(8,128)(2,1)S(1)} %get-tuple-element.37, bf16[1280,1152]{1,0:T(8,128)(2,1)S(1)} %constant_dynamic-update-slice_fusion.9), kind=kOutput, calls=%fused_computation.106 | convolution fusion | flops 1510539264 | bytes 7798784 | tf_op jit(solution)/shard_map/dot_general | solution.py:128
  84.6 0.3 fusion.16
  85.0 0.1 pad_maximum_fusion.1
  85.1 0.7 concatenate.63
  85.8 6.9 %collective-permute-start.10 = (bf16[256,1280]{0,1:T(8,128)(2,1)S(1)}, bf16[256,1280]{0,1:T(8,128)(2,1)S(1)}, u32[]{:S(2)}, u32[]{:S(2)}) collective-permute-start(bf16[256,1280]{0,1:T(8,128)(2,1)S(1)} %concatenate.63), channel_id=1, source_target_pairs={{0,128},{1,129},{2,130},{3,131},{4,132},{5,133},{6,134},{7,135},{8... | collective-permute-start | bytes 1966088 | tf_op jit(solution)/shard_map/ppermute | solution.py:66
  92.7 1.9 %convolution_convert_fusion = bf16[256,1152]{1,0:T(8,128)(2,1)S(1)} fusion(f32[512,256]{0,1:T(8,128)S(1)} %get-tuple-element.38, f32[]{:T(128)} %bitcast.26, bf16[128,1152]{0,1:T(8,128)(2,1)} %copy-done.11, bf16[128,1152]{0,1:T(8,128)(2,1)} %copy-done.7, bf16[128,1152]{0,1:T(8,128)(2,1)} %copy-done.9, bf16[128,1152]{0,1:T(8,128)(2,1)} %copy-done.5), kind=kOutput, calls=%fused_computation.5 | convolution fusion | flops 307658752 | bytes 2293764 | tf_op jit(solution)/shard_map/dot_general | solution.py:58
  94.7 7.0 %collective-permute-start.16 = (bf16[256,1152]{1,0:T(8,128)(2,1)S(1)}, bf16[256,1152]{1,0:T(8,128)(2,1)S(1)}, u32[]{:S(2)}, u32[]{:S(2)}) collective-permute-start(bf16[256,1152]{1,0:T(8,128)(2,1)S(1)} %convolution_convert_fusion), channel_id=1, source_target_pairs={{4,0},{5,1},{126,2},{127,3},{8,4},{9,5},{2,6},{3,7},{12,8},{13,9},... | collective-permute-start | bytes 1769480 | tf_op jit(solution)/shard_map/ppermute | solution.py:69
  101.7 2.1 %fusion.2 = bf16[256,1152]{1,0:T(8,128)(2,1)S(1)} fusion(bf16[256,1152]{1,0:T(8,128)(2,1)} %collective-permute-done.13, bf16[256,1152]{1,0:T(8,128)(2,1)} %collective-permute-done.12, f32[512,256]{0,1:T(8,128)S(1)} %get-tuple-element.30, f32[]{:T(128)} %bitcast.19, pred[]{:T(512)S(6)} %eq.27, s32[]{:T(128)S(6)} %select_n.97, s32[]{:T(128)S(6)} %select_n.96, ...), kind=kOutput, calls=%fused_computation.4 | convolution fusion | flops 310018048 | bytes 3478029 | tf_op jit(solution)/shard_map/dot_general | solution.py:58
  103.8 0.9 fusion.31
  104.7 2.0 %collective-permute-start.15 = (bf16[128,1152]{1,0:T(8,128)(2,1)}, bf16[128,1152]{1,0:T(8,128)(2,1)S(1)}, u32[]{:S(2)}, u32[]{:S(2)}) collective-permute-start(bf16[128,1152]{1,0:T(8,128)(2,1)} %get-tuple-element.14), channel_id=1, source_target_pairs={{256,0},{0,1},{258,2},{2,3},{260,4},{4,5},{262,6},{6,7},{264,8},{8... | collective-permute-start | bytes 884744 | tf_op jit(solution)/shard_map/ppermute | solution.py:69
  106.8 7.7 %collective-permute-start.14 = (bf16[128,1152]{1,0:T(8,128)(2,1)}, bf16[128,1152]{1,0:T(8,128)(2,1)S(1)}, u32[]{:S(2)}, u32[]{:S(2)}) collective-permute-start(bf16[128,1152]{1,0:T(8,128)(2,1)} %get-tuple-element.13), channel_id=1, source_target_pairs={{0,0},{256,1},{2,2},{258,3},{4,4},{260,5},{6,6},{262,7},{8,8},{264... | collective-permute-start | bytes 884744 | tf_op jit(solution)/shard_map/ppermute | solution.py:69
  114.5 0.1 fusion.29
  114.6 0.6 fusion.1
  115.2 0.9 fusion.32
  116.0 2.8 %collective-permute-start.18 = (bf16[128,1152]{1,0:T(8,128)(2,1)}, bf16[128,1152]{1,0:T(8,128)(2,1)S(1)}, u32[]{:S(2)}, u32[]{:S(2)}) collective-permute-start(bf16[128,1152]{1,0:T(8,128)(2,1)} %get-tuple-element.16), channel_id=1, source_target_pairs={{258,0},{2,1},{256,2},{0,3},{262,4},{6,5},{260,6},{4,7},{266,8},{1... | collective-permute-start | bytes 884744 | tf_op jit(solution)/shard_map/ppermute | solution.py:69
  118.9 5.3 %collective-permute-start.17 = (bf16[128,1152]{1,0:T(8,128)(2,1)}, bf16[128,1152]{1,0:T(8,128)(2,1)}, u32[]{:S(2)}, u32[]{:S(2)}) collective-permute-start(bf16[128,1152]{1,0:T(8,128)(2,1)} %get-tuple-element.15), channel_id=1, source_target_pairs={{2,0},{258,1},{0,2},{256,3},{6,4},{262,5},{4,6},{260,7},{10,8},{26... | collective-permute-start | bytes 884744 | tf_op jit(solution)/shard_map/ppermute | solution.py:69
  124.2 0.1 convert_element_type.123
  124.3 0.1 slice_add_fusion
  124.5 0.5 subtract_convert_fusion.1
  125.0 0.6 broadcast_in_dim.41
  125.6 4.0 %concatenate.65 = bf16[128,1280]{0,1:T(8,128)(2,1)} concatenate(bf16[128,1152]{0,1:T(8,128)(2,1)S(1)} %slice.164, bf16[128,1]{0,1:T(2,128)(2,1)S(1)} %slice.165, bf16[128,1]{0,1:T(2,128)(2,1)} %subtract_convert_fusion.1, bf16[128,126]{0,1:T(8,128)(2,1)} %broadcast_in_dim.41), dimensions={1} | concatenate | bytes 655360 | tf_op jit(solution)/shard_map/concatenate | solution.py:135
  129.6 1.9 %collective-permute-start.11 = (bf16[128,1280]{0,1:T(8,128)(2,1)}, bf16[128,1280]{0,1:T(8,128)(2,1)S(1)}, u32[]{:S(2)}, u32[]{:S(2)}) collective-permute-start(bf16[128,1280]{0,1:T(8,128)(2,1)} %concatenate.65), channel_id=1, source_target_pairs={{0,1},{1,0},{2,3},{3,2},{4,5},{5,4},{6,7},{7,6},{8,9},{9,8},{10,11... | collective-permute-start | bytes 983048 | tf_op jit(solution)/shard_map/ppermute | solution.py:66
  131.5 5.9 %collective-permute-done.17 = bf16[128,1152]{1,0:T(8,128)(2,1)} collective-permute-done((bf16[128,1152]{1,0:T(8,128)(2,1)}, bf16[128,1152]{1,0:T(8,128)(2,1)}, u32[]{:S(2)}, u32[]{:S(2)}) %collective-permute-start.17) | collective-permute-done | bytes 294944 | tf_op jit(solution)/shard_map/ppermute | solution.py:69
  137.4 1.2 multiply_reduce_fusion
  138.7 2.0 %subtract_divide_fusion = f32[128,1152]{1,0:T(8,128)} fusion(f32[128]{0:T(128)S(1)} %multiply_reduce_fusion, f32[128]{0:T(128)S(1)} %add_sqrt_fusion, bf16[128,1152]{1,0:T(8,128)(2,1)S(1)} %collective-permute-done.18, bf16[128,1152]{1,0:T(8,128)(2,1)} %collective-permute-done.17, bf16[128,1152]{1,0:T(8,128)(2,1)S(1)} %collective-permute-done.15, ...), kind=kLoop, calls=%fused_computation.32 | loop fusion | flops 1622016 | bytes 2360320 | tf_op jit(solution)/shard_map/div | solution.py:17
  140.7 1.8 %collective-permute-done.11 = bf16[128,1280]{0,1:T(8,128)(2,1)S(1)} collective-permute-done((bf16[128,1280]{0,1:T(8,128)(2,1)}, bf16[128,1280]{0,1:T(8,128)(2,1)S(1)}, u32[]{:S(2)}, u32[]{:S(2)}) %collective-permute-start.11) | collective-permute-done | bytes 327712 | tf_op jit(solution)/shard_map/ppermute | solution.py:66
  142.5 0.5 fusion.25
  143.0 0.2 multiply_reduce_fusion.1
  143.2 0.1 subtract_divide_fusion.1
  143.3 1.1 copy.22
  (58 shorter events, 0.4 us)
Async XLA Ops:
  0.6 7.9 %copy-start.1 = (f32[128,1152]{1,0:T(8,128)S(1)}, f32[128,1152]{1,0:T(8,128)}, u32[]{:S(2)}) copy-start(f32[128,1152]{1,0:T(8,128)} %param.4) | copy-start | bytes 1769476
  3.1 26.0 %collective-permute-start.3 = (bf16[128,1152]{1,0:T(8,128)(2,1)S(1)}, bf16[128,1152]{1,0:T(8,128)(2,1)S(1)}, u32[]{:S(2)}, u32[]{:S(2)}) collective-permute-start(bf16[128,1152]{1,0:T(8,128)(2,1)S(1)} %fusion.28), channel_id=1, source_target_pairs={{0,0},{1,256},{2,2},{3,258},{4,4},{5,260},{6,6},{7,262},{8,8},{9,2... | collective-permute-start | bytes 884744 | tf_op jit(solution)/shard_map/ppermute | solution.py:66
  8.9 71.8 %copy-start.5 = (bf16[128,1152]{0,1:T(8,128)(2,1)}, bf16[128,1152]{0,1:T(8,128)(2,1)S(1)}, u32[]{:S(2)}) copy-start(bf16[128,1152]{0,1:T(8,128)(2,1)S(1)} %fusion.27) | copy-start | bytes 884740
  8.9 28.3 %collective-permute-start.1 = (bf16[128,1152]{0,1:T(8,128)(2,1)S(1)}, bf16[128,1152]{0,1:T(8,128)(2,1)S(1)}, u32[]{:S(2)}, u32[]{:S(2)}) collective-permute-start(bf16[128,1152]{0,1:T(8,128)(2,1)S(1)} %fusion.27), channel_id=1, source_target_pairs={{0,1},{1,0},{2,3},{3,2},{4,5},{5,4},{6,7},{7,6},{8,9},{9,8},{10,11... | collective-permute-start | bytes 884744 | tf_op jit(solution)/shard_map/ppermute | solution.py:66
  18.7 20.5 %collective-permute-start.4 = (bf16[128,1152]{1,0:T(8,128)(2,1)S(1)}, bf16[128,1152]{1,0:T(8,128)(2,1)S(1)}, u32[]{:S(2)}, u32[]{:S(2)}) collective-permute-start(bf16[128,1152]{1,0:T(8,128)(2,1)S(1)} %fusion.28), channel_id=1, source_target_pairs={{0,256},{1,0},{2,258},{3,2},{4,260},{5,4},{6,262},{7,6},{8,264},{9... | collective-permute-start | bytes 884744 | tf_op jit(solution)/shard_map/ppermute | solution.py:66
  20.6 26.0 %collective-permute-start = (bf16[128,1152]{0,1:T(8,128)(2,1)S(1)}, bf16[128,1152]{0,1:T(8,128)(2,1)S(1)}, u32[]{:S(2)}, u32[]{:S(2)}) collective-permute-start(bf16[128,1152]{0,1:T(8,128)(2,1)S(1)} %fusion.27), channel_id=1, source_target_pairs={{0,128},{1,129},{2,130},{3,131},{4,132},{5,133},{6,134},{7,135},{8... | collective-permute-start | bytes 884744 | tf_op jit(solution)/shard_map/ppermute | solution.py:66
  23.2 40.0 %collective-permute-start.7 = (bf16[128,1152]{1,0:T(8,128)(2,1)S(1)}, bf16[128,1152]{1,0:T(8,128)(2,1)S(1)}, u32[]{:S(2)}, u32[]{:S(2)}) collective-permute-start(bf16[128,1152]{1,0:T(8,128)(2,1)S(1)} %fusion.28), channel_id=1, source_target_pairs={{0,2},{1,258},{2,0},{3,256},{4,6},{5,262},{6,4},{7,260},{8,10},{9,... | collective-permute-start | bytes 884744 | tf_op jit(solution)/shard_map/ppermute | solution.py:66
  29.0 34.2 %collective-permute-start.8 = (bf16[128,1152]{1,0:T(8,128)(2,1)S(1)}, bf16[128,1152]{1,0:T(8,128)(2,1)S(1)}, u32[]{:S(2)}, u32[]{:S(2)}) collective-permute-start(bf16[128,1152]{1,0:T(8,128)(2,1)S(1)} %fusion.28), channel_id=1, source_target_pairs={{0,258},{1,2},{2,256},{3,0},{4,262},{5,6},{6,260},{7,4},{8,266},{9... | collective-permute-start | bytes 884744 | tf_op jit(solution)/shard_map/ppermute | solution.py:66
  37.2 43.6 %copy-start.7 = (bf16[128,1152]{0,1:T(8,128)(2,1)}, bf16[128,1152]{0,1:T(8,128)(2,1)S(1)}, u32[]{:S(2)}) copy-start(bf16[128,1152]{0,1:T(8,128)(2,1)S(1)} %collective-permute-done.1) | copy-start | bytes 884740
  37.2 11.3 %collective-permute-start.2 = (bf16[128,1152]{0,1:T(8,128)(2,1)S(1)}, bf16[128,1152]{0,1:T(8,128)(2,1)S(1)}, u32[]{:S(2)}, u32[]{:S(2)}) collective-permute-start(bf16[128,1152]{0,1:T(8,128)(2,1)S(1)} %collective-permute-done.1), channel_id=1, source_target_pairs={{0,128},{1,129},{2,130},{3,131},{4,132},{5,133},{6,134},{7,135},{8... | collective-permute-start | bytes 884744 | tf_op jit(solution)/shard_map/ppermute | solution.py:66
  39.2 16.7 %collective-permute-start.5 = (bf16[256,1152]{1,0:T(8,128)(2,1)S(1)}, bf16[256,1152]{1,0:T(8,128)(2,1)S(1)}, u32[]{:S(2)}, u32[]{:S(2)}) collective-permute-start(bf16[256,1152]{1,0:T(8,128)(2,1)S(1)} %get-tuple-element.22), channel_id=1, source_target_pairs={{0,124},{1,125},{2,6},{3,7},{4,0},{5,1},{6,10},{7,11},{8,4},{9,5},... | collective-permute-start | bytes 1769480 | tf_op jit(solution)/shard_map/ppermute | solution.py:66
  46.6 34.2 %copy-start.9 = (bf16[128,1152]{0,1:T(8,128)(2,1)}, bf16[128,1152]{0,1:T(8,128)(2,1)S(1)}, u32[]{:S(2)}) copy-start(bf16[128,1152]{0,1:T(8,128)(2,1)S(1)} %collective-permute-done) | copy-start | bytes 884740
  46.6 16.5 %collective-permute-start.6 = (bf16[256,1152]{1,0:T(8,128)(2,1)S(1)}, bf16[256,1152]{1,0:T(8,128)(2,1)S(1)}, u32[]{:S(2)}, u32[]{:S(2)}) collective-permute-start(bf16[256,1152]{1,0:T(8,128)(2,1)S(1)} %get-tuple-element.22), channel_id=1, source_target_pairs={{0,4},{1,5},{2,126},{3,127},{4,8},{5,9},{6,2},{7,3},{8,12},{9,13},... | collective-permute-start | bytes 1769480 | tf_op jit(solution)/shard_map/ppermute | solution.py:66
  48.5 32.2 %copy-start.11 = (bf16[128,1152]{0,1:T(8,128)(2,1)}, bf16[128,1152]{0,1:T(8,128)(2,1)S(1)}, u32[]{:S(2)}) copy-start(bf16[128,1152]{0,1:T(8,128)(2,1)S(1)} %collective-permute-done.2) | copy-start | bytes 884740
  63.3 17.3 %collective-permute-start.9 = (bf16[256,1152]{1,0:T(8,128)(2,1)S(1)}, bf16[256,1152]{1,0:T(8,128)(2,1)S(1)}, u32[]{:S(2)}, u32[]{:S(2)}) collective-permute-start(bf16[256,1152]{1,0:T(8,128)(2,1)S(1)} %get-tuple-element.18), channel_id=1, source_target_pairs={{0,4},{1,5},{2,126},{3,127},{4,8},{5,9},{6,2},{7,3},{8,12},{9,13},... | collective-permute-start | bytes 1769480 | tf_op jit(solution)/shard_map/ppermute | solution.py:66
  68.1 33.5 %collective-permute-start.13 = (bf16[256,1152]{1,0:T(8,128)(2,1)}, bf16[256,1152]{1,0:T(8,128)(2,1)}, u32[]{:S(2)}, u32[]{:S(2)}) collective-permute-start(bf16[256,1152]{1,0:T(8,128)(2,1)} %convolution_convert_fusion.1), channel_id=1, source_target_pairs={{4,0},{5,1},{126,2},{127,3},{8,4},{9,5},{2,6},{3,7},{12,8},{13,9},... | collective-permute-start | bytes 1769480 | tf_op jit(solution)/shard_map/ppermute | solution.py:69
  76.3 25.3 %collective-permute-start.12 = (bf16[256,1152]{1,0:T(8,128)(2,1)}, bf16[256,1152]{1,0:T(8,128)(2,1)}, u32[]{:S(2)}, u32[]{:S(2)}) collective-permute-start(bf16[256,1152]{1,0:T(8,128)(2,1)} %convolution_convert_fusion.2), channel_id=1, source_target_pairs={{124,0},{125,1},{6,2},{7,3},{0,4},{1,5},{10,6},{11,7},{4,8},{5,9},... | collective-permute-start | bytes 1769480 | tf_op jit(solution)/shard_map/ppermute | solution.py:69
  78.9 1.9 %copy-start.3 = (f32[512,256]{0,1:T(8,128)}, f32[512,256]{0,1:T(8,128)S(1)}, u32[]{:S(2)}) copy-start(f32[512,256]{0,1:T(8,128)S(1)} %get-tuple-element.36) | copy-start | bytes 1572868
  85.8 38.3 %collective-permute-start.10 = (bf16[256,1280]{0,1:T(8,128)(2,1)S(1)}, bf16[256,1280]{0,1:T(8,128)(2,1)S(1)}, u32[]{:S(2)}, u32[]{:S(2)}) collective-permute-start(bf16[256,1280]{0,1:T(8,128)(2,1)S(1)} %concatenate.63), channel_id=1, source_target_pairs={{0,128},{1,129},{2,130},{3,131},{4,132},{5,133},{6,134},{7,135},{8... | collective-permute-start | bytes 1966088 | tf_op jit(solution)/shard_map/ppermute | solution.py:66
  92.7 8.9 %copy-start.6 = (bf16[128,1152]{0,1:T(8,128)(2,1)S(1)}, bf16[128,1152]{0,1:T(8,128)(2,1)}, u32[]{:S(2)}) copy-start(bf16[128,1152]{0,1:T(8,128)(2,1)} %copy-done.5) | copy-start | bytes 884740
  92.7 8.9 %copy-start.8 = (bf16[128,1152]{0,1:T(8,128)(2,1)S(1)}, bf16[128,1152]{0,1:T(8,128)(2,1)}, u32[]{:S(2)}) copy-start(bf16[128,1152]{0,1:T(8,128)(2,1)} %copy-done.7) | copy-start | bytes 884740
  92.7 8.9 %copy-start.10 = (bf16[128,1152]{0,1:T(8,128)(2,1)S(1)}, bf16[128,1152]{0,1:T(8,128)(2,1)}, u32[]{:S(2)}) copy-start(bf16[128,1152]{0,1:T(8,128)(2,1)} %copy-done.9) | copy-start | bytes 884740
  92.7 8.9 %copy-start.12 = (bf16[128,1152]{0,1:T(8,128)(2,1)S(1)}, bf16[128,1152]{0,1:T(8,128)(2,1)}, u32[]{:S(2)}) copy-start(bf16[128,1152]{0,1:T(8,128)(2,1)} %copy-done.11) | copy-start | bytes 884740
  94.7 19.9 %collective-permute-start.16 = (bf16[256,1152]{1,0:T(8,128)(2,1)S(1)}, bf16[256,1152]{1,0:T(8,128)(2,1)S(1)}, u32[]{:S(2)}, u32[]{:S(2)}) collective-permute-start(bf16[256,1152]{1,0:T(8,128)(2,1)S(1)} %convolution_convert_fusion), channel_id=1, source_target_pairs={{4,0},{5,1},{126,2},{127,3},{8,4},{9,5},{2,6},{3,7},{12,8},{13,9},... | collective-permute-start | bytes 1769480 | tf_op jit(solution)/shard_map/ppermute | solution.py:69
  101.7 12.8 %copy-start.2 = (f32[512,1152]{0,1:T(8,128)S(1)}, f32[512,1152]{0,1:T(8,128)}, u32[]{:S(2)}) copy-start(f32[512,1152]{0,1:T(8,128)} %get-tuple-element.40) | copy-start | bytes 7077892
  104.7 9.9 %copy-start.4 = (f32[512,256]{0,1:T(8,128)S(1)}, f32[512,256]{0,1:T(8,128)}, u32[]{:S(2)}) copy-start(f32[512,256]{0,1:T(8,128)} %copy-done.3) | copy-start | bytes 1572868
  104.7 26.8 %collective-permute-start.15 = (bf16[128,1152]{1,0:T(8,128)(2,1)}, bf16[128,1152]{1,0:T(8,128)(2,1)S(1)}, u32[]{:S(2)}, u32[]{:S(2)}) collective-permute-start(bf16[128,1152]{1,0:T(8,128)(2,1)} %get-tuple-element.14), channel_id=1, source_target_pairs={{256,0},{0,1},{258,2},{2,3},{260,4},{4,5},{262,6},{6,7},{264,8},{8... | collective-permute-start | bytes 884744 | tf_op jit(solution)/shard_map/ppermute | solution.py:69
  106.8 24.8 %collective-permute-start.14 = (bf16[128,1152]{1,0:T(8,128)(2,1)}, bf16[128,1152]{1,0:T(8,128)(2,1)S(1)}, u32[]{:S(2)}, u32[]{:S(2)}) collective-permute-start(bf16[128,1152]{1,0:T(8,128)(2,1)} %get-tuple-element.13), channel_id=1, source_target_pairs={{0,0},{256,1},{2,2},{258,3},{4,4},{260,5},{6,6},{262,7},{8,8},{264... | collective-permute-start | bytes 884744 | tf_op jit(solution)/shard_map/ppermute | solution.py:69
  116.0 15.5 %collective-permute-start.18 = (bf16[128,1152]{1,0:T(8,128)(2,1)}, bf16[128,1152]{1,0:T(8,128)(2,1)S(1)}, u32[]{:S(2)}, u32[]{:S(2)}) collective-permute-start(bf16[128,1152]{1,0:T(8,128)(2,1)} %get-tuple-element.16), channel_id=1, source_target_pairs={{258,0},{2,1},{256,2},{0,3},{262,4},{6,5},{260,6},{4,7},{266,8},{1... | collective-permute-start | bytes 884744 | tf_op jit(solution)/shard_map/ppermute | solution.py:69
  118.9 18.5 %collective-permute-start.17 = (bf16[128,1152]{1,0:T(8,128)(2,1)}, bf16[128,1152]{1,0:T(8,128)(2,1)}, u32[]{:S(2)}, u32[]{:S(2)}) collective-permute-start(bf16[128,1152]{1,0:T(8,128)(2,1)} %get-tuple-element.15), channel_id=1, source_target_pairs={{2,0},{258,1},{0,2},{256,3},{6,4},{262,5},{4,6},{260,7},{10,8},{26... | collective-permute-start | bytes 884744 | tf_op jit(solution)/shard_map/ppermute | solution.py:69
  124.4 13.0 %copy-start = (f32[128,1152]{1,0:T(8,128)S(1)}, f32[128,1152]{1,0:T(8,128)}, u32[]{:S(2)}) copy-start(f32[128,1152]{1,0:T(8,128)} %param.5) | copy-start | bytes 1769476
  129.6 12.8 %collective-permute-start.11 = (bf16[128,1280]{0,1:T(8,128)(2,1)}, bf16[128,1280]{0,1:T(8,128)(2,1)S(1)}, u32[]{:S(2)}, u32[]{:S(2)}) collective-permute-start(bf16[128,1280]{0,1:T(8,128)(2,1)} %concatenate.65), channel_id=1, source_target_pairs={{0,1},{1,0},{2,3},{3,2},{4,5},{5,4},{6,7},{7,6},{8,9},{9,8},{10,11... | collective-permute-start | bytes 983048 | tf_op jit(solution)/shard_map/ppermute | solution.py:66

commit v3 on v2

v3 whole, which is shorter than its diff:
```python
import functools

import jax
import jax.numpy as jnp
from jax import lax
from jax.experimental import pallas as pl
from jax.experimental.pallas import tpu as pltpu
from jax.sharding import PartitionSpec as P

AXES = ("narrow", "wide")
RUN = 4
TAIL = 16


def routes(n_wide):
    def flat(half, core, block):
        return (half * 2 + core) * n_wide + block % n_wide

    def along(half, core, block, step):
        place = (half * RUN + block % RUN + step) % (2 * RUN)
        return flat(place // RUN, core, block - block % RUN + place % RUN)

    pairs = {name: [] for name in ("core", "pair", "across", "up", "down", "small", "big")}
    for half in range(2):
        for core in range(2):
            for block in range(n_wide):
                me = flat(half, core, block)
                away = RUN if block // 2 % 2 == 0 else -RUN
                pairs["core"].append((me, flat(half, 1 - core, block)))
                pairs["pair"].append((me, flat(half, core, block ^ 1)))
                pairs["across"].append((me, flat(1 - half, core, block)))
                pairs["up"].append((me, along(half, core, block, 2)))
                pairs["down"].append((me, along(half, core, block, -2)))
                pairs["big"].append((me, flat(half, core, block + away)))
                pairs["small"].append((me, flat(half, core, block - away)))
    return pairs


def call(kernel, outs, *args, after=()):
    specs = [pl.BlockSpec(memory_space=pl.ANY) for _ in after] + [
        pl.BlockSpec(memory_space=pltpu.SMEM if a.size == 1 else pltpu.VMEM) for a in args
    ]
    return pl.pallas_call(
        lambda *refs: kernel(*refs[len(after) :]),
        out_shape=outs,
        in_specs=specs,
        out_specs=jax.tree.map(lambda _: pl.BlockSpec(memory_space=pltpu.VMEM), outs),
        compiler_params=pltpu.CompilerParams(vmem_limit_bytes=8 << 20),
        cost_estimate=pl.CostEstimate(flops=1000, bytes_accessed=1000, transcendentals=0),
    )(*after, *args)


def shape(rows, width, dtype):
    return jax.ShapeDtypeStruct((rows, width), dtype)


def normalize_kernel(raw_ref, low_ref):
    raw = raw_ref[...]
    size = jnp.sqrt(jnp.sum(raw * raw, axis=1, keepdims=True) + 1e-06)
    low_ref[...] = (raw / size).astype(low_ref.dtype)


def unit_kernel(kind, rows, flag_ref, scale_ref, shift_ref, texts_ref, *refs):
    images_refs, (coef_ref, loss_ref, part_ref) = refs[:-3], refs[-3:]
    images = jnp.concatenate([r[...] for r in images_refs])
    scale, shift = scale_ref[0], shift_ref[0]
    logits = scale * lax.dot_general(
        texts_ref[...], images, (((1,), (1,)), ((), ())), preferred_element_type=jnp.float32
    ) + shift
    small = jnp.exp(-jnp.abs(logits))
    loss = jnp.maximum(logits, 0.0) + jnp.log1p(small)
    prob = jnp.where(logits >= 0.0, 1.0, small) / (1.0 + small)
    row = lax.broadcasted_iota(jnp.int32, logits.shape, 0)
    col = lax.broadcasted_iota(jnp.int32, logits.shape, 1)
    if kind == "labels":
        same = (row == col) & (row < rows)
        loss = jnp.where(same, jnp.maximum(-logits, 0.0) + jnp.log1p(small), loss)
        prob = prob - jnp.where(same, 1.0, 0.0)
    coef = scale * prob
    if kind == "mask":
        out = (col >= 2 * rows) & (flag_ref[0] != 0)
        loss = jnp.where(out, 0.0, loss)
        coef = jnp.where(out, 0.0, coef)
    coef = coef.astype(jnp.bfloat16)
    coef_ref[...] = coef
    loss_ref[...] = jnp.sum(loss, axis=0, keepdims=True)
    part_ref[...] = jnp.dot(coef, images, preferred_element_type=jnp.float32).astype(
        part_ref.dtype
    )


def image_blocks(n, rows, blocks, refs):
    coefs, texts, losses = refs[:n], refs[n : 2 * n], refs[2 * n : 3 * n]
    grads = []
    for k in blocks:
        total = None
        for coef, text in zip(coefs, texts):
            part = lax.dot_general(
                coef[:, k * rows : (k + 1) * rows],
                text[...],
                (((0,), (0,)), ((), ())),
                preferred_element_type=jnp.float32,
            )
            total = part if total is None else total + part
        grads.append(total)
    loss = losses[0][...]
    for other in losses[1:]:
        loss = loss + other[...]
    loss = jnp.concatenate([loss[:, k * rows : (k + 1) * rows] for k in blocks], axis=1)
    return grads, loss


def pack(ref, grads, loss):
    rows, width = grads[0].shape
    for k, grad in enumerate(grads):
        ref[k * rows : (k + 1) * rows, :] = grad.astype(ref.dtype)
    n = loss.shape[1]
    high = loss.astype(ref.dtype).astype(jnp.float32)
    line = jnp.concatenate([high, loss - high, jnp.zeros((1, width - 2 * n), jnp.float32)], axis=1)
    ref[len(grads) * rows :, :] = jnp.broadcast_to(line, (TAIL, width)).astype(ref.dtype)


def unpack_loss(ref, n):
    line = ref[ref.shape[0] - TAIL :, :].astype(jnp.float32)[:1]
    return line[:, :n] + line[:, n : 2 * n]


def send_kernel(n, rows, *refs):
    grads, loss = image_blocks(n, rows, (1, 3), refs)
    pack(refs[-1], grads, loss)


def keep_kernel(n, rows, *refs):
    grads, loss = image_blocks(n, rows, (0, 2), refs)
    refs[-2][:rows, :] = grads[0]
    refs[-2][rows:, :] = grads[1]
    refs[-1][...] = loss


def half_kernel(rows, grad_ref, loss_ref, got_ref, send_ref, grad_out, loss_out):
    loss = loss_ref[...] + unpack_loss(got_ref, 2 * rows)
    pack(
        send_ref,
        [grad_ref[rows:, :] + got_ref[rows : 2 * rows, :].astype(jnp.float32)],
        loss[:, rows:],
    )
    grad_out[...] = grad_ref[:rows, :] + got_ref[:rows, :].astype(jnp.float32)
    loss_out[...] = loss[:, :rows]


def project(raw, grad):
    size = jnp.sqrt(jnp.sum(raw * raw, axis=1, keepdims=True) + 1e-06)
    unit = raw / size
    along = jnp.sum(grad * unit, axis=1, keepdims=True)
    return (grad - along * unit) / size


def image_end_kernel(rows, raw_ref, grad_ref, loss_ref, got_ref, grad_out, loss_out):
    loss_out[...] = loss_ref[...] + unpack_loss(got_ref, rows)
    grad = grad_ref[...] + got_ref[:rows, :].astype(jnp.float32)
    grad_out[...] = project(raw_ref[...], grad)


def text_end_kernel(raw_ref, *refs):
    grad = refs[0][...].astype(jnp.float32)
    for other in refs[1:-1]:
        grad = grad + other[...].astype(jnp.float32)
    refs[-1][...] = project(raw_ref[...], grad)


def sum_kernel(*refs):
    upper, lower = refs[-2:]
    rows = upper.shape[0]
    total = refs[0][...].astype(jnp.float32)
    for other in refs[1:-2]:
        total = total + other[...].astype(jnp.float32)
    upper[...] = total[:rows].astype(upper.dtype)
    lower[...] = total[rows:].astype(lower.dtype)


def make_body(pairs):
    def send(x, name):
        return lax.ppermute(x, AXES, pairs[name])

    def send_back(x, name):
        return lax.ppermute(x, AXES, [(b, a) for a, b in pairs[name]])

    def body(picture_vectors, caption_vectors, sharpness_factor, score_shift_term):
        bf16, f32, i32 = jnp.bfloat16, jnp.float32, jnp.int32
        rows, width = picture_vectors.shape
        wide = lax.axis_index("wide")
        pair, odd = wide // 2 % 2, wide % 2

        nothing = jnp.zeros((1,), i32)
        out_big = (odd == pair).astype(i32).reshape(1)
        out_small = (odd != pair).astype(i32).reshape(1)

        txt_low = call(normalize_kernel, shape(rows, width, bf16), caption_vectors)
        img_low = call(normalize_kernel, shape(rows, width, bf16), picture_vectors)

        near = jnp.concatenate([txt_low, send(txt_low, "across")])
        far = jnp.concatenate([send(txt_low, "up"), send(txt_low, "down")])
        img_own = jnp.concatenate([img_low, send(img_low, "pair")])
        img_core = send(img_own, "core")
        got_small = send(near, "small")
        got_big = send(near, "big")
        got_far = send(far, "big")

        def unit(kind, flag, texts, dtype):
            outs = (
                shape(2 * rows, 4 * rows, bf16),
                shape(1, 4 * rows, f32),
                shape(2 * rows, width, dtype),
            )
            kernel = functools.partial(unit_kernel, kind, rows)
            images = [
                img_own[:rows], img_core[:rows], img_own[rows:], img_core[rows:]
            ]
            return call(kernel, outs, flag, sharpness_factor, score_shift_term, texts, *images)

        coef_n, loss_n, text_n = unit("labels", nothing, near, f32)
        coef_s, loss_s, text_s = unit("mask", out_small, got_small, bf16)
        coef_b, loss_b, text_b = unit("mask", out_big, got_big, bf16)
        coef_f, loss_f, text_f = unit("plain", nothing, far, f32)
        coef_g, loss_g, text_g = unit("plain", nothing, got_far, bf16)

        ordered = lax.optimization_barrier
        back_b, back_s = send_back(text_b, "big"), send_back(text_s, "small")
        total = ordered(text_n + back_b.astype(f32))
        total = ordered(total + back_s.astype(f32))
        total = ordered(jnp.concatenate([total[rows:], total[:rows]]))
        away, home = ordered((total[:rows].astype(bf16), total[rows:]))
        back_across = send_back(away, "across")
        total = text_f + send_back(text_g, "big").astype(f32)
        far0, far1 = ordered((total[:rows].astype(bf16), total[rows:].astype(bf16)))
        back_up, back_down = send_back(far0, "up"), send_back(far1, "down")

        units = (
            coef_n, coef_s, coef_b, coef_f, coef_g,
            near, got_small, got_big, far, got_far,
            loss_n, loss_s, loss_b, loss_f, loss_g,
        )
        packed = call(
            functools.partial(send_kernel, 5, rows), shape(2 * rows + TAIL, width, bf16), *units
        )
        img_part, loss = call(
            functools.partial(keep_kernel, 5, rows),
            (shape(2 * rows, width, f32), shape(1, 2 * rows, f32)),
            *units,
        )
        packed, img_part, loss = call(
            functools.partial(half_kernel, rows),
            (shape(rows + TAIL, width, bf16), shape(rows, width, f32), shape(1, rows, f32)),
            img_part, loss, send(packed, "core"),
        )
        grad_images, row_loss = call(
            functools.partial(image_end_kernel, rows),
            (shape(rows, width, f32), shape(1, rows, f32)),
            picture_vectors, img_part, loss, send(packed, "pair"),
        )
        grad_texts = call(
            text_end_kernel, shape(rows, width, f32),
            caption_vectors, home, back_across, back_up, back_down,
        )
        return (row_loss.reshape(rows), grad_images, grad_texts)

    return body


def solution(mesh):
    pairs = routes(mesh.shape["wide"])
    return jax.shard_map(
        make_body(pairs),
        mesh=mesh,
        in_specs=(P(AXES, None), P(AXES, None), P(), P()),
        out_specs=(P(AXES), P(AXES, None), P(AXES, None)),
        check_vma=False,
    )
```

time: 145 us -> 134 us (0.924)
  the two profiles are of different devices: /device:TPU:1 before, /device:TPU:64 now
where the time goes in v3:
time: 134 us; the launch traced here: 133 us
  starting transfers between devices  66.9 us (50%)
  waiting for transfers between devices  44 us (33%)
  Pallas kernels  13 us (10%)
  local copies, waits for them, and re-layouts  3.91 us (3%)
  other arithmetic  2.6 us (2%)
  between operations  2.35 us (2%)
    ppermute x10, starting transfers between devices, send(): return lax.ppermute(x, AXES, pairs[name])  43.7 us
    ppermute x6, waiting for transfers between devices, send_back(): return lax.ppermute(x, AXES, [(b, a) for a, b in pairs[name]])  28.6 us
    ppermute x6, starting transfers between devices, send_back(): return lax.ppermute(x, AXES, [(b, a) for a, b in pairs[name]])  23.2 us
    ppermute x10, waiting for transfers between devices, send(): return lax.ppermute(x, AXES, pairs[name])  15.4 us
    pallas_call x12, Pallas kernels, call(): pl.pallas_call(lambda *refs: kernel(*refs[len(after):]), out_shape=outs,...  13 us
    unnamed x21, local copies, waits for them, and re-layouts  3.63 us
  transfers between devices with their start and end apart: 16, of which 8 were waited for; matrix products, arithmetic and copies ran while one was open for 3% of the time, Pallas kernels for 9%

profile of v3, /device:TPU:64, one launch (start us, length us, event | category | flops | bytes accessed | tf_op | source)
XLA Modules:
  0.0 132.8 jit_solution(10923899717127366593)
XLA Ops:
  0.6 0.0 copy-start.2
  0.6 1.1 copy-done.2
  1.7 0.2 shard_map.68.refs_4_
  1.9 7.1 %collective-permute-start.1 = (bf16[128,1152]{1,0:T(8,128)(2,1)S(1)}, bf16[128,1152]{1,0:T(8,128)(2,1)S(1)}, u32[]{:S(2)}, u32[]{:S(2)}) collective-permute-start(bf16[128,1152]{1,0:T(8,128)(2,1)S(1)} %shard_map.68.refs_4_), channel_id=1, source_target_pairs={{0,1},{1,0},{2,3},{3,2},{4,5},{5,4},{6,7},{7,6},{8,9},{9,8},{10,11... | collective-permute-start | bytes 884744 | tf_op jit(solution)/shard_map/ppermute | solution.py:183
  8.9 0.0 copy-done.4
  8.9 0.2 shard_map.67
  9.1 5.5 %collective-permute-start = (bf16[128,1152]{1,0:T(8,128)(2,1)S(1)}, bf16[128,1152]{1,0:T(8,128)(2,1)S(1)}, u32[]{:S(2)}, u32[]{:S(2)}) collective-permute-start(bf16[128,1152]{1,0:T(8,128)(2,1)S(1)} %shard_map.67), channel_id=1, source_target_pairs={{0,256},{1,257},{2,258},{3,259},{4,260},{5,261},{6,262},{7,263},{8... | collective-permute-start | bytes 884744 | tf_op jit(solution)/shard_map/ppermute | solution.py:183
  14.7 4.3 %collective-permute-start.5 = (bf16[128,1152]{1,0:T(8,128)(2,1)S(1)}, bf16[128,1152]{1,0:T(8,128)(2,1)}, u32[]{:S(2)}, u32[]{:S(2)}) collective-permute-start(bf16[128,1152]{1,0:T(8,128)(2,1)S(1)} %shard_map.67), channel_id=1, source_target_pairs={{0,2},{1,3},{2,256},{3,257},{4,6},{5,7},{6,260},{7,261},{8,10},{9,... | collective-permute-start | bytes 884744 | tf_op jit(solution)/shard_map/ppermute | solution.py:183
  19.0 3.7 %collective-permute-start.6 = (bf16[128,1152]{1,0:T(8,128)(2,1)S(1)}, bf16[128,1152]{1,0:T(8,128)(2,1)S(1)}, u32[]{:S(2)}, u32[]{:S(2)}) collective-permute-start(bf16[128,1152]{1,0:T(8,128)(2,1)S(1)} %shard_map.67), channel_id=1, source_target_pairs={{0,258},{1,259},{2,0},{3,1},{4,262},{5,263},{6,4},{7,5},{8,266},{9... | collective-permute-start | bytes 884744 | tf_op jit(solution)/shard_map/ppermute | solution.py:183
  24.0 0.0 collective-permute-done.1.refs_6_
  24.0 1.9 %collective-permute-start.2 = (bf16[256,1152]{1,0:T(8,128)(2,1)S(1)}, bf16[256,1152]{1,0:T(8,128)(2,1)S(1)}, u32[]{:S(2)}, u32[]{:S(2)}) collective-permute-start(bf16[256,1152]{1,0:T(8,128)(2,1)S(1)} %pad_maximum_fusion.2), channel_id=1, source_target_pairs={{0,128},{1,129},{2,130},{3,131},{4,132},{5,133},{6,134},{7,135},{8... | collective-permute-start | bytes 1769480 | tf_op jit(solution)/shard_map/ppermute | solution.py:183
  25.9 4.8 %collective-permute-done = bf16[128,1152]{1,0:T(8,128)(2,1)S(1)} collective-permute-done((bf16[128,1152]{1,0:T(8,128)(2,1)S(1)}, bf16[128,1152]{1,0:T(8,128)(2,1)S(1)}, u32[]{:S(2)}, u32[]{:S(2)}) %collective-permute-start) | collective-permute-done | bytes 294944 | tf_op jit(solution)/shard_map/ppermute | solution.py:183
  30.8 3.5 %collective-permute-start.4 = (bf16[256,1152]{1,0:T(8,128)(2,1)S(1)}, bf16[256,1152]{1,0:T(8,128)(2,1)S(1)}, u32[]{:S(2)}, u32[]{:S(2)}) collective-permute-start(bf16[256,1152]{1,0:T(8,128)(2,1)S(1)} %pad_maximum_fusion.1.refs_3_.refs_5_), channel_id=1, source_target_pairs={{0,4},{1,5},{2,126},{3,127},{4,8},{5,9},{6,2},{7,3},{8,12},{9,13},... | collective-permute-start | bytes 1769480 | tf_op jit(solution)/shard_map/ppermute | solution.py:183
  34.3 6.0 %collective-permute-start.3 = (bf16[256,1152]{1,0:T(8,128)(2,1)S(1)}, bf16[256,1152]{1,0:T(8,128)(2,1)S(1)}, u32[]{:S(2)}, u32[]{:S(2)}) collective-permute-start(bf16[256,1152]{1,0:T(8,128)(2,1)S(1)} %pad_maximum_fusion.1.refs_3_.refs_5_), channel_id=1, source_target_pairs={{0,124},{1,125},{2,6},{3,7},{4,0},{5,1},{6,10},{7,11},{8,4},{9,5},... | collective-permute-start | bytes 1769480 | tf_op jit(solution)/shard_map/ppermute | solution.py:183
  40.3 2.2 %collective-permute-done.5 = bf16[128,1152]{1,0:T(8,128)(2,1)} collective-permute-done((bf16[128,1152]{1,0:T(8,128)(2,1)S(1)}, bf16[128,1152]{1,0:T(8,128)(2,1)}, u32[]{:S(2)}, u32[]{:S(2)}) %collective-permute-start.5) | collective-permute-done | bytes 294944 | tf_op jit(solution)/shard_map/ppermute | solution.py:183
  42.5 1.0 constant_dynamic-update-slice_fusion.1
  43.5 0.0 collective-permute-done.6
  43.5 3.5 %collective-permute-start.7 = (bf16[256,1152]{1,0:T(8,128)(2,1)S(1)}, bf16[256,1152]{1,0:T(8,128)(2,1)S(1)}, u32[]{:S(2)}, u32[]{:S(2)}) collective-permute-start(bf16[256,1152]{1,0:T(8,128)(2,1)S(1)} %constant_dynamic-update-slice_fusion.refs_3_.refs_8_), channel_id=1, source_target_pairs={{0,4},{1,5},{2,126},{3,127},{4,8},{5,9},{6,2},{7,3},{8,12},{9,13},... | collective-permute-start | bytes 1769480 | tf_op jit(solution)/shard_map/ppermute | solution.py:183
  47.0 0.0 collective-permute-done.2
  47.1 0.5 collective-permute-done.4.refs_3_.refs_7_
  47.6 2.1 %shard_map.71 = (bf16[256,512]{1,0:T(8,128)(2,1)S(1)}, f32[1,512]{1,0:T(1,128)S(1)}, bf16[256,1152]{1,0:T(8,128)(2,1)}) custom-call(s32[1]{0:T(128)} %bitcast.1.refs_0_, f32[1]{0:T(128)S(6)} %copy.8.refs_1_, f32[1]{0:T(128)S(6)} %copy.9.refs_2_, bf16[256,1152]{1,0:T(8,128)(2,1)S(1)} %collective-permute-done.4.refs_3_.refs_7_, ...), custom_call_target="tpu_custom_call" | custom-call | flops 1000 | bytes 1000 | tf_op jit(solution)/shard_map/pallas_call | solution.py:43
  49.7 5.6 %collective-permute-start.10 = (bf16[256,1152]{1,0:T(8,128)(2,1)}, bf16[256,1152]{1,0:T(8,128)(2,1)}, u32[]{:S(2)}, u32[]{:S(2)}) collective-permute-start(bf16[256,1152]{1,0:T(8,128)(2,1)} %get-tuple-element.47), channel_id=1, source_target_pairs={{4,0},{5,1},{126,2},{127,3},{8,4},{9,5},{2,6},{3,7},{12,8},{13,9},... | collective-permute-start | bytes 1769480 | tf_op jit(solution)/shard_map/ppermute | solution.py:186
  55.3 7.9 %collective-permute-done.7.refs_3_.refs_9_ = bf16[256,1152]{1,0:T(8,128)(2,1)S(1)} collective-permute-done((bf16[256,1152]{1,0:T(8,128)(2,1)S(1)}, bf16[256,1152]{1,0:T(8,128)(2,1)S(1)}, u32[]{:S(2)}, u32[]{:S(2)}) %collective-permute-start.7) | collective-permute-done | bytes 589856 | tf_op jit(solution)/shard_map/ppermute | solution.py:183
  63.2 2.1 %shard_map.73 = (bf16[256,512]{1,0:T(8,128)(2,1)S(1)}, f32[1,512]{1,0:T(1,128)S(1)}, bf16[256,1152]{1,0:T(8,128)(2,1)}) custom-call(s32[1]{0:T(128)} %constant.28.clone.1.refs_0_, f32[1]{0:T(128)S(6)} %copy.8.refs_1_, f32[1]{0:T(128)S(6)} %copy.9.refs_2_, bf16[256,1152]{1,0:T(8,128)(2,1)S(1)} %collective-permute-done.7.refs_3_.refs_9_, ...), custom_call_target="tpu_custom_call" | custom-call | flops 1000 | bytes 1000 | tf_op jit(solution)/shard_map/pallas_call | solution.py:43
  65.3 0.0 copy-done.6
  65.3 0.8 copy-done
  66.2 0.7 copy-done.8
  66.9 3.6 %collective-permute-start.13 = (bf16[256,1152]{1,0:T(8,128)(2,1)}, bf16[256,1152]{1,0:T(8,128)(2,1)}, u32[]{:S(2)}, u32[]{:S(2)}) collective-permute-start(bf16[256,1152]{1,0:T(8,128)(2,1)} %get-tuple-element.52), channel_id=1, source_target_pairs={{4,0},{5,1},{126,2},{127,3},{8,4},{9,5},{2,6},{3,7},{12,8},{13,9},... | collective-permute-start | bytes 1769480 | tf_op jit(solution)/shard_map/ppermute | solution.py:186
  70.5 0.0 collective-permute-done.3.refs_3_.refs_6_
  70.5 1.3 shard_map.70
  71.8 2.2 %collective-permute-start.11 = (bf16[256,1152]{1,0:T(8,128)(2,1)S(1)}, bf16[256,1152]{1,0:T(8,128)(2,1)S(1)}, u32[]{:S(2)}, u32[]{:S(2)}) collective-permute-start(bf16[256,1152]{1,0:T(8,128)(2,1)S(1)} %get-tuple-element.48), channel_id=1, source_target_pairs={{124,0},{125,1},{6,2},{7,3},{0,4},{1,5},{10,6},{11,7},{4,8},{5,9},... | collective-permute-start | bytes 1769480 | tf_op jit(solution)/shard_map/ppermute | solution.py:186
  74.1 1.3 shard_map.72
  75.4 0.0 copy-start.1
  75.4 0.0 copy-start.7
  75.4 0.0 copy-start.9
  75.4 1.3 shard_map.69
  76.7 0.0 copy-done.1
  76.7 0.0 copy-done.7
  76.7 0.0 copy-done.9
  76.7 1.1 shard_map.75
  77.8 1.9 %collective-permute-start.8 = (bf16[272,1152]{1,0:T(8,128)(2,1)S(1)}, bf16[272,1152]{1,0:T(8,128)(2,1)S(1)}, u32[]{:S(2)}, u32[]{:S(2)}) collective-permute-start(bf16[272,1152]{1,0:T(8,128)(2,1)S(1)} %shard_map.75), channel_id=1, source_target_pairs={{0,128},{1,129},{2,130},{3,131},{4,132},{5,133},{6,134},{7,135},{8... | collective-permute-start | bytes 1880072 | tf_op jit(solution)/shard_map/ppermute | solution.py:183
  79.8 1.1 shard_map.74
  80.8 0.0 collective-permute-done.10
  80.8 1.2 convert_add_fusion.1
  82.0 0.2 collective-permute-done.13
  82.2 1.2 add_convert_fusion
  83.4 6.4 %collective-permute-done.11 = bf16[256,1152]{1,0:T(8,128)(2,1)S(1)} collective-permute-done((bf16[256,1152]{1,0:T(8,128)(2,1)S(1)}, bf16[256,1152]{1,0:T(8,128)(2,1)S(1)}, u32[]{:S(2)}, u32[]{:S(2)}) %collective-permute-start.11) | collective-permute-done | bytes 589856 | tf_op jit(solution)/shard_map/ppermute | solution.py:186
  89.8 0.1 convert_add_fusion
  89.9 0.1 fusion
  90.0 0.0 collective-permute-done.8.refs_2_
  90.0 0.1 shard_map.76
  90.2 6.3 %collective-permute-start.9 = (bf16[144,1152]{1,0:T(8,128)(2,1)S(1)}, bf16[144,1152]{1,0:T(8,128)(2,1)S(1)}, u32[]{:S(2)}, u32[]{:S(2)}) collective-permute-start(bf16[144,1152]{1,0:T(8,128)(2,1)S(1)} %get-tuple-element.43), channel_id=1, source_target_pairs={{0,1},{1,0},{2,3},{3,2},{4,5},{5,4},{6,7},{7,6},{8,9},{9,8},{10,11... | collective-permute-start | bytes 995336 | tf_op jit(solution)/shard_map/ppermute | solution.py:183
  96.5 0.1 pad_maximum_fusion
  96.6 0.0 copy-start.5
  96.7 0.0 copy-start.3
  96.7 3.9 %collective-permute-start.14 = (bf16[128,1152]{1,0:T(8,128)(2,1)S(1)}, bf16[128,1152]{1,0:T(8,128)(2,1)S(1)}, u32[]{:S(2)}, u32[]{:S(2)}) collective-permute-start(bf16[128,1152]{1,0:T(8,128)(2,1)S(1)} %get-tuple-element.53), channel_id=1, source_target_pairs={{2,0},{3,1},{256,2},{257,3},{6,4},{7,5},{260,6},{261,7},{10,8},{11... | collective-permute-start | bytes 884744 | tf_op jit(solution)/shard_map/ppermute | solution.py:186
  100.6 2.9 %collective-permute-start.15 = (bf16[128,1152]{1,0:T(8,128)(2,1)S(1)}, bf16[128,1152]{1,0:T(8,128)(2,1)S(1)}, u32[]{:S(2)}, u32[]{:S(2)}) collective-permute-start(bf16[128,1152]{1,0:T(8,128)(2,1)S(1)} %get-tuple-element.54), channel_id=1, source_target_pairs={{258,0},{259,1},{0,2},{1,3},{262,4},{263,5},{4,6},{5,7},{266,8},{2... | collective-permute-start | bytes 884744 | tf_op jit(solution)/shard_map/ppermute | solution.py:186
  103.6 4.9 %collective-permute-start.12 = (bf16[128,1152]{1,0:T(8,128)(2,1)S(1)}, bf16[128,1152]{1,0:T(8,128)(2,1)S(1)}, u32[]{:S(2)}, u32[]{:S(2)}) collective-permute-start(bf16[128,1152]{1,0:T(8,128)(2,1)S(1)} %slice.52), channel_id=1, source_target_pairs={{256,0},{257,1},{258,2},{259,3},{260,4},{261,5},{262,6},{263,7},{2... | collective-permute-start | bytes 884744 | tf_op jit(solution)/shard_map/ppermute | solution.py:186
  108.5 12.7 %collective-permute-done.14.refs_3_ = bf16[128,1152]{1,0:T(8,128)(2,1)S(1)} collective-permute-done((bf16[128,1152]{1,0:T(8,128)(2,1)S(1)}, bf16[128,1152]{1,0:T(8,128)(2,1)S(1)}, u32[]{:S(2)}, u32[]{:S(2)}) %collective-permute-start.14) | collective-permute-done | bytes 294944 | tf_op jit(solution)/shard_map/ppermute | solution.py:186
  121.2 9.3 %collective-permute-done.15.refs_4_ = bf16[128,1152]{1,0:T(8,128)(2,1)S(1)} collective-permute-done((bf16[128,1152]{1,0:T(8,128)(2,1)S(1)}, bf16[128,1152]{1,0:T(8,128)(2,1)S(1)}, u32[]{:S(2)}, u32[]{:S(2)}) %collective-permute-start.15) | collective-permute-done | bytes 294944 | tf_op jit(solution)/shard_map/ppermute | solution.py:186
  130.5 0.0 collective-permute-done.12.refs_2_
  130.5 1.2 shard_map.78
  131.7 0.0 collective-permute-done.9.refs_3_
  131.7 1.1 shard_map.77
  (13 shorter events, 0.3 us)
Async XLA Ops:
  0.6 1.1 copy-start.2
  1.7 7.2 %copy-start.4 = (f32[128,1152]{1,0:T(8,128)S(1)}, f32[128,1152]{1,0:T(8,128)}, u32[]{:S(2)}) copy-start(f32[128,1152]{1,0:T(8,128)} %refs_0_.7) | copy-start | bytes 1769476
  1.9 22.1 %collective-permute-start.1 = (bf16[128,1152]{1,0:T(8,128)(2,1)S(1)}, bf16[128,1152]{1,0:T(8,128)(2,1)S(1)}, u32[]{:S(2)}, u32[]{:S(2)}) collective-permute-start(bf16[128,1152]{1,0:T(8,128)(2,1)S(1)} %shard_map.68.refs_4_), channel_id=1, source_target_pairs={{0,1},{1,0},{2,3},{3,2},{4,5},{5,4},{6,7},{7,6},{8,9},{9,8},{10,11... | collective-permute-start | bytes 884744 | tf_op jit(solution)/shard_map/ppermute | solution.py:183
  9.1 21.6 %collective-permute-start = (bf16[128,1152]{1,0:T(8,128)(2,1)S(1)}, bf16[128,1152]{1,0:T(8,128)(2,1)S(1)}, u32[]{:S(2)}, u32[]{:S(2)}) collective-permute-start(bf16[128,1152]{1,0:T(8,128)(2,1)S(1)} %shard_map.67), channel_id=1, source_target_pairs={{0,256},{1,257},{2,258},{3,259},{4,260},{5,261},{6,262},{7,263},{8... | collective-permute-start | bytes 884744 | tf_op jit(solution)/shard_map/ppermute | solution.py:183
  14.7 27.9 %collective-permute-start.5 = (bf16[128,1152]{1,0:T(8,128)(2,1)S(1)}, bf16[128,1152]{1,0:T(8,128)(2,1)}, u32[]{:S(2)}, u32[]{:S(2)}) collective-permute-start(bf16[128,1152]{1,0:T(8,128)(2,1)S(1)} %shard_map.67), channel_id=1, source_target_pairs={{0,2},{1,3},{2,256},{3,257},{4,6},{5,7},{6,260},{7,261},{8,10},{9,... | collective-permute-start | bytes 884744 | tf_op jit(solution)/shard_map/ppermute | solution.py:183
  19.0 24.5 %collective-permute-start.6 = (bf16[128,1152]{1,0:T(8,128)(2,1)S(1)}, bf16[128,1152]{1,0:T(8,128)(2,1)S(1)}, u32[]{:S(2)}, u32[]{:S(2)}) collective-permute-start(bf16[128,1152]{1,0:T(8,128)(2,1)S(1)} %shard_map.67), channel_id=1, source_target_pairs={{0,258},{1,259},{2,0},{3,1},{4,262},{5,263},{6,4},{7,5},{8,266},{9... | collective-permute-start | bytes 884744 | tf_op jit(solution)/shard_map/ppermute | solution.py:183
  24.0 23.0 %collective-permute-start.2 = (bf16[256,1152]{1,0:T(8,128)(2,1)S(1)}, bf16[256,1152]{1,0:T(8,128)(2,1)S(1)}, u32[]{:S(2)}, u32[]{:S(2)}) collective-permute-start(bf16[256,1152]{1,0:T(8,128)(2,1)S(1)} %pad_maximum_fusion.2), channel_id=1, source_target_pairs={{0,128},{1,129},{2,130},{3,131},{4,132},{5,133},{6,134},{7,135},{8... | collective-permute-start | bytes 1769480 | tf_op jit(solution)/shard_map/ppermute | solution.py:183
  30.8 16.8 %collective-permute-start.4 = (bf16[256,1152]{1,0:T(8,128)(2,1)S(1)}, bf16[256,1152]{1,0:T(8,128)(2,1)S(1)}, u32[]{:S(2)}, u32[]{:S(2)}) collective-permute-start(bf16[256,1152]{1,0:T(8,128)(2,1)S(1)} %pad_maximum_fusion.1.refs_3_.refs_5_), channel_id=1, source_target_pairs={{0,4},{1,5},{2,126},{3,127},{4,8},{5,9},{6,2},{7,3},{8,12},{9,13},... | collective-permute-start | bytes 1769480 | tf_op jit(solution)/shard_map/ppermute | solution.py:183
  34.3 36.3 %collective-permute-start.3 = (bf16[256,1152]{1,0:T(8,128)(2,1)S(1)}, bf16[256,1152]{1,0:T(8,128)(2,1)S(1)}, u32[]{:S(2)}, u32[]{:S(2)}) collective-permute-start(bf16[256,1152]{1,0:T(8,128)(2,1)S(1)} %pad_maximum_fusion.1.refs_3_.refs_5_), channel_id=1, source_target_pairs={{0,124},{1,125},{2,6},{3,7},{4,0},{5,1},{6,10},{7,11},{8,4},{9,5},... | collective-permute-start | bytes 1769480 | tf_op jit(solution)/shard_map/ppermute | solution.py:183
  43.5 19.6 %collective-permute-start.7 = (bf16[256,1152]{1,0:T(8,128)(2,1)S(1)}, bf16[256,1152]{1,0:T(8,128)(2,1)S(1)}, u32[]{:S(2)}, u32[]{:S(2)}) collective-permute-start(bf16[256,1152]{1,0:T(8,128)(2,1)S(1)} %constant_dynamic-update-slice_fusion.refs_3_.refs_8_), channel_id=1, source_target_pairs={{0,4},{1,5},{2,126},{3,127},{4,8},{5,9},{6,2},{7,3},{8,12},{9,13},... | collective-permute-start | bytes 1769480 | tf_op jit(solution)/shard_map/ppermute | solution.py:183
  49.7 15.6 %copy-start.6 = (bf16[256,512]{1,0:T(8,128)(2,1)}, bf16[256,512]{1,0:T(8,128)(2,1)S(1)}, u32[]{:S(2)}) copy-start(bf16[256,512]{1,0:T(8,128)(2,1)S(1)} %get-tuple-element.31.refs_2_) | copy-start | bytes 786436
  49.7 31.1 %collective-permute-start.10 = (bf16[256,1152]{1,0:T(8,128)(2,1)}, bf16[256,1152]{1,0:T(8,128)(2,1)}, u32[]{:S(2)}, u32[]{:S(2)}) collective-permute-start(bf16[256,1152]{1,0:T(8,128)(2,1)} %get-tuple-element.47), channel_id=1, source_target_pairs={{4,0},{5,1},{126,2},{127,3},{8,4},{9,5},{2,6},{3,7},{12,8},{13,9},... | collective-permute-start | bytes 1769480 | tf_op jit(solution)/shard_map/ppermute | solution.py:186
  65.3 0.8 copy-start
  66.2 0.7 copy-start.8
  66.9 15.4 %collective-permute-start.13 = (bf16[256,1152]{1,0:T(8,128)(2,1)}, bf16[256,1152]{1,0:T(8,128)(2,1)}, u32[]{:S(2)}, u32[]{:S(2)}) collective-permute-start(bf16[256,1152]{1,0:T(8,128)(2,1)} %get-tuple-element.52), channel_id=1, source_target_pairs={{4,0},{5,1},{126,2},{127,3},{8,4},{9,5},{2,6},{3,7},{12,8},{13,9},... | collective-permute-start | bytes 1769480 | tf_op jit(solution)/shard_map/ppermute | solution.py:186
  71.8 17.9 %collective-permute-start.11 = (bf16[256,1152]{1,0:T(8,128)(2,1)S(1)}, bf16[256,1152]{1,0:T(8,128)(2,1)S(1)}, u32[]{:S(2)}, u32[]{:S(2)}) collective-permute-start(bf16[256,1152]{1,0:T(8,128)(2,1)S(1)} %get-tuple-element.48), channel_id=1, source_target_pairs={{124,0},{125,1},{6,2},{7,3},{0,4},{1,5},{10,6},{11,7},{4,8},{5,9},... | collective-permute-start | bytes 1769480 | tf_op jit(solution)/shard_map/ppermute | solution.py:186
  75.4 1.4 %copy-start.1 = (bf16[256,1152]{1,0:T(8,128)(2,1)S(1)}, bf16[256,1152]{1,0:T(8,128)(2,1)}, u32[]{:S(2)}) copy-start(bf16[256,1152]{1,0:T(8,128)(2,1)} %copy-done) | copy-start | bytes 1769476
  75.4 1.4 %copy-start.7 = (bf16[256,512]{1,0:T(8,128)(2,1)S(1)}, bf16[256,512]{1,0:T(8,128)(2,1)}, u32[]{:S(2)}) copy-start(bf16[256,512]{1,0:T(8,128)(2,1)} %copy-done.6) | copy-start | bytes 786436
  75.4 1.4 %copy-start.9 = (bf16[256,512]{1,0:T(8,128)(2,1)S(1)}, bf16[256,512]{1,0:T(8,128)(2,1)}, u32[]{:S(2)}) copy-start(bf16[256,512]{1,0:T(8,128)(2,1)} %copy-done.8) | copy-start | bytes 786436
  77.8 12.2 %collective-permute-start.8 = (bf16[272,1152]{1,0:T(8,128)(2,1)S(1)}, bf16[272,1152]{1,0:T(8,128)(2,1)S(1)}, u32[]{:S(2)}, u32[]{:S(2)}) collective-permute-start(bf16[272,1152]{1,0:T(8,128)(2,1)S(1)} %shard_map.75), channel_id=1, source_target_pairs={{0,128},{1,129},{2,130},{3,131},{4,132},{5,133},{6,134},{7,135},{8... | collective-permute-start | bytes 1880072 | tf_op jit(solution)/shard_map/ppermute | solution.py:183
  90.2 41.5 %collective-permute-start.9 = (bf16[144,1152]{1,0:T(8,128)(2,1)S(1)}, bf16[144,1152]{1,0:T(8,128)(2,1)S(1)}, u32[]{:S(2)}, u32[]{:S(2)}) collective-permute-start(bf16[144,1152]{1,0:T(8,128)(2,1)S(1)} %get-tuple-element.43), channel_id=1, source_target_pairs={{0,1},{1,0},{2,3},{3,2},{4,5},{5,4},{6,7},{7,6},{8,9},{9,8},{10,11... | collective-permute-start | bytes 995336 | tf_op jit(solution)/shard_map/ppermute | solution.py:183
  96.6 33.9 %copy-start.5 = (f32[128,1152]{1,0:T(8,128)S(1)}, f32[128,1152]{1,0:T(8,128)}, u32[]{:S(2)}) copy-start(f32[128,1152]{1,0:T(8,128)} %refs_0_.7) | copy-start | bytes 1769476
  96.7 35.0 %copy-start.3 = (f32[128,1152]{1,0:T(8,128)S(1)}, f32[128,1152]{1,0:T(8,128)}, u32[]{:S(2)}) copy-start(f32[128,1152]{1,0:T(8,128)} %refs_0_.6) | copy-start | bytes 1769476
  96.7 24.6 %collective-permute-start.14 = (bf16[128,1152]{1,0:T(8,128)(2,1)S(1)}, bf16[128,1152]{1,0:T(8,128)(2,1)S(1)}, u32[]{:S(2)}, u32[]{:S(2)}) collective-permute-start(bf16[128,1152]{1,0:T(8,128)(2,1)S(1)} %get-tuple-element.53), channel_id=1, source_target_pairs={{2,0},{3,1},{256,2},{257,3},{6,4},{7,5},{260,6},{261,7},{10,8},{11... | collective-permute-start | bytes 884744 | tf_op jit(solution)/shard_map/ppermute | solution.py:186
  100.6 29.9 %collective-permute-start.15 = (bf16[128,1152]{1,0:T(8,128)(2,1)S(1)}, bf16[128,1152]{1,0:T(8,128)(2,1)S(1)}, u32[]{:S(2)}, u32[]{:S(2)}) collective-permute-start(bf16[128,1152]{1,0:T(8,128)(2,1)S(1)} %get-tuple-element.54), channel_id=1, source_target_pairs={{258,0},{259,1},{0,2},{1,3},{262,4},{263,5},{4,6},{5,7},{266,8},{2... | collective-permute-start | bytes 884744 | tf_op jit(solution)/shard_map/ppermute | solution.py:186
  103.6 26.9 %collective-permute-start.12 = (bf16[128,1152]{1,0:T(8,128)(2,1)S(1)}, bf16[128,1152]{1,0:T(8,128)(2,1)S(1)}, u32[]{:S(2)}, u32[]{:S(2)}) collective-permute-start(bf16[128,1152]{1,0:T(8,128)(2,1)S(1)} %slice.52), channel_id=1, source_target_pairs={{256,0},{257,1},{258,2},{259,3},{260,4},{261,5},{262,6},{263,7},{2... | collective-permute-start | bytes 884744 | tf_op jit(solution)/shard_map/ppermute | solution.py:186

commit v4 on v3

--- a/solution.py
+++ b/solution.py
@@ -126,12 +126,12 @@
 
 
 def send_kernel(n, rows, *refs):
-    grads, loss = image_blocks(n, rows, (1, 3), refs)
+    grads, loss = image_blocks(n, rows, (2, 3), refs)
     pack(refs[-1], grads, loss)
 
 
 def keep_kernel(n, rows, *refs):
-    grads, loss = image_blocks(n, rows, (0, 2), refs)
+    grads, loss = image_blocks(n, rows, (0, 1), refs)
     refs[-2][:rows, :] = grads[0]
     refs[-2][rows:, :] = grads[1]
     refs[-1][...] = loss
@@ -251,16 +251,17 @@
         packed, img_part, loss = call(
             functools.partial(half_kernel, rows),
             (shape(rows + TAIL, width, bf16), shape(rows, width, f32), shape(1, rows, f32)),
-            img_part, loss, send(packed, "core"),
+            img_part, loss, send(packed, "pair"),
         )
         grad_images, row_loss = call(
             functools.partial(image_end_kernel, rows),
             (shape(rows, width, f32), shape(1, rows, f32)),
-            picture_vectors, img_part, loss, send(packed, "pair"),
-        )
+            picture_vectors, img_part, loss, send(packed, "core"),
+        )
+        total = ordered(home + back_across.astype(f32))
+        total = ordered(total + back_up.astype(f32) + back_down.astype(f32))
         grad_texts = call(
-            text_end_kernel, shape(rows, width, f32),
-            caption_vectors, home, back_across, back_up, back_down,
+            text_end_kernel, shape(rows, width, f32), caption_vectors, total
         )
         return (row_loss.reshape(rows), grad_images, grad_texts)
 

time: 134 us -> 123 us (0.918)
  the two profiles are of different devices: /device:TPU:64 before, /device:TPU:54 now
where the time goes in v4:
time: 123 us; the launch traced here: 122 us
  starting transfers between devices  62.6 us (51%)
  waiting for transfers between devices  37.4 us (30%)
  Pallas kernels  15.3 us (12%)
  local copies, waits for them, and re-layouts  3.08 us (3%)
  between operations  2.38 us (2%)
  other arithmetic  1.74 us (1%)
    ppermute x10, starting transfers between devices, send(): return lax.ppermute(x, AXES, pairs[name])  36.4 us
    ppermute x6, starting transfers between devices, send_back(): return lax.ppermute(x, AXES, [(b, a) for a, b in pairs[name]])  26.2 us
    ppermute x6, waiting for transfers between devices, send_back(): return lax.ppermute(x, AXES, [(b, a) for a, b in pairs[name]])  18.7 us
    ppermute x10, waiting for transfers between devices, send(): return lax.ppermute(x, AXES, pairs[name])  18.7 us
    pallas_call x12, Pallas kernels, call(): pl.pallas_call(lambda *refs: kernel(*refs[len(after):]), out_shape=outs,...  15.3 us
    unnamed x15, local copies, waits for them, and re-layouts  2.84 us
  transfers between devices with their start and end apart: 16, of which 7 were waited for; matrix products, arithmetic and copies ran while one was open for 2% of the time, Pallas kernels for 11%

profile of v4, /device:TPU:54, one launch (start us, length us, event | category | flops | bytes accessed | tf_op | source)
XLA Modules:
  0.0 122.5 jit_solution(2550356948721418960)
XLA Ops:
  0.6 0.0 copy-start
  0.6 0.0 copy-start.2
  0.7 1.1 copy-done.2
  1.8 0.2 shard_map.68.refs_4_
  1.9 4.3 %collective-permute-start.1 = (bf16[128,1152]{1,0:T(8,128)(2,1)S(1)}, bf16[128,1152]{1,0:T(8,128)(2,1)S(1)}, u32[]{:S(2)}, u32[]{:S(2)}) collective-permute-start(bf16[128,1152]{1,0:T(8,128)(2,1)S(1)} %shard_map.68.refs_4_), channel_id=1, source_target_pairs={{0,1},{1,0},{2,3},{3,2},{4,5},{5,4},{6,7},{7,6},{8,9},{9,8},{10,11... | collective-permute-start | bytes 884744 | tf_op jit(solution)/shard_map/ppermute | solution.py:183
  6.2 0.0 copy-done
  6.2 0.2 shard_map.67
  6.4 10.0 %collective-permute-start = (bf16[128,1152]{1,0:T(8,128)(2,1)S(1)}, bf16[128,1152]{1,0:T(8,128)(2,1)S(1)}, u32[]{:S(2)}, u32[]{:S(2)}) collective-permute-start(bf16[128,1152]{1,0:T(8,128)(2,1)S(1)} %shard_map.67), channel_id=1, source_target_pairs={{0,256},{1,257},{2,258},{3,259},{4,260},{5,261},{6,262},{7,263},{8... | collective-permute-start | bytes 884744 | tf_op jit(solution)/shard_map/ppermute | solution.py:183
  16.4 4.3 %collective-permute-start.5 = (bf16[128,1152]{1,0:T(8,128)(2,1)S(1)}, bf16[128,1152]{1,0:T(8,128)(2,1)}, u32[]{:S(2)}, u32[]{:S(2)}) collective-permute-start(bf16[128,1152]{1,0:T(8,128)(2,1)S(1)} %shard_map.67), channel_id=1, source_target_pairs={{0,2},{1,3},{2,256},{3,257},{4,6},{5,7},{6,260},{7,261},{8,10},{9,... | collective-permute-start | bytes 884744 | tf_op jit(solution)/shard_map/ppermute | solution.py:183
  20.7 3.7 %collective-permute-start.6 = (bf16[128,1152]{1,0:T(8,128)(2,1)S(1)}, bf16[128,1152]{1,0:T(8,128)(2,1)S(1)}, u32[]{:S(2)}, u32[]{:S(2)}) collective-permute-start(bf16[128,1152]{1,0:T(8,128)(2,1)S(1)} %shard_map.67), channel_id=1, source_target_pairs={{0,258},{1,259},{2,0},{3,1},{4,262},{5,263},{6,4},{7,5},{8,266},{9... | collective-permute-start | bytes 884744 | tf_op jit(solution)/shard_map/ppermute | solution.py:183
  25.7 0.0 collective-permute-done.1.refs_6_
  25.8 1.9 %collective-permute-start.2 = (bf16[256,1152]{1,0:T(8,128)(2,1)S(1)}, bf16[256,1152]{1,0:T(8,128)(2,1)S(1)}, u32[]{:S(2)}, u32[]{:S(2)}) collective-permute-start(bf16[256,1152]{1,0:T(8,128)(2,1)S(1)} %pad_maximum_fusion.2), channel_id=1, source_target_pairs={{0,128},{1,129},{2,130},{3,131},{4,132},{5,133},{6,134},{7,135},{8... | collective-permute-start | bytes 1769480 | tf_op jit(solution)/shard_map/ppermute | solution.py:183
  27.7 10.1 %collective-permute-done = bf16[128,1152]{1,0:T(8,128)(2,1)S(1)} collective-permute-done((bf16[128,1152]{1,0:T(8,128)(2,1)S(1)}, bf16[128,1152]{1,0:T(8,128)(2,1)S(1)}, u32[]{:S(2)}, u32[]{:S(2)}) %collective-permute-start) | collective-permute-done | bytes 294944 | tf_op jit(solution)/shard_map/ppermute | solution.py:183
  37.9 2.6 %collective-permute-start.4 = (bf16[256,1152]{1,0:T(8,128)(2,1)S(1)}, bf16[256,1152]{1,0:T(8,128)(2,1)S(1)}, u32[]{:S(2)}, u32[]{:S(2)}) collective-permute-start(bf16[256,1152]{1,0:T(8,128)(2,1)S(1)} %pad_maximum_fusion.1.refs_3_.refs_5_), channel_id=1, source_target_pairs={{0,4},{1,5},{2,126},{3,127},{4,8},{5,9},{6,2},{7,3},{8,12},{9,13},... | collective-permute-start | bytes 1769480 | tf_op jit(solution)/shard_map/ppermute | solution.py:183
  40.5 3.3 %collective-permute-start.3 = (bf16[256,1152]{1,0:T(8,128)(2,1)S(1)}, bf16[256,1152]{1,0:T(8,128)(2,1)S(1)}, u32[]{:S(2)}, u32[]{:S(2)}) collective-permute-start(bf16[256,1152]{1,0:T(8,128)(2,1)S(1)} %pad_maximum_fusion.1.refs_3_.refs_5_), channel_id=1, source_target_pairs={{0,124},{1,125},{2,6},{3,7},{4,0},{5,1},{6,10},{7,11},{8,4},{9,5},... | collective-permute-start | bytes 1769480 | tf_op jit(solution)/shard_map/ppermute | solution.py:183
  43.7 2.7 %collective-permute-done.5 = bf16[128,1152]{1,0:T(8,128)(2,1)} collective-permute-done((bf16[128,1152]{1,0:T(8,128)(2,1)S(1)}, bf16[128,1152]{1,0:T(8,128)(2,1)}, u32[]{:S(2)}, u32[]{:S(2)}) %collective-permute-start.5) | collective-permute-done | bytes 294944 | tf_op jit(solution)/shard_map/ppermute | solution.py:183
  46.4 1.0 constant_dynamic-update-slice_fusion.1
  47.4 0.0 collective-permute-done.6
  47.5 2.6 %collective-permute-start.7 = (bf16[256,1152]{1,0:T(8,128)(2,1)S(1)}, bf16[256,1152]{1,0:T(8,128)(2,1)}, u32[]{:S(2)}, u32[]{:S(2)}) collective-permute-start(bf16[256,1152]{1,0:T(8,128)(2,1)S(1)} %constant_dynamic-update-slice_fusion.refs_3_.refs_8_), channel_id=1, source_target_pairs={{0,4},{1,5},{2,126},{3,127},{4,8},{5,9},{6,2},{7,3},{8,12},{9,13},... | collective-permute-start | bytes 1769480 | tf_op jit(solution)/shard_map/ppermute | solution.py:183
  50.1 0.0 collective-permute-done.2
  50.1 0.0 collective-permute-done.4.refs_3_.refs_7_
  50.1 2.1 %shard_map.71 = (bf16[256,512]{1,0:T(8,128)(2,1)S(1)}, f32[1,512]{1,0:T(1,128)S(1)}, bf16[256,1152]{1,0:T(8,128)(2,1)}) custom-call(s32[1]{0:T(128)} %bitcast.1.refs_0_, f32[1]{0:T(128)S(6)} %copy.8.refs_1_, f32[1]{0:T(128)S(6)} %copy.9.refs_2_, bf16[256,1152]{1,0:T(8,128)(2,1)S(1)} %collective-permute-done.4.refs_3_.refs_7_, ...), custom_call_target="tpu_custom_call" | custom-call | flops 1000 | bytes 1000 | tf_op jit(solution)/shard_map/pallas_call | solution.py:43
  52.3 0.7 copy-done.4
  53.0 3.3 %collective-permute-start.10 = (bf16[256,1152]{1,0:T(8,128)(2,1)}, bf16[256,1152]{1,0:T(8,128)(2,1)}, u32[]{:S(2)}, u32[]{:S(2)}) collective-permute-start(bf16[256,1152]{1,0:T(8,128)(2,1)} %get-tuple-element.47), channel_id=1, source_target_pairs={{4,0},{5,1},{126,2},{127,3},{8,4},{9,5},{2,6},{3,7},{12,8},{13,9},... | collective-permute-start | bytes 1769480 | tf_op jit(solution)/shard_map/ppermute | solution.py:186
  56.2 0.0 collective-permute-done.3.refs_3_.refs_6_
  56.3 1.3 %shard_map.70 = (bf16[256,512]{1,0:T(8,128)(2,1)S(1)}, f32[1,512]{1,0:T(1,128)S(1)}, bf16[256,1152]{1,0:T(8,128)(2,1)S(1)}) custom-call(s32[1]{0:T(128)} %bitcast.refs_0_, f32[1]{0:T(128)S(6)} %copy.8.refs_1_, f32[1]{0:T(128)S(6)} %copy.9.refs_2_, bf16[256,1152]{1,0:T(8,128)(2,1)S(1)} %collective-permute-done.3.refs_3_.refs_6_, ...), custom_call_target="tpu_custom_call" | custom-call | flops 1000 | bytes 1000 | tf_op jit(solution)/shard_map/pallas_call | solution.py:43
  57.6 2.6 %collective-permute-start.11 = (bf16[256,1152]{1,0:T(8,128)(2,1)S(1)}, bf16[256,1152]{1,0:T(8,128)(2,1)S(1)}, u32[]{:S(2)}, u32[]{:S(2)}) collective-permute-start(bf16[256,1152]{1,0:T(8,128)(2,1)S(1)} %get-tuple-element.48), channel_id=1, source_target_pairs={{124,0},{125,1},{6,2},{7,3},{0,4},{1,5},{10,6},{11,7},{4,8},{5,9},... | collective-permute-start | bytes 1769480 | tf_op jit(solution)/shard_map/ppermute | solution.py:186
  60.2 5.6 %collective-permute-done.7.refs_3_.refs_9_ = bf16[256,1152]{1,0:T(8,128)(2,1)} collective-permute-done((bf16[256,1152]{1,0:T(8,128)(2,1)S(1)}, bf16[256,1152]{1,0:T(8,128)(2,1)}, u32[]{:S(2)}, u32[]{:S(2)}) %collective-permute-start.7) | collective-permute-done | bytes 589856 | tf_op jit(solution)/shard_map/ppermute | solution.py:183
  65.7 2.4 %shard_map.73 = (bf16[256,512]{1,0:T(8,128)(2,1)S(1)}, f32[1,512]{1,0:T(1,128)S(1)}, bf16[256,1152]{1,0:T(8,128)(2,1)S(1)}) custom-call(s32[1]{0:T(128)} %constant.28.clone.1.refs_0_, f32[1]{0:T(128)S(6)} %copy.8.refs_1_, f32[1]{0:T(128)S(6)} %copy.9.refs_2_, bf16[256,1152]{1,0:T(8,128)(2,1)} %collective-permute-done.7.refs_3_.refs_9_, ...), custom_call_target="tpu_custom_call" | custom-call | flops 1000 | bytes 1000 | tf_op jit(solution)/shard_map/pallas_call | solution.py:43
  68.1 3.3 %collective-permute-start.13 = (bf16[256,1152]{1,0:T(8,128)(2,1)S(1)}, bf16[256,1152]{1,0:T(8,128)(2,1)S(1)}, u32[]{:S(2)}, u32[]{:S(2)}) collective-permute-start(bf16[256,1152]{1,0:T(8,128)(2,1)S(1)} %get-tuple-element.52), channel_id=1, source_target_pairs={{4,0},{5,1},{126,2},{127,3},{8,4},{9,5},{2,6},{3,7},{12,8},{13,9},... | collective-permute-start | bytes 1769480 | tf_op jit(solution)/shard_map/ppermute | solution.py:186
  71.4 1.3 %shard_map.69 = (bf16[256,512]{1,0:T(8,128)(2,1)S(1)}, f32[1,512]{1,0:T(1,128)S(1)}, f32[256,1152]{1,0:T(8,128)S(1)}) custom-call(s32[1]{0:T(128)} %constant.28.clone.1.refs_0_, f32[1]{0:T(128)S(6)} %copy.8.refs_1_, f32[1]{0:T(128)S(6)} %copy.9.refs_2_, bf16[256,1152]{1,0:T(8,128)(2,1)S(1)} %pad_maximum_fusion.1.refs_3_.refs_5_, ...), custom_call_target="tpu_custom_call" | custom-call | flops 1000 | bytes 1000 | tf_op jit(solution)/shard_map/pallas_call | solution.py:43
  72.7 0.0 copy-start.5
  72.7 1.3 %shard_map.72 = (bf16[256,512]{1,0:T(8,128)(2,1)S(1)}, f32[1,512]{1,0:T(1,128)S(1)}, f32[256,1152]{1,0:T(8,128)S(1)}) custom-call(s32[1]{0:T(128)} %constant.28.clone.1.refs_0_, f32[1]{0:T(128)S(6)} %copy.8.refs_1_, f32[1]{0:T(128)S(6)} %copy.9.refs_2_, bf16[256,1152]{1,0:T(8,128)(2,1)S(1)} %constant_dynamic-update-slice_fusion.refs_3_.refs_8_, ...), custom_call_target="tpu_custom_call" | custom-call | flops 1000 | bytes 1000 | tf_op jit(solution)/shard_map/pallas_call | solution.py:43
  74.0 0.0 copy-done.5
  74.0 2.1 %shard_map.75 = bf16[272,1152]{1,0:T(8,128)(2,1)S(1)} custom-call(bf16[256,512]{1,0:T(8,128)(2,1)S(1)} %get-tuple-element.29.refs_0_, bf16[256,512]{1,0:T(8,128)(2,1)S(1)} %get-tuple-element.30.refs_1_, bf16[256,512]{1,0:T(8,128)(2,1)S(1)} %copy-done.5, bf16[256,512]{1,0:T(8,128)(2,1)S(1)} %get-tuple-element.32.refs_3_, ...), custom_call_target="tpu_custom_call" | custom-call | flops 1000 | bytes 1000 | tf_op jit(solution)/shard_map/pallas_call | solution.py:43
  76.2 1.9 %collective-permute-start.8 = (bf16[272,1152]{1,0:T(8,128)(2,1)S(1)}, bf16[272,1152]{1,0:T(8,128)(2,1)S(1)}, u32[]{:S(2)}, u32[]{:S(2)}) collective-permute-start(bf16[272,1152]{1,0:T(8,128)(2,1)S(1)} %shard_map.75), channel_id=1, source_target_pairs={{0,1},{1,0},{2,3},{3,2},{4,5},{5,4},{6,7},{7,6},{8,9},{9,8},{10,11... | collective-permute-start | bytes 1880072 | tf_op jit(solution)/shard_map/ppermute | solution.py:183
  78.1 2.1 %shard_map.74 = (f32[256,1152]{1,0:T(8,128)S(1)}, f32[1,256]{1,0:T(1,128)S(1)}) custom-call(bf16[256,512]{1,0:T(8,128)(2,1)S(1)} %get-tuple-element.29.refs_0_, bf16[256,512]{1,0:T(8,128)(2,1)S(1)} %get-tuple-element.30.refs_1_, bf16[256,512]{1,0:T(8,128)(2,1)S(1)} %copy-done.5, bf16[256,512]{1,0:T(8,128)(2,1)S(1)} %get-tuple-element.32.refs_3_, ...), custom_call_target="tpu_custom_call" | custom-call | flops 1000 | bytes 1000 | tf_op jit(solution)/shard_map/pallas_call | solution.py:43
  80.2 0.0 collective-permute-done.10
  80.2 1.2 convert_add_fusion.1
  81.4 0.0 collective-permute-done.11
  81.4 0.1 convert_add_fusion
  81.5 0.1 fusion
  81.6 0.1 pad_maximum_fusion
  81.7 4.7 %collective-permute-start.12 = (bf16[128,1152]{1,0:T(8,128)(2,1)S(1)}, bf16[128,1152]{1,0:T(8,128)(2,1)S(1)}, u32[]{:S(2)}, u32[]{:S(2)}) collective-permute-start(bf16[128,1152]{1,0:T(8,128)(2,1)S(1)} %slice.52), channel_id=1, source_target_pairs={{256,0},{257,1},{258,2},{259,3},{260,4},{261,5},{262,6},{263,7},{2... | collective-permute-start | bytes 884744 | tf_op jit(solution)/shard_map/ppermute | solution.py:186
  86.4 0.0 collective-permute-done.13
  86.4 0.1 add_convert_fusion
  86.6 0.0 copy-done.6
  86.6 0.0 slice-start
  86.7 10.5 %collective-permute-start.14 = (bf16[128,1152]{1,0:T(8,128)(2,1)S(1)}, bf16[128,1152]{1,0:T(8,128)(2,1)S(1)}, u32[]{:S(2)}, u32[]{:S(2)}) collective-permute-start(bf16[128,1152]{1,0:T(8,128)(2,1)S(1)} %get-tuple-element.53), channel_id=1, source_target_pairs={{2,0},{3,1},{256,2},{257,3},{6,4},{7,5},{260,6},{261,7},{10,8},{11... | collective-permute-start | bytes 884744 | tf_op jit(solution)/shard_map/ppermute | solution.py:186
  97.1 1.9 %collective-permute-start.15 = (bf16[128,1152]{1,0:T(8,128)(2,1)S(1)}, bf16[128,1152]{1,0:T(8,128)(2,1)S(1)}, u32[]{:S(2)}, u32[]{:S(2)}) collective-permute-start(bf16[128,1152]{1,0:T(8,128)(2,1)S(1)} %get-tuple-element.54), channel_id=1, source_target_pairs={{258,0},{259,1},{0,2},{1,3},{262,4},{263,5},{4,6},{5,7},{266,8},{2... | collective-permute-start | bytes 884744 | tf_op jit(solution)/shard_map/ppermute | solution.py:186
  99.1 0.2 collective-permute-done.8.refs_2_
  99.3 0.1 shard_map.76
  99.5 1.9 %collective-permute-start.9 = (bf16[144,1152]{1,0:T(8,128)(2,1)S(1)}, bf16[144,1152]{1,0:T(8,128)(2,1)S(1)}, u32[]{:S(2)}, u32[]{:S(2)}) collective-permute-start(bf16[144,1152]{1,0:T(8,128)(2,1)S(1)} %get-tuple-element.43), channel_id=1, source_target_pairs={{0,128},{1,129},{2,130},{3,131},{4,132},{5,133},{6,134},{7,135},{8... | collective-permute-start | bytes 995336 | tf_op jit(solution)/shard_map/ppermute | solution.py:183
  101.4 10.3 %collective-permute-done.12 = bf16[128,1152]{1,0:T(8,128)(2,1)S(1)} collective-permute-done((bf16[128,1152]{1,0:T(8,128)(2,1)S(1)}, bf16[128,1152]{1,0:T(8,128)(2,1)S(1)}, u32[]{:S(2)}, u32[]{:S(2)}) %collective-permute-start.12) | collective-permute-done | bytes 294944 | tf_op jit(solution)/shard_map/ppermute | solution.py:186
  111.7 0.1 convert_add_fusion.3
  111.8 0.0 copy-start.1
  111.8 0.2 collective-permute-done.14
  112.0 8.2 %collective-permute-done.15 = bf16[128,1152]{1,0:T(8,128)(2,1)S(1)} collective-permute-done((bf16[128,1152]{1,0:T(8,128)(2,1)S(1)}, bf16[128,1152]{1,0:T(8,128)(2,1)S(1)}, u32[]{:S(2)}, u32[]{:S(2)}) %collective-permute-start.15) | collective-permute-done | bytes 294944 | tf_op jit(solution)/shard_map/ppermute | solution.py:186
  120.2 0.1 convert_add_fusion.2.refs_1_
  120.3 0.0 copy-done.1
  120.3 0.0 copy-start.3
  120.3 1.1 shard_map.78
  121.4 0.0 collective-permute-done.9.refs_3_
  121.4 1.1 shard_map.77
  (10 shorter events, 0.3 us)
Async XLA Ops:
  0.6 5.6 %copy-start = (f32[128,1152]{1,0:T(8,128)S(1)}, f32[128,1152]{1,0:T(8,128)}, u32[]{:S(2)}) copy-start(f32[128,1152]{1,0:T(8,128)} %refs_0_.7) | copy-start | bytes 1769476
  0.6 1.1 copy-start.2
  1.9 23.8 %collective-permute-start.1 = (bf16[128,1152]{1,0:T(8,128)(2,1)S(1)}, bf16[128,1152]{1,0:T(8,128)(2,1)S(1)}, u32[]{:S(2)}, u32[]{:S(2)}) collective-permute-start(bf16[128,1152]{1,0:T(8,128)(2,1)S(1)} %shard_map.68.refs_4_), channel_id=1, source_target_pairs={{0,1},{1,0},{2,3},{3,2},{4,5},{5,4},{6,7},{7,6},{8,9},{9,8},{10,11... | collective-permute-start | bytes 884744 | tf_op jit(solution)/shard_map/ppermute | solution.py:183
  6.4 31.4 %collective-permute-start = (bf16[128,1152]{1,0:T(8,128)(2,1)S(1)}, bf16[128,1152]{1,0:T(8,128)(2,1)S(1)}, u32[]{:S(2)}, u32[]{:S(2)}) collective-permute-start(bf16[128,1152]{1,0:T(8,128)(2,1)S(1)} %shard_map.67), channel_id=1, source_target_pairs={{0,256},{1,257},{2,258},{3,259},{4,260},{5,261},{6,262},{7,263},{8... | collective-permute-start | bytes 884744 | tf_op jit(solution)/shard_map/ppermute | solution.py:183
  16.4 30.0 %collective-permute-start.5 = (bf16[128,1152]{1,0:T(8,128)(2,1)S(1)}, bf16[128,1152]{1,0:T(8,128)(2,1)}, u32[]{:S(2)}, u32[]{:S(2)}) collective-permute-start(bf16[128,1152]{1,0:T(8,128)(2,1)S(1)} %shard_map.67), channel_id=1, source_target_pairs={{0,2},{1,3},{2,256},{3,257},{4,6},{5,7},{6,260},{7,261},{8,10},{9,... | collective-permute-start | bytes 884744 | tf_op jit(solution)/shard_map/ppermute | solution.py:183
  20.7 26.7 %collective-permute-start.6 = (bf16[128,1152]{1,0:T(8,128)(2,1)S(1)}, bf16[128,1152]{1,0:T(8,128)(2,1)S(1)}, u32[]{:S(2)}, u32[]{:S(2)}) collective-permute-start(bf16[128,1152]{1,0:T(8,128)(2,1)S(1)} %shard_map.67), channel_id=1, source_target_pairs={{0,258},{1,259},{2,0},{3,1},{4,262},{5,263},{6,4},{7,5},{8,266},{9... | collective-permute-start | bytes 884744 | tf_op jit(solution)/shard_map/ppermute | solution.py:183
  25.8 24.3 %collective-permute-start.2 = (bf16[256,1152]{1,0:T(8,128)(2,1)S(1)}, bf16[256,1152]{1,0:T(8,128)(2,1)S(1)}, u32[]{:S(2)}, u32[]{:S(2)}) collective-permute-start(bf16[256,1152]{1,0:T(8,128)(2,1)S(1)} %pad_maximum_fusion.2), channel_id=1, source_target_pairs={{0,128},{1,129},{2,130},{3,131},{4,132},{5,133},{6,134},{7,135},{8... | collective-permute-start | bytes 1769480 | tf_op jit(solution)/shard_map/ppermute | solution.py:183
  37.9 12.3 %collective-permute-start.4 = (bf16[256,1152]{1,0:T(8,128)(2,1)S(1)}, bf16[256,1152]{1,0:T(8,128)(2,1)S(1)}, u32[]{:S(2)}, u32[]{:S(2)}) collective-permute-start(bf16[256,1152]{1,0:T(8,128)(2,1)S(1)} %pad_maximum_fusion.1.refs_3_.refs_5_), channel_id=1, source_target_pairs={{0,4},{1,5},{2,126},{3,127},{4,8},{5,9},{6,2},{7,3},{8,12},{9,13},... | collective-permute-start | bytes 1769480 | tf_op jit(solution)/shard_map/ppermute | solution.py:183
  40.5 15.8 %collective-permute-start.3 = (bf16[256,1152]{1,0:T(8,128)(2,1)S(1)}, bf16[256,1152]{1,0:T(8,128)(2,1)S(1)}, u32[]{:S(2)}, u32[]{:S(2)}) collective-permute-start(bf16[256,1152]{1,0:T(8,128)(2,1)S(1)} %pad_maximum_fusion.1.refs_3_.refs_5_), channel_id=1, source_target_pairs={{0,124},{1,125},{2,6},{3,7},{4,0},{5,1},{6,10},{7,11},{8,4},{9,5},... | collective-permute-start | bytes 1769480 | tf_op jit(solution)/shard_map/ppermute | solution.py:183
  47.5 18.3 %collective-permute-start.7 = (bf16[256,1152]{1,0:T(8,128)(2,1)S(1)}, bf16[256,1152]{1,0:T(8,128)(2,1)}, u32[]{:S(2)}, u32[]{:S(2)}) collective-permute-start(bf16[256,1152]{1,0:T(8,128)(2,1)S(1)} %constant_dynamic-update-slice_fusion.refs_3_.refs_8_), channel_id=1, source_target_pairs={{0,4},{1,5},{2,126},{3,127},{4,8},{5,9},{6,2},{7,3},{8,12},{9,13},... | collective-permute-start | bytes 1769480 | tf_op jit(solution)/shard_map/ppermute | solution.py:183
  52.3 0.7 copy-start.4
  53.0 27.3 %collective-permute-start.10 = (bf16[256,1152]{1,0:T(8,128)(2,1)}, bf16[256,1152]{1,0:T(8,128)(2,1)}, u32[]{:S(2)}, u32[]{:S(2)}) collective-permute-start(bf16[256,1152]{1,0:T(8,128)(2,1)} %get-tuple-element.47), channel_id=1, source_target_pairs={{4,0},{5,1},{126,2},{127,3},{8,4},{9,5},{2,6},{3,7},{12,8},{13,9},... | collective-permute-start | bytes 1769480 | tf_op jit(solution)/shard_map/ppermute | solution.py:186
  57.6 23.8 %collective-permute-start.11 = (bf16[256,1152]{1,0:T(8,128)(2,1)S(1)}, bf16[256,1152]{1,0:T(8,128)(2,1)S(1)}, u32[]{:S(2)}, u32[]{:S(2)}) collective-permute-start(bf16[256,1152]{1,0:T(8,128)(2,1)S(1)} %get-tuple-element.48), channel_id=1, source_target_pairs={{124,0},{125,1},{6,2},{7,3},{0,4},{1,5},{10,6},{11,7},{4,8},{5,9},... | collective-permute-start | bytes 1769480 | tf_op jit(solution)/shard_map/ppermute | solution.py:186
  68.1 18.3 %collective-permute-start.13 = (bf16[256,1152]{1,0:T(8,128)(2,1)S(1)}, bf16[256,1152]{1,0:T(8,128)(2,1)S(1)}, u32[]{:S(2)}, u32[]{:S(2)}) collective-permute-start(bf16[256,1152]{1,0:T(8,128)(2,1)S(1)} %get-tuple-element.52), channel_id=1, source_target_pairs={{4,0},{5,1},{126,2},{127,3},{8,4},{9,5},{2,6},{3,7},{12,8},{13,9},... | collective-permute-start | bytes 1769480 | tf_op jit(solution)/shard_map/ppermute | solution.py:186
  72.7 1.3 %copy-start.5 = (bf16[256,512]{1,0:T(8,128)(2,1)S(1)}, bf16[256,512]{1,0:T(8,128)(2,1)}, u32[]{:S(2)}) copy-start(bf16[256,512]{1,0:T(8,128)(2,1)} %copy-done.4) | copy-start | bytes 786436
  76.2 23.2 %collective-permute-start.8 = (bf16[272,1152]{1,0:T(8,128)(2,1)S(1)}, bf16[272,1152]{1,0:T(8,128)(2,1)S(1)}, u32[]{:S(2)}, u32[]{:S(2)}) collective-permute-start(bf16[272,1152]{1,0:T(8,128)(2,1)S(1)} %shard_map.75), channel_id=1, source_target_pairs={{0,1},{1,0},{2,3},{3,2},{4,5},{5,4},{6,7},{7,6},{8,9},{9,8},{10,11... | collective-permute-start | bytes 1880072 | tf_op jit(solution)/shard_map/ppermute | solution.py:183
  81.7 4.9 %copy-start.6 = (f32[256,1152]{1,0:T(8,128)}, f32[256,1152]{1,0:T(8,128)S(1)}, u32[]{:S(2)}) copy-start(f32[256,1152]{1,0:T(8,128)S(1)} %pad_maximum_fusion) | copy-start | bytes 3538948
  81.7 30.0 %collective-permute-start.12 = (bf16[128,1152]{1,0:T(8,128)(2,1)S(1)}, bf16[128,1152]{1,0:T(8,128)(2,1)S(1)}, u32[]{:S(2)}, u32[]{:S(2)}) collective-permute-start(bf16[128,1152]{1,0:T(8,128)(2,1)S(1)} %slice.52), channel_id=1, source_target_pairs={{256,0},{257,1},{258,2},{259,3},{260,4},{261,5},{262,6},{263,7},{2... | collective-permute-start | bytes 884744 | tf_op jit(solution)/shard_map/ppermute | solution.py:186
  86.6 25.1 %slice-start = ((f32[256,1152]{1,0:T(8,128)}), f32[128,1152]{1,0:T(8,128)S(1)}, s32[]{:S(2)}) async-start(f32[256,1152]{1,0:T(8,128)} %copy-done.6), calls=%async_computation | async-start | bytes 1179648 | tf_op jit(solution)/shard_map/slice | solution.py:232
  86.7 25.3 %collective-permute-start.14 = (bf16[128,1152]{1,0:T(8,128)(2,1)S(1)}, bf16[128,1152]{1,0:T(8,128)(2,1)S(1)}, u32[]{:S(2)}, u32[]{:S(2)}) collective-permute-start(bf16[128,1152]{1,0:T(8,128)(2,1)S(1)} %get-tuple-element.53), channel_id=1, source_target_pairs={{2,0},{3,1},{256,2},{257,3},{6,4},{7,5},{260,6},{261,7},{10,8},{11... | collective-permute-start | bytes 884744 | tf_op jit(solution)/shard_map/ppermute | solution.py:186
  97.1 23.0 %collective-permute-start.15 = (bf16[128,1152]{1,0:T(8,128)(2,1)S(1)}, bf16[128,1152]{1,0:T(8,128)(2,1)S(1)}, u32[]{:S(2)}, u32[]{:S(2)}) collective-permute-start(bf16[128,1152]{1,0:T(8,128)(2,1)S(1)} %get-tuple-element.54), channel_id=1, source_target_pairs={{258,0},{259,1},{0,2},{1,3},{262,4},{263,5},{4,6},{5,7},{266,8},{2... | collective-permute-start | bytes 884744 | tf_op jit(solution)/shard_map/ppermute | solution.py:186
  99.5 21.9 %collective-permute-start.9 = (bf16[144,1152]{1,0:T(8,128)(2,1)S(1)}, bf16[144,1152]{1,0:T(8,128)(2,1)S(1)}, u32[]{:S(2)}, u32[]{:S(2)}) collective-permute-start(bf16[144,1152]{1,0:T(8,128)(2,1)S(1)} %get-tuple-element.43), channel_id=1, source_target_pairs={{0,128},{1,129},{2,130},{3,131},{4,132},{5,133},{6,134},{7,135},{8... | collective-permute-start | bytes 995336 | tf_op jit(solution)/shard_map/ppermute | solution.py:183
  111.8 8.5 %copy-start.1 = (f32[128,1152]{1,0:T(8,128)S(1)}, f32[128,1152]{1,0:T(8,128)}, u32[]{:S(2)}) copy-start(f32[128,1152]{1,0:T(8,128)} %refs_0_.7) | copy-start | bytes 1769476
  120.3 1.1 copy-start.3

commit v5 on v4

--- a/solution.py
+++ b/solution.py
@@ -155,17 +155,13 @@
     return (grad - along * unit) / size
 
 
-def image_end_kernel(rows, raw_ref, grad_ref, loss_ref, got_ref, grad_out, loss_out):
+def end_kernel(
+    rows, images_ref, grad_ref, loss_ref, got_ref, texts_ref, total_ref, img_out, loss_out, txt_out
+):
     loss_out[...] = loss_ref[...] + unpack_loss(got_ref, rows)
     grad = grad_ref[...] + got_ref[:rows, :].astype(jnp.float32)
-    grad_out[...] = project(raw_ref[...], grad)
-
-
-def text_end_kernel(raw_ref, *refs):
-    grad = refs[0][...].astype(jnp.float32)
-    for other in refs[1:-1]:
-        grad = grad + other[...].astype(jnp.float32)
-    refs[-1][...] = project(raw_ref[...], grad)
+    img_out[...] = project(images_ref[...], grad)
+    txt_out[...] = project(texts_ref[...], total_ref[...])
 
 
 def sum_kernel(*refs):
@@ -253,15 +249,12 @@
             (shape(rows + TAIL, width, bf16), shape(rows, width, f32), shape(1, rows, f32)),
             img_part, loss, send(packed, "pair"),
         )
-        grad_images, row_loss = call(
-            functools.partial(image_end_kernel, rows),
-            (shape(rows, width, f32), shape(1, rows, f32)),
-            picture_vectors, img_part, loss, send(packed, "core"),
-        )
         total = ordered(home + back_across.astype(f32))
         total = ordered(total + back_up.astype(f32) + back_down.astype(f32))
-        grad_texts = call(
-            text_end_kernel, shape(rows, width, f32), caption_vectors, total
+        grad_images, row_loss, grad_texts = call(
+            functools.partial(end_kernel, rows),
+            (shape(rows, width, f32), shape(1, rows, f32), shape(rows, width, f32)),
+            picture_vectors, img_part, loss, send(packed, "core"), caption_vectors, total,
         )
         return (row_loss.reshape(rows), grad_images, grad_texts)
 

time: 123 us -> 123 us (level)
    pallas_call x12 -> x11, Pallas kernels: 15.3 us -> 14.5 us  [call(): pl.pallas_call(lambda *refs: kernel(*refs[len(after):]), out_shape=outs,...]
where the time goes in v5:
time: 123 us; the launch traced here: 122 us
  starting transfers between devices  62.7 us (51%)
  waiting for transfers between devices  37.4 us (30%)
  Pallas kernels  14.5 us (12%)
  local copies, waits for them, and re-layouts  3.02 us (2%)
  between operations  2.39 us (2%)
  other arithmetic  1.72 us (1%)
    ppermute x10, starting transfers between devices, send(): return lax.ppermute(x, AXES, pairs[name])  36.6 us
    ppermute x6, starting transfers between devices, send_back(): return lax.ppermute(x, AXES, [(b, a) for a, b in pairs[name]])  26.2 us
    ppermute x6, waiting for transfers between devices, send_back(): return lax.ppermute(x, AXES, [(b, a) for a, b in pairs[name]])  18.7 us
    ppermute x10, waiting for transfers between devices, send(): return lax.ppermute(x, AXES, pairs[name])  18.7 us
    pallas_call x11, Pallas kernels, call(): pl.pallas_call(lambda *refs: kernel(*refs[len(after):]), out_shape=outs,...  14.5 us
    unnamed x15, local copies, waits for them, and re-layouts  2.77 us
  transfers between devices with their start and end apart: 16, of which 7 were waited for; matrix products, arithmetic and copies ran while one was open for 2% of the time, Pallas kernels for 11%

profile of v5, /device:TPU:54, one launch (start us, length us, event | category | flops | bytes accessed | tf_op | source)
XLA Modules:
  0.0 121.7 jit_solution(13683975117729973885)
XLA Ops:
  0.6 0.0 copy-start
  0.6 1.1 copy-done
  1.7 0.2 shard_map.68.refs_4_
  1.9 4.4 %collective-permute-start.1 = (bf16[128,1152]{1,0:T(8,128)(2,1)S(1)}, bf16[128,1152]{1,0:T(8,128)(2,1)S(1)}, u32[]{:S(2)}, u32[]{:S(2)}) collective-permute-start(bf16[128,1152]{1,0:T(8,128)(2,1)S(1)} %shard_map.68.refs_4_), channel_id=1, source_target_pairs={{0,1},{1,0},{2,3},{3,2},{4,5},{5,4},{6,7},{7,6},{8,9},{9,8},{10,11... | collective-permute-start | bytes 884744 | tf_op jit(solution)/shard_map/ppermute | solution.py:179
  6.3 0.0 copy-done.2
  6.3 0.2 shard_map.67
  6.4 10.0 %collective-permute-start = (bf16[128,1152]{1,0:T(8,128)(2,1)S(1)}, bf16[128,1152]{1,0:T(8,128)(2,1)S(1)}, u32[]{:S(2)}, u32[]{:S(2)}) collective-permute-start(bf16[128,1152]{1,0:T(8,128)(2,1)S(1)} %shard_map.67), channel_id=1, source_target_pairs={{0,256},{1,257},{2,258},{3,259},{4,260},{5,261},{6,262},{7,263},{8... | collective-permute-start | bytes 884744 | tf_op jit(solution)/shard_map/ppermute | solution.py:179
  16.5 4.3 %collective-permute-start.5 = (bf16[128,1152]{1,0:T(8,128)(2,1)S(1)}, bf16[128,1152]{1,0:T(8,128)(2,1)}, u32[]{:S(2)}, u32[]{:S(2)}) collective-permute-start(bf16[128,1152]{1,0:T(8,128)(2,1)S(1)} %shard_map.67), channel_id=1, source_target_pairs={{0,2},{1,3},{2,256},{3,257},{4,6},{5,7},{6,260},{7,261},{8,10},{9,... | collective-permute-start | bytes 884744 | tf_op jit(solution)/shard_map/ppermute | solution.py:179
  20.8 3.7 %collective-permute-start.6 = (bf16[128,1152]{1,0:T(8,128)(2,1)S(1)}, bf16[128,1152]{1,0:T(8,128)(2,1)S(1)}, u32[]{:S(2)}, u32[]{:S(2)}) collective-permute-start(bf16[128,1152]{1,0:T(8,128)(2,1)S(1)} %shard_map.67), channel_id=1, source_target_pairs={{0,258},{1,259},{2,0},{3,1},{4,262},{5,263},{6,4},{7,5},{8,266},{9... | collective-permute-start | bytes 884744 | tf_op jit(solution)/shard_map/ppermute | solution.py:179
  25.8 0.0 collective-permute-done.1.refs_6_
  25.8 1.9 %collective-permute-start.2 = (bf16[256,1152]{1,0:T(8,128)(2,1)S(1)}, bf16[256,1152]{1,0:T(8,128)(2,1)S(1)}, u32[]{:S(2)}, u32[]{:S(2)}) collective-permute-start(bf16[256,1152]{1,0:T(8,128)(2,1)S(1)} %pad_maximum_fusion.2), channel_id=1, source_target_pairs={{0,128},{1,129},{2,130},{3,131},{4,132},{5,133},{6,134},{7,135},{8... | collective-permute-start | bytes 1769480 | tf_op jit(solution)/shard_map/ppermute | solution.py:179
  27.8 10.1 %collective-permute-done = bf16[128,1152]{1,0:T(8,128)(2,1)S(1)} collective-permute-done((bf16[128,1152]{1,0:T(8,128)(2,1)S(1)}, bf16[128,1152]{1,0:T(8,128)(2,1)S(1)}, u32[]{:S(2)}, u32[]{:S(2)}) %collective-permute-start) | collective-permute-done | bytes 294944 | tf_op jit(solution)/shard_map/ppermute | solution.py:179
  37.9 2.6 %collective-permute-start.4 = (bf16[256,1152]{1,0:T(8,128)(2,1)S(1)}, bf16[256,1152]{1,0:T(8,128)(2,1)S(1)}, u32[]{:S(2)}, u32[]{:S(2)}) collective-permute-start(bf16[256,1152]{1,0:T(8,128)(2,1)S(1)} %pad_maximum_fusion.1.refs_3_.refs_5_), channel_id=1, source_target_pairs={{0,4},{1,5},{2,126},{3,127},{4,8},{5,9},{6,2},{7,3},{8,12},{9,13},... | collective-permute-start | bytes 1769480 | tf_op jit(solution)/shard_map/ppermute | solution.py:179
  40.5 3.3 %collective-permute-start.3 = (bf16[256,1152]{1,0:T(8,128)(2,1)S(1)}, bf16[256,1152]{1,0:T(8,128)(2,1)S(1)}, u32[]{:S(2)}, u32[]{:S(2)}) collective-permute-start(bf16[256,1152]{1,0:T(8,128)(2,1)S(1)} %pad_maximum_fusion.1.refs_3_.refs_5_), channel_id=1, source_target_pairs={{0,124},{1,125},{2,6},{3,7},{4,0},{5,1},{6,10},{7,11},{8,4},{9,5},... | collective-permute-start | bytes 1769480 | tf_op jit(solution)/shard_map/ppermute | solution.py:179
  43.8 2.7 %collective-permute-done.5 = bf16[128,1152]{1,0:T(8,128)(2,1)} collective-permute-done((bf16[128,1152]{1,0:T(8,128)(2,1)S(1)}, bf16[128,1152]{1,0:T(8,128)(2,1)}, u32[]{:S(2)}, u32[]{:S(2)}) %collective-permute-start.5) | collective-permute-done | bytes 294944 | tf_op jit(solution)/shard_map/ppermute | solution.py:179
  46.5 1.0 constant_dynamic-update-slice_fusion.1
  47.5 0.0 collective-permute-done.6
  47.5 2.6 %collective-permute-start.7 = (bf16[256,1152]{1,0:T(8,128)(2,1)S(1)}, bf16[256,1152]{1,0:T(8,128)(2,1)}, u32[]{:S(2)}, u32[]{:S(2)}) collective-permute-start(bf16[256,1152]{1,0:T(8,128)(2,1)S(1)} %constant_dynamic-update-slice_fusion.refs_3_.refs_8_), channel_id=1, source_target_pairs={{0,4},{1,5},{2,126},{3,127},{4,8},{5,9},{6,2},{7,3},{8,12},{9,13},... | collective-permute-start | bytes 1769480 | tf_op jit(solution)/shard_map/ppermute | solution.py:179
  50.1 0.0 collective-permute-done.2
  50.2 0.0 collective-permute-done.4.refs_3_.refs_7_
  50.2 2.1 %shard_map.71 = (bf16[256,512]{1,0:T(8,128)(2,1)S(1)}, f32[1,512]{1,0:T(1,128)S(1)}, bf16[256,1152]{1,0:T(8,128)(2,1)}) custom-call(s32[1]{0:T(128)} %bitcast.1.refs_0_, f32[1]{0:T(128)S(6)} %copy.8.refs_1_, f32[1]{0:T(128)S(6)} %copy.9.refs_2_, bf16[256,1152]{1,0:T(8,128)(2,1)S(1)} %collective-permute-done.4.refs_3_.refs_7_, ...), custom_call_target="tpu_custom_call" | custom-call | flops 1000 | bytes 1000 | tf_op jit(solution)/shard_map/pallas_call | solution.py:43
  52.3 0.7 copy-done.4
  53.0 3.2 %collective-permute-start.10 = (bf16[256,1152]{1,0:T(8,128)(2,1)}, bf16[256,1152]{1,0:T(8,128)(2,1)}, u32[]{:S(2)}, u32[]{:S(2)}) collective-permute-start(bf16[256,1152]{1,0:T(8,128)(2,1)} %get-tuple-element.46), channel_id=1, source_target_pairs={{4,0},{5,1},{126,2},{127,3},{8,4},{9,5},{2,6},{3,7},{12,8},{13,9},... | collective-permute-start | bytes 1769480 | tf_op jit(solution)/shard_map/ppermute | solution.py:182
  56.3 0.0 collective-permute-done.3.refs_3_.refs_6_
  56.3 1.3 %shard_map.70 = (bf16[256,512]{1,0:T(8,128)(2,1)S(1)}, f32[1,512]{1,0:T(1,128)S(1)}, bf16[256,1152]{1,0:T(8,128)(2,1)S(1)}) custom-call(s32[1]{0:T(128)} %bitcast.refs_0_, f32[1]{0:T(128)S(6)} %copy.8.refs_1_, f32[1]{0:T(128)S(6)} %copy.9.refs_2_, bf16[256,1152]{1,0:T(8,128)(2,1)S(1)} %collective-permute-done.3.refs_3_.refs_6_, ...), custom_call_target="tpu_custom_call" | custom-call | flops 1000 | bytes 1000 | tf_op jit(solution)/shard_map/pallas_call | solution.py:43
  57.6 2.6 %collective-permute-start.11 = (bf16[256,1152]{1,0:T(8,128)(2,1)S(1)}, bf16[256,1152]{1,0:T(8,128)(2,1)S(1)}, u32[]{:S(2)}, u32[]{:S(2)}) collective-permute-start(bf16[256,1152]{1,0:T(8,128)(2,1)S(1)} %get-tuple-element.47), channel_id=1, source_target_pairs={{124,0},{125,1},{6,2},{7,3},{0,4},{1,5},{10,6},{11,7},{4,8},{5,9},... | collective-permute-start | bytes 1769480 | tf_op jit(solution)/shard_map/ppermute | solution.py:182
  60.2 5.6 %collective-permute-done.7.refs_3_.refs_9_ = bf16[256,1152]{1,0:T(8,128)(2,1)} collective-permute-done((bf16[256,1152]{1,0:T(8,128)(2,1)S(1)}, bf16[256,1152]{1,0:T(8,128)(2,1)}, u32[]{:S(2)}, u32[]{:S(2)}) %collective-permute-start.7) | collective-permute-done | bytes 589856 | tf_op jit(solution)/shard_map/ppermute | solution.py:179
  65.8 2.4 %shard_map.73 = (bf16[256,512]{1,0:T(8,128)(2,1)S(1)}, f32[1,512]{1,0:T(1,128)S(1)}, bf16[256,1152]{1,0:T(8,128)(2,1)S(1)}) custom-call(s32[1]{0:T(128)} %constant.28.clone.1.refs_0_, f32[1]{0:T(128)S(6)} %copy.8.refs_1_, f32[1]{0:T(128)S(6)} %copy.9.refs_2_, bf16[256,1152]{1,0:T(8,128)(2,1)} %collective-permute-done.7.refs_3_.refs_9_, ...), custom_call_target="tpu_custom_call" | custom-call | flops 1000 | bytes 1000 | tf_op jit(solution)/shard_map/pallas_call | solution.py:43
  68.2 3.3 %collective-permute-start.13 = (bf16[256,1152]{1,0:T(8,128)(2,1)S(1)}, bf16[256,1152]{1,0:T(8,128)(2,1)S(1)}, u32[]{:S(2)}, u32[]{:S(2)}) collective-permute-start(bf16[256,1152]{1,0:T(8,128)(2,1)S(1)} %get-tuple-element.51), channel_id=1, source_target_pairs={{4,0},{5,1},{126,2},{127,3},{8,4},{9,5},{2,6},{3,7},{12,8},{13,9},... | collective-permute-start | bytes 1769480 | tf_op jit(solution)/shard_map/ppermute | solution.py:182
  71.4 1.3 %shard_map.69 = (bf16[256,512]{1,0:T(8,128)(2,1)S(1)}, f32[1,512]{1,0:T(1,128)S(1)}, f32[256,1152]{1,0:T(8,128)S(1)}) custom-call(s32[1]{0:T(128)} %constant.28.clone.1.refs_0_, f32[1]{0:T(128)S(6)} %copy.8.refs_1_, f32[1]{0:T(128)S(6)} %copy.9.refs_2_, bf16[256,1152]{1,0:T(8,128)(2,1)S(1)} %pad_maximum_fusion.1.refs_3_.refs_5_, ...), custom_call_target="tpu_custom_call" | custom-call | flops 1000 | bytes 1000 | tf_op jit(solution)/shard_map/pallas_call | solution.py:43
  72.7 0.0 copy-start.5
  72.8 1.3 %shard_map.72 = (bf16[256,512]{1,0:T(8,128)(2,1)S(1)}, f32[1,512]{1,0:T(1,128)S(1)}, f32[256,1152]{1,0:T(8,128)S(1)}) custom-call(s32[1]{0:T(128)} %constant.28.clone.1.refs_0_, f32[1]{0:T(128)S(6)} %copy.8.refs_1_, f32[1]{0:T(128)S(6)} %copy.9.refs_2_, bf16[256,1152]{1,0:T(8,128)(2,1)S(1)} %constant_dynamic-update-slice_fusion.refs_3_.refs_8_, ...), custom_call_target="tpu_custom_call" | custom-call | flops 1000 | bytes 1000 | tf_op jit(solution)/shard_map/pallas_call | solution.py:43
  74.1 0.0 copy-done.5
  74.1 2.1 %shard_map.75 = bf16[272,1152]{1,0:T(8,128)(2,1)S(1)} custom-call(bf16[256,512]{1,0:T(8,128)(2,1)S(1)} %get-tuple-element.30.refs_0_, bf16[256,512]{1,0:T(8,128)(2,1)S(1)} %get-tuple-element.31.refs_1_, bf16[256,512]{1,0:T(8,128)(2,1)S(1)} %copy-done.5, bf16[256,512]{1,0:T(8,128)(2,1)S(1)} %get-tuple-element.33.refs_3_, ...), custom_call_target="tpu_custom_call" | custom-call | flops 1000 | bytes 1000 | tf_op jit(solution)/shard_map/pallas_call | solution.py:43
  76.2 1.9 %collective-permute-start.8 = (bf16[272,1152]{1,0:T(8,128)(2,1)S(1)}, bf16[272,1152]{1,0:T(8,128)(2,1)S(1)}, u32[]{:S(2)}, u32[]{:S(2)}) collective-permute-start(bf16[272,1152]{1,0:T(8,128)(2,1)S(1)} %shard_map.75), channel_id=1, source_target_pairs={{0,1},{1,0},{2,3},{3,2},{4,5},{5,4},{6,7},{7,6},{8,9},{9,8},{10,11... | collective-permute-start | bytes 1880072 | tf_op jit(solution)/shard_map/ppermute | solution.py:179
  78.1 2.1 %shard_map.74 = (f32[256,1152]{1,0:T(8,128)S(1)}, f32[1,256]{1,0:T(1,128)S(1)}) custom-call(bf16[256,512]{1,0:T(8,128)(2,1)S(1)} %get-tuple-element.30.refs_0_, bf16[256,512]{1,0:T(8,128)(2,1)S(1)} %get-tuple-element.31.refs_1_, bf16[256,512]{1,0:T(8,128)(2,1)S(1)} %copy-done.5, bf16[256,512]{1,0:T(8,128)(2,1)S(1)} %get-tuple-element.33.refs_3_, ...), custom_call_target="tpu_custom_call" | custom-call | flops 1000 | bytes 1000 | tf_op jit(solution)/shard_map/pallas_call | solution.py:43
  80.3 0.0 collective-permute-done.10
  80.3 1.2 convert_add_fusion.1
  81.5 0.0 collective-permute-done.11
  81.5 0.1 convert_add_fusion
  81.6 0.1 fusion
  81.7 0.1 pad_maximum_fusion
  81.7 0.0 copy-start.6
  81.8 4.7 %collective-permute-start.12 = (bf16[128,1152]{1,0:T(8,128)(2,1)S(1)}, bf16[128,1152]{1,0:T(8,128)(2,1)S(1)}, u32[]{:S(2)}, u32[]{:S(2)}) collective-permute-start(bf16[128,1152]{1,0:T(8,128)(2,1)S(1)} %slice.52), channel_id=1, source_target_pairs={{256,0},{257,1},{258,2},{259,3},{260,4},{261,5},{262,6},{263,7},{2... | collective-permute-start | bytes 884744 | tf_op jit(solution)/shard_map/ppermute | solution.py:182
  86.5 0.0 collective-permute-done.13
  86.5 0.1 add_convert_fusion
  86.6 0.0 copy-done.6
  86.7 0.0 slice-start
  86.7 10.5 %collective-permute-start.14 = (bf16[128,1152]{1,0:T(8,128)(2,1)S(1)}, bf16[128,1152]{1,0:T(8,128)(2,1)S(1)}, u32[]{:S(2)}, u32[]{:S(2)}) collective-permute-start(bf16[128,1152]{1,0:T(8,128)(2,1)S(1)} %get-tuple-element.52), channel_id=1, source_target_pairs={{2,0},{3,1},{256,2},{257,3},{6,4},{7,5},{260,6},{261,7},{10,8},{11... | collective-permute-start | bytes 884744 | tf_op jit(solution)/shard_map/ppermute | solution.py:182
  97.2 1.9 %collective-permute-start.15 = (bf16[128,1152]{1,0:T(8,128)(2,1)S(1)}, bf16[128,1152]{1,0:T(8,128)(2,1)S(1)}, u32[]{:S(2)}, u32[]{:S(2)}) collective-permute-start(bf16[128,1152]{1,0:T(8,128)(2,1)S(1)} %get-tuple-element.53), channel_id=1, source_target_pairs={{258,0},{259,1},{0,2},{1,3},{262,4},{263,5},{4,6},{5,7},{266,8},{2... | collective-permute-start | bytes 884744 | tf_op jit(solution)/shard_map/ppermute | solution.py:182
  99.1 0.3 collective-permute-done.8.refs_2_
  99.4 0.1 shard_map.76
  99.5 1.9 %collective-permute-start.9 = (bf16[144,1152]{1,0:T(8,128)(2,1)S(1)}, bf16[144,1152]{1,0:T(8,128)(2,1)S(1)}, u32[]{:S(2)}, u32[]{:S(2)}) collective-permute-start(bf16[144,1152]{1,0:T(8,128)(2,1)S(1)} %get-tuple-element.44), channel_id=1, source_target_pairs={{0,128},{1,129},{2,130},{3,131},{4,132},{5,133},{6,134},{7,135},{8... | collective-permute-start | bytes 995336 | tf_op jit(solution)/shard_map/ppermute | solution.py:179
  101.4 10.3 %collective-permute-done.12 = bf16[128,1152]{1,0:T(8,128)(2,1)S(1)} collective-permute-done((bf16[128,1152]{1,0:T(8,128)(2,1)S(1)}, bf16[128,1152]{1,0:T(8,128)(2,1)S(1)}, u32[]{:S(2)}, u32[]{:S(2)}) %collective-permute-start.12) | collective-permute-done | bytes 294944 | tf_op jit(solution)/shard_map/ppermute | solution.py:182
  111.8 0.1 convert_add_fusion.3
  111.8 0.0 copy-start.1
  111.8 0.0 copy-start.3
  111.9 0.2 collective-permute-done.14
  112.0 8.2 %collective-permute-done.15 = bf16[128,1152]{1,0:T(8,128)(2,1)S(1)} collective-permute-done((bf16[128,1152]{1,0:T(8,128)(2,1)S(1)}, bf16[128,1152]{1,0:T(8,128)(2,1)S(1)}, u32[]{:S(2)}, u32[]{:S(2)}) %collective-permute-start.15) | collective-permute-done | bytes 294944 | tf_op jit(solution)/shard_map/ppermute | solution.py:182
  120.2 0.1 convert_add_fusion.2.refs_5_
  120.3 0.0 collective-permute-done.9.refs_3_
  120.3 0.0 copy-done.1
  120.3 0.0 copy-done.3
  120.3 1.4 %shard_map.77 = (f32[128,1152]{1,0:T(8,128)}, f32[1,128]{1,0:T(1,128)}, f32[128,1152]{1,0:T(8,128)}) custom-call(f32[128,1152]{1,0:T(8,128)S(1)} %copy-done.1, f32[128,1152]{1,0:T(8,128)S(1)} %get-tuple-element.42.refs_1_, f32[1,128]{1,0:T(1,128)S(1)} %get-tuple-element.43.refs_2_, bf16[144,1152]{1,0:T(8,128)(2,1)S(1)} %collective-permute-done.9.refs_3_, ...), custom_call_target="tpu_custom_call" | custom-call | flops 1000 | bytes 1000 | tf_op jit(solution)/shard_map/pallas_call | solution.py:43
  (9 shorter events, 0.3 us)
Async XLA Ops:
  0.6 1.1 copy-start
  1.7 4.6 %copy-start.2 = (f32[128,1152]{1,0:T(8,128)S(1)}, f32[128,1152]{1,0:T(8,128)}, u32[]{:S(2)}) copy-start(f32[128,1152]{1,0:T(8,128)} %refs_4_.1) | copy-start | bytes 1769476
  1.9 23.9 %collective-permute-start.1 = (bf16[128,1152]{1,0:T(8,128)(2,1)S(1)}, bf16[128,1152]{1,0:T(8,128)(2,1)S(1)}, u32[]{:S(2)}, u32[]{:S(2)}) collective-permute-start(bf16[128,1152]{1,0:T(8,128)(2,1)S(1)} %shard_map.68.refs_4_), channel_id=1, source_target_pairs={{0,1},{1,0},{2,3},{3,2},{4,5},{5,4},{6,7},{7,6},{8,9},{9,8},{10,11... | collective-permute-start | bytes 884744 | tf_op jit(solution)/shard_map/ppermute | solution.py:179
  6.4 31.4 %collective-permute-start = (bf16[128,1152]{1,0:T(8,128)(2,1)S(1)}, bf16[128,1152]{1,0:T(8,128)(2,1)S(1)}, u32[]{:S(2)}, u32[]{:S(2)}) collective-permute-start(bf16[128,1152]{1,0:T(8,128)(2,1)S(1)} %shard_map.67), channel_id=1, source_target_pairs={{0,256},{1,257},{2,258},{3,259},{4,260},{5,261},{6,262},{7,263},{8... | collective-permute-start | bytes 884744 | tf_op jit(solution)/shard_map/ppermute | solution.py:179
  16.5 30.0 %collective-permute-start.5 = (bf16[128,1152]{1,0:T(8,128)(2,1)S(1)}, bf16[128,1152]{1,0:T(8,128)(2,1)}, u32[]{:S(2)}, u32[]{:S(2)}) collective-permute-start(bf16[128,1152]{1,0:T(8,128)(2,1)S(1)} %shard_map.67), channel_id=1, source_target_pairs={{0,2},{1,3},{2,256},{3,257},{4,6},{5,7},{6,260},{7,261},{8,10},{9,... | collective-permute-start | bytes 884744 | tf_op jit(solution)/shard_map/ppermute | solution.py:179
  20.8 26.7 %collective-permute-start.6 = (bf16[128,1152]{1,0:T(8,128)(2,1)S(1)}, bf16[128,1152]{1,0:T(8,128)(2,1)S(1)}, u32[]{:S(2)}, u32[]{:S(2)}) collective-permute-start(bf16[128,1152]{1,0:T(8,128)(2,1)S(1)} %shard_map.67), channel_id=1, source_target_pairs={{0,258},{1,259},{2,0},{3,1},{4,262},{5,263},{6,4},{7,5},{8,266},{9... | collective-permute-start | bytes 884744 | tf_op jit(solution)/shard_map/ppermute | solution.py:179
  25.8 24.3 %collective-permute-start.2 = (bf16[256,1152]{1,0:T(8,128)(2,1)S(1)}, bf16[256,1152]{1,0:T(8,128)(2,1)S(1)}, u32[]{:S(2)}, u32[]{:S(2)}) collective-permute-start(bf16[256,1152]{1,0:T(8,128)(2,1)S(1)} %pad_maximum_fusion.2), channel_id=1, source_target_pairs={{0,128},{1,129},{2,130},{3,131},{4,132},{5,133},{6,134},{7,135},{8... | collective-permute-start | bytes 1769480 | tf_op jit(solution)/shard_map/ppermute | solution.py:179
  37.9 12.3 %collective-permute-start.4 = (bf16[256,1152]{1,0:T(8,128)(2,1)S(1)}, bf16[256,1152]{1,0:T(8,128)(2,1)S(1)}, u32[]{:S(2)}, u32[]{:S(2)}) collective-permute-start(bf16[256,1152]{1,0:T(8,128)(2,1)S(1)} %pad_maximum_fusion.1.refs_3_.refs_5_), channel_id=1, source_target_pairs={{0,4},{1,5},{2,126},{3,127},{4,8},{5,9},{6,2},{7,3},{8,12},{9,13},... | collective-permute-start | bytes 1769480 | tf_op jit(solution)/shard_map/ppermute | solution.py:179
  40.5 15.8 %collective-permute-start.3 = (bf16[256,1152]{1,0:T(8,128)(2,1)S(1)}, bf16[256,1152]{1,0:T(8,128)(2,1)S(1)}, u32[]{:S(2)}, u32[]{:S(2)}) collective-permute-start(bf16[256,1152]{1,0:T(8,128)(2,1)S(1)} %pad_maximum_fusion.1.refs_3_.refs_5_), channel_id=1, source_target_pairs={{0,124},{1,125},{2,6},{3,7},{4,0},{5,1},{6,10},{7,11},{8,4},{9,5},... | collective-permute-start | bytes 1769480 | tf_op jit(solution)/shard_map/ppermute | solution.py:179
  47.5 18.3 %collective-permute-start.7 = (bf16[256,1152]{1,0:T(8,128)(2,1)S(1)}, bf16[256,1152]{1,0:T(8,128)(2,1)}, u32[]{:S(2)}, u32[]{:S(2)}) collective-permute-start(bf16[256,1152]{1,0:T(8,128)(2,1)S(1)} %constant_dynamic-update-slice_fusion.refs_3_.refs_8_), channel_id=1, source_target_pairs={{0,4},{1,5},{2,126},{3,127},{4,8},{5,9},{6,2},{7,3},{8,12},{9,13},... | collective-permute-start | bytes 1769480 | tf_op jit(solution)/shard_map/ppermute | solution.py:179
  52.3 0.7 copy-start.4
  53.0 27.2 %collective-permute-start.10 = (bf16[256,1152]{1,0:T(8,128)(2,1)}, bf16[256,1152]{1,0:T(8,128)(2,1)}, u32[]{:S(2)}, u32[]{:S(2)}) collective-permute-start(bf16[256,1152]{1,0:T(8,128)(2,1)} %get-tuple-element.46), channel_id=1, source_target_pairs={{4,0},{5,1},{126,2},{127,3},{8,4},{9,5},{2,6},{3,7},{12,8},{13,9},... | collective-permute-start | bytes 1769480 | tf_op jit(solution)/shard_map/ppermute | solution.py:182
  57.6 23.8 %collective-permute-start.11 = (bf16[256,1152]{1,0:T(8,128)(2,1)S(1)}, bf16[256,1152]{1,0:T(8,128)(2,1)S(1)}, u32[]{:S(2)}, u32[]{:S(2)}) collective-permute-start(bf16[256,1152]{1,0:T(8,128)(2,1)S(1)} %get-tuple-element.47), channel_id=1, source_target_pairs={{124,0},{125,1},{6,2},{7,3},{0,4},{1,5},{10,6},{11,7},{4,8},{5,9},... | collective-permute-start | bytes 1769480 | tf_op jit(solution)/shard_map/ppermute | solution.py:182
  68.2 18.3 %collective-permute-start.13 = (bf16[256,1152]{1,0:T(8,128)(2,1)S(1)}, bf16[256,1152]{1,0:T(8,128)(2,1)S(1)}, u32[]{:S(2)}, u32[]{:S(2)}) collective-permute-start(bf16[256,1152]{1,0:T(8,128)(2,1)S(1)} %get-tuple-element.51), channel_id=1, source_target_pairs={{4,0},{5,1},{126,2},{127,3},{8,4},{9,5},{2,6},{3,7},{12,8},{13,9},... | collective-permute-start | bytes 1769480 | tf_op jit(solution)/shard_map/ppermute | solution.py:182
  72.7 1.3 %copy-start.5 = (bf16[256,512]{1,0:T(8,128)(2,1)S(1)}, bf16[256,512]{1,0:T(8,128)(2,1)}, u32[]{:S(2)}) copy-start(bf16[256,512]{1,0:T(8,128)(2,1)} %copy-done.4) | copy-start | bytes 786436
  76.2 23.2 %collective-permute-start.8 = (bf16[272,1152]{1,0:T(8,128)(2,1)S(1)}, bf16[272,1152]{1,0:T(8,128)(2,1)S(1)}, u32[]{:S(2)}, u32[]{:S(2)}) collective-permute-start(bf16[272,1152]{1,0:T(8,128)(2,1)S(1)} %shard_map.75), channel_id=1, source_target_pairs={{0,1},{1,0},{2,3},{3,2},{4,5},{5,4},{6,7},{7,6},{8,9},{9,8},{10,11... | collective-permute-start | bytes 1880072 | tf_op jit(solution)/shard_map/ppermute | solution.py:179
  81.7 4.9 %copy-start.6 = (f32[256,1152]{1,0:T(8,128)}, f32[256,1152]{1,0:T(8,128)S(1)}, u32[]{:S(2)}) copy-start(f32[256,1152]{1,0:T(8,128)S(1)} %pad_maximum_fusion) | copy-start | bytes 3538948
  81.8 30.0 %collective-permute-start.12 = (bf16[128,1152]{1,0:T(8,128)(2,1)S(1)}, bf16[128,1152]{1,0:T(8,128)(2,1)S(1)}, u32[]{:S(2)}, u32[]{:S(2)}) collective-permute-start(bf16[128,1152]{1,0:T(8,128)(2,1)S(1)} %slice.52), channel_id=1, source_target_pairs={{256,0},{257,1},{258,2},{259,3},{260,4},{261,5},{262,6},{263,7},{2... | collective-permute-start | bytes 884744 | tf_op jit(solution)/shard_map/ppermute | solution.py:182
  86.7 25.1 %slice-start = ((f32[256,1152]{1,0:T(8,128)}), f32[128,1152]{1,0:T(8,128)S(1)}, s32[]{:S(2)}) async-start(f32[256,1152]{1,0:T(8,128)} %copy-done.6), calls=%async_computation | async-start | bytes 1179648 | tf_op jit(solution)/shard_map/slice | solution.py:228
  86.7 25.3 %collective-permute-start.14 = (bf16[128,1152]{1,0:T(8,128)(2,1)S(1)}, bf16[128,1152]{1,0:T(8,128)(2,1)S(1)}, u32[]{:S(2)}, u32[]{:S(2)}) collective-permute-start(bf16[128,1152]{1,0:T(8,128)(2,1)S(1)} %get-tuple-element.52), channel_id=1, source_target_pairs={{2,0},{3,1},{256,2},{257,3},{6,4},{7,5},{260,6},{261,7},{10,8},{11... | collective-permute-start | bytes 884744 | tf_op jit(solution)/shard_map/ppermute | solution.py:182
  97.2 23.0 %collective-permute-start.15 = (bf16[128,1152]{1,0:T(8,128)(2,1)S(1)}, bf16[128,1152]{1,0:T(8,128)(2,1)S(1)}, u32[]{:S(2)}, u32[]{:S(2)}) collective-permute-start(bf16[128,1152]{1,0:T(8,128)(2,1)S(1)} %get-tuple-element.53), channel_id=1, source_target_pairs={{258,0},{259,1},{0,2},{1,3},{262,4},{263,5},{4,6},{5,7},{266,8},{2... | collective-permute-start | bytes 884744 | tf_op jit(solution)/shard_map/ppermute | solution.py:182
  99.5 20.8 %collective-permute-start.9 = (bf16[144,1152]{1,0:T(8,128)(2,1)S(1)}, bf16[144,1152]{1,0:T(8,128)(2,1)S(1)}, u32[]{:S(2)}, u32[]{:S(2)}) collective-permute-start(bf16[144,1152]{1,0:T(8,128)(2,1)S(1)} %get-tuple-element.44), channel_id=1, source_target_pairs={{0,128},{1,129},{2,130},{3,131},{4,132},{5,133},{6,134},{7,135},{8... | collective-permute-start | bytes 995336 | tf_op jit(solution)/shard_map/ppermute | solution.py:179
  111.8 8.5 %copy-start.1 = (f32[128,1152]{1,0:T(8,128)S(1)}, f32[128,1152]{1,0:T(8,128)}, u32[]{:S(2)}) copy-start(f32[128,1152]{1,0:T(8,128)} %refs_0_.5) | copy-start | bytes 1769476
  111.8 8.5 %copy-start.3 = (f32[128,1152]{1,0:T(8,128)S(1)}, f32[128,1152]{1,0:T(8,128)}, u32[]{:S(2)}) copy-start(f32[128,1152]{1,0:T(8,128)} %refs_4_.1) | copy-start | bytes 1769476
